TPU v7x, 512 devices: a whole 4x8x8 slice. The times are simulated.
512 devices in a mesh: dp: 4 (over y_lo, core), tensor: 4 (over x), context: 32 (over y_hi, z).
Axes of the slice: x: 4, y: 8 (y_hi: 4, y_lo: 2; y = y_hi * 2 + y_lo), z: 8, core: 2. Of those that a mesh axis runs over, the one named last changes fastest.
Arguments:
- inputs: bfloat16 [4, 4096, 4096], P('dp', 'context', 'tensor'), may hold values from -6 to 6
- value_weight: bfloat16 [4096, 4096], P(('tensor', 'context')), may hold values from -0.09375 to 0.09375
- query: bfloat16 [4, 4096, 4096], P('dp', 'tensor', 'context'), may hold values from -6 to 6
- key: bfloat16 [4, 4096, 4096], P('dp', 'tensor', 'context'), may hold values from -6 to 6
- filters: float32 [4096, 4096], P(('tensor', 'context')), may hold values from -5 to 5
- skip: float32 [4096], P(('tensor', 'context')), may hold values from 0.1 to 1.9
- cotangent: bfloat16 [4, 4096, 4096], P('dp', 'tensor', 'context'), may hold values from -6 to 6
Outputs:
- gated: bfloat16 [4, 4096, 4096], P('dp', 'tensor', 'context')
- query_grad: bfloat16 [4, 4096, 4096], P('dp', 'tensor', 'context')
- key_grad: bfloat16 [4, 4096, 4096], P('dp', 'tensor', 'context')
- input_grad: bfloat16 [4, 4096, 4096], P('dp', 'context', 'tensor')
- filter_grad: float32 [4096, 4096], P(('tensor', 'context'))
- skip_grad: float32 [4096], P(('tensor', 'context'))
All inputs are finite; a program needn't handle non-finite values.
Results may differ from a plain program's by a relative error of at most 0.018.
Values may be sent and summed in bfloat16 or wider, within the bound.
No kernel may reach another device: no remote copies, remote signals or barrier semaphores. Data moves between devices by JAX's collectives and lax.ppermute only.
A program may use at most 64 MiB of HBM per device.

v0:
```python
import jax
import jax.numpy as jnp
from jax import lax
from jax.experimental import pallas as pl
from jax.experimental.pallas import tpu as pltpu
from jax.sharding import PartitionSpec as P

f32 = jnp.float32
bf16 = jnp.bfloat16

LANES = 128
GROUP = 8
SEQS = 4
BLOCKS = 32
ROWS = BLOCKS * SEQS
SIGNAL = ROWS * GROUP
TAPS = BLOCKS * LANES
WIDE = TAPS + LANES


def load_pair(pair_ref):
    both = pair_ref[...].astype(f32).reshape(ROWS, 2, GROUP, LANES)
    return both[:, 0].reshape(SIGNAL, LANES), both[:, 1].reshape(SIGNAL, LANES)


def early_kernel(filters_ref, skip_ref, pair_ref, dmix_ref, dvalue_ref, taps_ref, rolled, grads, ahead, wide, result):
    chan = pl.program_id(0)

    @pl.when(chan == 0)
    def _():
        dconv, _ = load_pair(pair_ref)
        grads[0:SIGNAL, :] = dconv
        grads[SIGNAL:, :] = jnp.zeros((SIGNAL, LANES), f32)
        padded = jnp.concatenate([filters_ref[...], jnp.zeros((GROUP, LANES), f32)], axis=1)
        for row in range(GROUP):
            turned = pltpu.roll(padded, row, 1) if row else padded
            for block in range(BLOCKS + 1):
                rolled[block, row * GROUP : (row + 1) * GROUP, :] = turned[:, block * LANES : (block + 1) * LANES]

    base = jnp.concatenate(
        [rolled[block, pl.ds(chan, GROUP, stride=GROUP), :] for block in range(BLOCKS + 1)], axis=1
    )
    for pair in range(LANES // 16):
        low = pltpu.roll(base, 16 * pair, 1) if pair else base
        high = pltpu.roll(base, 16 * pair + 8, 1)
        tile = jnp.concatenate([low[:, :TAPS], high[:, :TAPS]], axis=0).astype(bf16)
        wide[16 * pair : 16 * pair + 16, :] = tile
        for block in range(BLOCKS):
            taps_ref[0, block * LANES + 16 * pair : block * LANES + 16 * pair + 16, :] = tile[
                :, block * LANES : (block + 1) * LANES
            ]
    for block in range(BLOCKS):
        ahead[:, block * LANES : (block + 1) * LANES] = grads[
            pl.ds(block * SEQS * GROUP + chan, ROWS, stride=GROUP), :
        ].astype(bf16)
    total = lax.dot_general(ahead[...], wide[...], (((1,), (1,)), ((), ())), preferred_element_type=f32)
    own = grads[pl.ds(chan, ROWS, stride=GROUP), :]
    result[pl.ds(chan, ROWS, stride=GROUP), :] = total + skip_ref[chan] * own

    @pl.when(chan == GROUP - 1)
    def _():
        _, key = load_pair(pair_ref)
        dmix = result[...].astype(bf16)
        dmix_ref[...] = dmix
        dvalue = (dmix.astype(f32) * key).reshape(BLOCKS, SEQS, GROUP, LANES)
        for seq in range(SEQS):
            dvalue_ref[:, seq * LANES : (seq + 1) * LANES] = (
                dvalue[:, seq].reshape(BLOCKS * GROUP, LANES).astype(bf16)
            )


def late_kernel(taps_ref, skip_ref, pair_ref, value_ref, dmix_ref, out_ref, fgrad_ref, mixes, grads, behind, ahead, corr, sums, result, kgrad):
    chan = pl.program_id(0)

    @pl.when(chan == 0)
    def _():
        dconv, key = load_pair(pair_ref)
        grads[0:SIGNAL, :] = dconv
        grads[SIGNAL:, :] = jnp.zeros((SIGNAL, LANES), f32)
        value = value_ref[...].astype(f32)
        parts = [
            value[:, seq * LANES : (seq + 1) * LANES].reshape(BLOCKS, 1, GROUP, LANES) for seq in range(SEQS)
        ]
        value = jnp.concatenate(parts, axis=1).reshape(SIGNAL, LANES)
        mixes[0:SIGNAL, :] = jnp.zeros((SIGNAL, LANES), f32)
        mixes[SIGNAL:, :] = (key * value).astype(bf16).astype(f32)
        kgrad[...] = dmix_ref[...].astype(f32) * value
        corr[:, TAPS:] = jnp.zeros((LANES, LANES), f32)

    for block in range(BLOCKS):
        lanes = slice(block * LANES, (block + 1) * LANES)
        behind[:, lanes] = mixes[pl.ds(SIGNAL - block * SEQS * GROUP + chan, ROWS, stride=GROUP), :].astype(bf16)
        ahead[:, lanes] = grads[pl.ds(block * SEQS * GROUP + chan, ROWS, stride=GROUP), :].astype(bf16)
    own = mixes[pl.ds(SIGNAL + chan, ROWS, stride=GROUP), :]
    total = jnp.dot(behind[...], taps_ref[0], preferred_element_type=f32)
    result[pl.ds(chan, ROWS, stride=GROUP), :] = total + skip_ref[chan] * own
    corr[:, :TAPS] = jnp.dot(own.T.astype(bf16), ahead[...], preferred_element_type=f32)
    acc = corr[0:GROUP, :]
    for group in range(1, LANES // GROUP):
        acc = acc + pltpu.roll(corr[group * GROUP : (group + 1) * GROUP, :], WIDE - group * GROUP, 1)
    for block in range(BLOCKS + 1):
        sums[block, pl.ds(pl.multiple_of(chan * GROUP, GROUP), GROUP), :] = acc[:, block * LANES : (block + 1) * LANES]

    @pl.when(chan == GROUP - 1)
    def _():
        both = [
            result[...].reshape(ROWS, 1, GROUP, LANES),
            kgrad[...].reshape(ROWS, 1, GROUP, LANES),
        ]
        out_ref[...] = jnp.concatenate(both, axis=1).reshape(2 * SIGNAL, LANES).astype(bf16)
        fgrad = None
        for row in range(GROUP):
            part = jnp.concatenate(
                [sums[block, pl.ds(row, GROUP, stride=GROUP), :] for block in range(BLOCKS + 1)], axis=1
            )
            fgrad = part if row == 0 else fgrad + pltpu.roll(part, WIDE - row, 1)
        fgrad_ref[...] = fgrad[:, :TAPS].astype(bf16)


def whole(shape):
    return pl.BlockSpec(shape, lambda chan: (0,) * len(shape))


params = pltpu.CompilerParams(vmem_limit_bytes=48 * 1024 * 1024)
smem = pl.BlockSpec(memory_space=pltpu.SMEM)
taps_spec = pl.BlockSpec((1, TAPS, LANES), lambda chan: (chan, 0, 0))


def early(filters, skip, pair):
    return pl.pallas_call(
        early_kernel,
        grid=(GROUP,),
        in_specs=[whole((GROUP, TAPS)), smem, whole((2 * SIGNAL, LANES))],
        out_specs=[whole((SIGNAL, LANES)), whole((BLOCKS * GROUP, SEQS * LANES)), taps_spec],
        out_shape=[
            jax.ShapeDtypeStruct((SIGNAL, LANES), bf16),
            jax.ShapeDtypeStruct((BLOCKS * GROUP, SEQS * LANES), bf16),
            jax.ShapeDtypeStruct((GROUP, TAPS, LANES), bf16),
        ],
        scratch_shapes=[
            pltpu.VMEM((BLOCKS + 1, GROUP * GROUP, LANES), f32),
            pltpu.VMEM((2 * SIGNAL, LANES), f32),
            pltpu.VMEM((ROWS, TAPS), bf16),
            pltpu.VMEM((LANES, TAPS), bf16),
            pltpu.VMEM((SIGNAL, LANES), f32),
        ],
        compiler_params=params,
        name="early",
    )(filters, skip, pair)


def late(taps, skip, pair, value, dmix):
    return pl.pallas_call(
        late_kernel,
        grid=(GROUP,),
        in_specs=[
            taps_spec,
            smem,
            whole((2 * SIGNAL, LANES)),
            whole((BLOCKS * GROUP, SEQS * LANES)),
            whole((SIGNAL, LANES)),
        ],
        out_specs=[whole((2 * SIGNAL, LANES)), whole((GROUP, TAPS))],
        out_shape=[
            jax.ShapeDtypeStruct((2 * SIGNAL, LANES), bf16),
            jax.ShapeDtypeStruct((GROUP, TAPS), bf16),
        ],
        scratch_shapes=[
            pltpu.VMEM((2 * SIGNAL, LANES), f32),
            pltpu.VMEM((2 * SIGNAL, LANES), f32),
            pltpu.VMEM((ROWS, TAPS), bf16),
            pltpu.VMEM((ROWS, TAPS), bf16),
            pltpu.VMEM((LANES, WIDE), f32),
            pltpu.VMEM((BLOCKS + 1, GROUP * GROUP, LANES), f32),
            pltpu.VMEM((SIGNAL, LANES), f32),
            pltpu.VMEM((SIGNAL, LANES), f32),
        ],
        compiler_params=params,
        name="late",
    )(taps, skip, pair, value, dmix)


def swap(values, axes):
    return lax.all_to_all(values, axes, split_axis=0, concat_axis=0, tiled=True)


def pick_columns(weight, quarter):
    span = 512
    source = lax.broadcasted_iota(jnp.int32, (span, LANES), 0)
    target = lax.broadcasted_iota(jnp.int32, (span, LANES), 1)
    chosen = (source == (target // GROUP) * (GROUP * SEQS) + quarter * GROUP + target % GROUP).astype(bf16)
    parts = [
        jnp.dot(weight[:, start : start + span], chosen, preferred_element_type=f32).astype(bf16)
        for start in range(0, weight.shape[1], span)
    ]
    return jnp.concatenate(parts, axis=1)


def per_device(inputs, value_weight, query, key, filters, skip, cotangent):
    quarter = lax.axis_index("dp")
    rows = value_weight.shape[0]
    picked = pick_columns(value_weight, quarter)
    half = picked.shape[1] // 2
    halves = [
        swap(jnp.broadcast_to(part[None], (BLOCKS,) + part.shape), "context").reshape(BLOCKS * rows, half)
        for part in (picked[:, :half], picked[:, half:])
    ]
    tokens = lax.all_gather(inputs[0], "dp", axis=0, tiled=True)

    query_part = query[0].astype(f32)
    upstream = cotangent[0].astype(f32)
    dconv = (upstream * query_part).astype(bf16)
    pair = jnp.concatenate([dconv.reshape(ROWS, 1, GROUP, LANES), key[0].reshape(ROWS, 1, GROUP, LANES)], axis=1)
    pair = swap(pair, ("context", "dp")).reshape(2 * SIGNAL, LANES)
    own_filters = lax.dynamic_slice_in_dim(filters, quarter * GROUP, GROUP, 0)
    own_skip = lax.dynamic_slice_in_dim(skip, quarter * GROUP, GROUP, 0)
    dmix, dvalue, taps = early(own_filters, own_skip, pair)
    dvalue = swap(dvalue.reshape(BLOCKS, GROUP, SEQS * LANES), "context").reshape(BLOCKS * GROUP, SEQS * LANES)
    dvalue = lax.all_gather(dvalue, "tensor", axis=0, tiled=True)

    weight = jnp.concatenate(halves, axis=1)
    partial = lax.dot_general(weight, tokens, (((0,), (1,)), ((), ())), preferred_element_type=f32).astype(bf16)
    partial = swap(partial.reshape(4, BLOCKS * GROUP, SEQS * LANES), "tensor").astype(f32)
    value = (partial[0] + partial[1] + partial[2] + partial[3]).astype(bf16)
    value = swap(value.reshape(BLOCKS, GROUP, SEQS * LANES), "context").reshape(BLOCKS * GROUP, SEQS * LANES)
    out, fgrad = late(taps, own_skip, pair, value, dmix)
    out = swap(out.reshape(ROWS, 2, GROUP, LANES), ("context", "dp"))
    conv = out[:, 0].reshape(SIGNAL, LANES).astype(f32)
    key_grad = out[:, 1].reshape(SIGNAL, LANES)
    gated = (query_part * conv).astype(bf16)
    query_grad = (upstream * conv).astype(bf16)
    filter_grad = lax.all_gather(fgrad, "dp", axis=0, tiled=True).astype(f32)
    skip_grad = filter_grad[:, 0]

    grad = lax.dot_general(dvalue, weight, (((0,), (1,)), ((), ())), preferred_element_type=f32).astype(bf16)
    grad = swap(grad.reshape(SEQS, LANES, grad.shape[1]), "dp").astype(f32)
    input_grad = (grad[0] + grad[1] + grad[2] + grad[3]).astype(bf16)
    return (gated[None], query_grad[None], key_grad[None], input_grad[None], filter_grad, skip_grad)


def solution(mesh):
    by_channel = P("dp", "tensor", "context")
    by_row = P(("tensor", "context"), None)
    in_specs = (
        P("dp", "context", "tensor"),
        by_row,
        by_channel,
        by_channel,
        by_row,
        P(("tensor", "context")),
        by_channel,
    )
    out_specs = (
        by_channel,
        by_channel,
        by_channel,
        P("dp", "context", "tensor"),
        by_row,
        P(("tensor", "context")),
    )
    return jax.shard_map(
        per_device, mesh=mesh, in_specs=in_specs, out_specs=out_specs, check_vma=False
    )
```

profile of v0, /device:TPU:1, one launch (start us, length us, event | category | flops | bytes accessed | tf_op | source)
XLA Modules:
  0.0 251.4 jit_solution(6213222837963626500)
XLA Ops:
  8.0 0.0 copy-start
  8.0 0.0 copy-start.6
  8.0 1.2 fusion.15
  9.2 1.8 pad_maximum_fusion.3
  11.0 18.4 %all-to-all-start = ((bf16[128,2,8,128]{3,2,1,0:T(8,128)(2,1)}), bf16[128,2,8,128]{3,2,1,0:T(8,128)(2,1)S(1)}, u32[]{:S(2)}, u32[]{:S(2)}) async-start(bf16[128,2,8,128]{3,2,1,0:T(8,128)(2,1)} %pad_maximum_fusion.3), calls=%async_computation | async-start | bytes 1048576 | tf_op jit(solution)/shard_map/all_to_all | solution.py:184
  29.5 0.1 add_compare_fusion
  29.6 0.0 copy-done.6
  29.6 0.2 fusion.3
  29.7 0.2 fusion.2
  29.9 0.2 fusion.1
  30.1 0.2 fusion
  30.2 19.3 %all-to-all-done = bf16[128,2,8,128]{3,2,1,0:T(8,128)(2,1)S(1)} async-done(((bf16[128,2,8,128]{3,2,1,0:T(8,128)(2,1)}), bf16[128,2,8,128]{3,2,1,0:T(8,128)(2,1)S(1)}, u32[]{:S(2)}, u32[]{:S(2)}) %all-to-all-start) | async-done | bytes 524320 | tf_op jit(solution)/shard_map/all_to_all | solution.py:184
  49.5 1.1 broadcast_in_dim.4
  50.6 4.2 %all-to-all-start.1 = ((bf16[32,32,512]{2,1,0:T(8,128)(2,1)}), bf16[32,32,512]{2,1,0:T(8,128)(2,1)S(1)}, u32[]{:S(2)}, u32[]{:S(2)}) async-start(bf16[32,32,512]{2,1,0:T(8,128)(2,1)} %broadcast_in_dim.4), calls=%async_computation.1 | async-start | bytes 2097152 | tf_op jit(solution)/shard_map/all_to_all | solution.py:184
  54.8 0.0 copy-start.7
  54.8 0.2 fusion.7
  55.0 0.2 fusion.6
  55.1 0.2 fusion.5
  55.3 0.2 fusion.4
  55.5 23.9 %all-to-all-done.1 = bf16[32,32,512]{2,1,0:T(8,128)(2,1)S(1)} async-done(((bf16[32,32,512]{2,1,0:T(8,128)(2,1)}), bf16[32,32,512]{2,1,0:T(8,128)(2,1)S(1)}, u32[]{:S(2)}, u32[]{:S(2)}) %all-to-all-start.1) | async-done | bytes 1048608 | tf_op jit(solution)/shard_map/all_to_all | solution.py:184
  79.3 1.2 broadcast_in_dim.5
  80.5 11.1 %all-to-all-start.2 = ((bf16[32,32,512]{2,1,0:T(8,128)(2,1)}), bf16[32,32,512]{2,1,0:T(8,128)(2,1)S(1)}, u32[]{:S(2)}, u32[]{:S(2)}) async-start(bf16[32,32,512]{2,1,0:T(8,128)(2,1)} %broadcast_in_dim.5), calls=%async_computation.2 | async-start | bytes 2097152 | tf_op jit(solution)/shard_map/all_to_all | solution.py:184
  91.6 0.0 all-gather.6.cloned.1.call-start
  91.6 0.7 all-gather.6.cloned.1.call-update
  92.3 0.0 copy-done.7
  92.3 0.1 dynamic_slice.7.skip_ref
  92.4 0.0 copy-done
  92.4 9.4 %early.1 = (bf16[1024,128]{1,0:T(8,128)(2,1)S(1)}, bf16[256,512]{1,0:T(8,128)(2,1)}, bf16[8,4096,128]{2,1,0:T(8,128)(2,1)}) custom-call(f32[8,4096]{1,0:T(8,128)S(1)} %constant_dynamic-slice_fusion.filters_ref, f32[8]{0:T(128)S(1)} %dynamic_slice.7.skip_ref, bf16[2048,128]{1,0:T(8,128)(2,1)S(1)} %bitcast.55), custom_call_target="tpu_custom_call" | custom-call | tf_op jit(solution)/shard_map/early/pallas_call | solution.py:130
  101.9 14.8 %all-to-all-done.2 = bf16[32,32,512]{2,1,0:T(8,128)(2,1)S(1)} async-done(((bf16[32,32,512]{2,1,0:T(8,128)(2,1)}), bf16[32,32,512]{2,1,0:T(8,128)(2,1)S(1)}, u32[]{:S(2)}, u32[]{:S(2)}) %all-to-all-start.2) | async-done | bytes 1048608 | tf_op jit(solution)/shard_map/all_to_all | solution.py:184
  116.6 0.0 copy-start.3
  116.7 10.7 %all-to-all-start.6 = ((bf16[32,8,512]{2,1,0:T(8,128)(2,1)}), bf16[32,8,512]{2,1,0:T(8,128)(2,1)}, u32[]{:S(2)}, u32[]{:S(2)}) async-start(bf16[32,8,512]{2,1,0:T(8,128)(2,1)} %bitcast.23), calls=%async_computation.6 | async-start | bytes 524288 | tf_op jit(solution)/shard_map/all_to_all | solution.py:184
  127.3 0.0 all-gather.6.cloned.1.call-done
  127.3 3.5 %convolution_convert_fusion.1 = bf16[1024,512]{1,0:T(8,128)(2,1)} fusion(bf16[1024,512]{1,0:T(8,128)(2,1)S(1)} %bitcast.60, bf16[1024,512]{1,0:T(8,128)(2,1)S(1)} %bitcast.58, bf16[1,512,1024]{2,1,0:T(8,128)(2,1)} %all-gather.6.cloned.1.call-done), kind=kOutput, calls=%fused_computation.2 | convolution fusion | flops 1078460416 | bytes 4194304 | tf_op jit(solution)/shard_map/dot_general | solution.py:222
  130.8 0.0 copy-done.3
  130.8 8.6 %all-to-all-done.6 = bf16[32,8,512]{2,1,0:T(8,128)(2,1)} async-done(((bf16[32,8,512]{2,1,0:T(8,128)(2,1)}), bf16[32,8,512]{2,1,0:T(8,128)(2,1)}, u32[]{:S(2)}, u32[]{:S(2)}) %all-to-all-start.6) | async-done | bytes 262176 | tf_op jit(solution)/shard_map/all_to_all | solution.py:184
  139.4 4.0 %all-to-all-start.3 = ((bf16[4,256,512]{2,1,0:T(8,128)(2,1)}), bf16[4,256,512]{2,1,0:T(8,128)(2,1)S(1)}, u32[]{:S(2)}, u32[]{:S(2)}) async-start(bf16[4,256,512]{2,1,0:T(8,128)(2,1)} %bitcast.63), calls=%async_computation.3 | async-start | bytes 2097152 | tf_op jit(solution)/shard_map/all_to_all | solution.py:184
  143.4 0.0 all-gather.4.cloned.1.call-start
  143.4 0.6 all-gather.4.cloned.1.call-update
  144.0 11.4 %all-to-all-done.3 = bf16[4,256,512]{2,1,0:T(8,128)(2,1)S(1)} async-done(((bf16[4,256,512]{2,1,0:T(8,128)(2,1)}), bf16[4,256,512]{2,1,0:T(8,128)(2,1)S(1)}, u32[]{:S(2)}, u32[]{:S(2)}) %all-to-all-start.3) | async-done | bytes 1048608 | tf_op jit(solution)/shard_map/all_to_all | solution.py:184
  155.4 0.3 convert_element_type.155
  155.7 0.2 fusion.14
  155.9 21.1 %all_to_all.40 = bf16[32,8,512]{2,1,0:T(8,128)(2,1)S(1)} all-to-all(bf16[32,8,512]{2,1,0:T(8,128)(2,1)S(1)} %fusion.14), channel_id=1, replica_groups=mesh['dp'=4,'tensor'=4,'context'=32] {'context'}, dimensions={0} | all-to-all | bytes 524288 | tf_op jit(solution)/shard_map/all_to_all | solution.py:184
  177.0 0.0 copy-start.4
  177.0 14.7 %late.1 = (bf16[2048,128]{1,0:T(8,128)(2,1)}, bf16[8,4096]{1,0:T(8,128)(2,1)S(1)}) custom-call(bf16[8,4096,128]{2,1,0:T(8,128)(2,1)} %get-tuple-element.11.taps_ref, f32[8]{0:T(128)S(1)} %dynamic_slice.7.skip_ref, bf16[2048,128]{1,0:T(8,128)(2,1)S(1)} %bitcast.56, bf16[256,512]{1,0:T(8,128)(2,1)S(1)} %bitcast.57, ...), custom_call_target="tpu_custom_call" | custom-call | tf_op jit(solution)/shard_map/late/pallas_call | solution.py:153
  191.7 8.2 %all-to-all-start.5 = ((bf16[128,2,8,128]{3,2,1,0:T(8,128)(2,1)}), bf16[128,2,8,128]{3,2,1,0:T(8,128)(2,1)S(1)}, u32[]{:S(2)}, u32[]{:S(2)}) async-start(bf16[128,2,8,128]{3,2,1,0:T(8,128)(2,1)} %bitcast.19), calls=%async_computation.5 | async-start | bytes 1048576 | tf_op jit(solution)/shard_map/all_to_all | solution.py:184
  199.9 0.0 all-gather.4.cloned.1.call-done
  199.9 0.0 copy-done.4
  199.9 3.5 %convolution_convert_fusion = bf16[512,1024]{1,0:T(8,128)(2,1)} fusion(bf16[1024,512]{1,0:T(8,128)(2,1)} %all-gather.4.cloned.1.call-done, bf16[1024,512]{1,0:T(8,128)(2,1)S(1)} %bitcast.61, bf16[1024,512]{1,0:T(8,128)(2,1)S(1)} %bitcast.59), kind=kOutput, calls=%fused_computation.1 | convolution fusion | flops 1078460416 | bytes 4194304 | tf_op jit(solution)/shard_map/dot_general | solution.py:235
  203.4 0.0 copy-start.1
  203.4 0.0 copy-start.2
  203.4 16.6 %all-to-all-done.5 = bf16[128,2,8,128]{3,2,1,0:T(8,128)(2,1)S(1)} async-done(((bf16[128,2,8,128]{3,2,1,0:T(8,128)(2,1)}), bf16[128,2,8,128]{3,2,1,0:T(8,128)(2,1)S(1)}, u32[]{:S(2)}, u32[]{:S(2)}) %all-to-all-start.5) | async-done | bytes 524320 | tf_op jit(solution)/shard_map/all_to_all | solution.py:184
  220.0 3.9 %all-to-all-start.7 = ((bf16[4,128,1024]{2,1,0:T(8,128)(2,1)}), bf16[4,128,1024]{2,1,0:T(8,128)(2,1)S(1)}, u32[]{:S(2)}, u32[]{:S(2)}) async-start(bf16[4,128,1024]{2,1,0:T(8,128)(2,1)} %bitcast.62), calls=%async_computation.7 | async-start | bytes 2097152 | tf_op jit(solution)/shard_map/all_to_all | solution.py:184
  223.9 16.6 %all_gather.11 = bf16[32,4096]{1,0:T(8,128)(2,1)S(1)} all-gather(bf16[8,4096]{1,0:T(8,128)(2,1)S(1)} %get-tuple-element.15), channel_id=1, replica_groups=mesh['dp'=4,'tensor'=4,'context'=32] {'dp'}, dimensions={0}, use_global_device_ids=true | all-gather | bytes 327680 | tf_op jit(solution)/shard_map/all_gather | solution.py:232
  240.5 0.0 copy-start.5
  240.5 0.7 slice_reduce_fusion
  241.2 0.7 slice_bitcast_fusion
  241.9 0.0 copy-done.1
  241.9 0.0 copy-done.2
  241.9 0.9 fusion.11
  242.8 0.0 all-to-all-done.7
  242.8 0.2 convert_element_type.163
  243.1 0.0 copy-done.5
  243.1 0.8 fusion.12
  (7 shorter events, 0.1 us)
Async XLA Ops:
  8.0 84.4 %copy-start = (f32[32,4096]{1,0:T(8,128)S(1)}, f32[32,4096]{1,0:T(8,128)}, u32[]{:S(2)}) copy-start(f32[32,4096]{1,0:T(8,128)} %param.11) | copy-start | bytes 1572868
  8.0 21.5 %copy-start.6 = (bf16[32,4096]{1,0:T(8,128)(2,1)S(1)}, bf16[32,4096]{1,0:T(8,128)(2,1)}, u32[]{:S(2)}) copy-start(bf16[32,4096]{1,0:T(8,128)(2,1)} %param.8) | copy-start | bytes 786436
  11.0 38.5 %all-to-all-start = ((bf16[128,2,8,128]{3,2,1,0:T(8,128)(2,1)}), bf16[128,2,8,128]{3,2,1,0:T(8,128)(2,1)S(1)}, u32[]{:S(2)}, u32[]{:S(2)}) async-start(bf16[128,2,8,128]{3,2,1,0:T(8,128)(2,1)} %pad_maximum_fusion.3), calls=%async_computation | async-start | bytes 1048576 | tf_op jit(solution)/shard_map/all_to_all | solution.py:184
  50.6 28.7 %all-to-all-start.1 = ((bf16[32,32,512]{2,1,0:T(8,128)(2,1)}), bf16[32,32,512]{2,1,0:T(8,128)(2,1)S(1)}, u32[]{:S(2)}, u32[]{:S(2)}) async-start(bf16[32,32,512]{2,1,0:T(8,128)(2,1)} %broadcast_in_dim.4), calls=%async_computation.1 | async-start | bytes 2097152 | tf_op jit(solution)/shard_map/all_to_all | solution.py:184
  54.8 37.5 %copy-start.7 = (f32[32]{0:T(128)S(1)}, f32[32]{0:T(128)}, u32[]{:S(2)}) copy-start(f32[32]{0:T(128)} %param.12) | copy-start | bytes 388
  80.5 36.2 %all-to-all-start.2 = ((bf16[32,32,512]{2,1,0:T(8,128)(2,1)}), bf16[32,32,512]{2,1,0:T(8,128)(2,1)S(1)}, u32[]{:S(2)}, u32[]{:S(2)}) async-start(bf16[32,32,512]{2,1,0:T(8,128)(2,1)} %broadcast_in_dim.5), calls=%async_computation.2 | async-start | bytes 2097152 | tf_op jit(solution)/shard_map/all_to_all | solution.py:184
  91.6 35.8 %all-gather.6.cloned.1.call-start = ((), (), s32[]{:S(2)}) async-start(), calls=%async_computation.9 | async-start | bytes 1310720 | tf_op jit(solution)/shard_map/all_gather | solution.py:208
  116.6 14.2 %copy-start.3 = (bf16[32,32,512]{2,1,0:T(8,128)(2,1)}, bf16[32,32,512]{2,1,0:T(8,128)(2,1)S(1)}, u32[]{:S(2)}) copy-start(bf16[32,32,512]{2,1,0:T(8,128)(2,1)S(1)} %all-to-all-done.2) | copy-start | bytes 3145732
  116.7 22.8 %all-to-all-start.6 = ((bf16[32,8,512]{2,1,0:T(8,128)(2,1)}), bf16[32,8,512]{2,1,0:T(8,128)(2,1)}, u32[]{:S(2)}, u32[]{:S(2)}) async-start(bf16[32,8,512]{2,1,0:T(8,128)(2,1)} %bitcast.23), calls=%async_computation.6 | async-start | bytes 524288 | tf_op jit(solution)/shard_map/all_to_all | solution.py:184
  139.4 16.0 %all-to-all-start.3 = ((bf16[4,256,512]{2,1,0:T(8,128)(2,1)}), bf16[4,256,512]{2,1,0:T(8,128)(2,1)S(1)}, u32[]{:S(2)}, u32[]{:S(2)}) async-start(bf16[4,256,512]{2,1,0:T(8,128)(2,1)} %bitcast.63), calls=%async_computation.3 | async-start | bytes 2097152 | tf_op jit(solution)/shard_map/all_to_all | solution.py:184
  143.4 56.5 %all-gather.4.cloned.1.call-start = ((), (), s32[]{:S(2)}) async-start(), calls=%async_computation.8 | async-start | bytes 1310720 | tf_op jit(solution)/shard_map/all_gather | solution.py:219
  177.0 22.9 %copy-start.4 = (bf16[32,32,512]{2,1,0:T(8,128)(2,1)S(1)}, bf16[32,32,512]{2,1,0:T(8,128)(2,1)}, u32[]{:S(2)}) copy-start(bf16[32,32,512]{2,1,0:T(8,128)(2,1)} %copy-done.3) | copy-start | bytes 3145732
  191.7 28.4 %all-to-all-start.5 = ((bf16[128,2,8,128]{3,2,1,0:T(8,128)(2,1)}), bf16[128,2,8,128]{3,2,1,0:T(8,128)(2,1)S(1)}, u32[]{:S(2)}, u32[]{:S(2)}) async-start(bf16[128,2,8,128]{3,2,1,0:T(8,128)(2,1)} %bitcast.19), calls=%async_computation.5 | async-start | bytes 1048576 | tf_op jit(solution)/shard_map/all_to_all | solution.py:184
  203.4 38.5 %copy-start.1 = (bf16[1,1024,128]{2,1,0:T(8,128)(2,1)S(1)}, bf16[1,1024,128]{2,1,0:T(8,128)(2,1)}, u32[]{:S(2)}) copy-start(bf16[1,1024,128]{2,1,0:T(8,128)(2,1)} %param.13) | copy-start | bytes 786436
  203.4 38.5 %copy-start.2 = (bf16[1,1024,128]{2,1,0:T(8,128)(2,1)S(1)}, bf16[1,1024,128]{2,1,0:T(8,128)(2,1)}, u32[]{:S(2)}) copy-start(bf16[1,1024,128]{2,1,0:T(8,128)(2,1)} %param.9) | copy-start | bytes 786436
  220.0 22.8 %all-to-all-start.7 = ((bf16[4,128,1024]{2,1,0:T(8,128)(2,1)}), bf16[4,128,1024]{2,1,0:T(8,128)(2,1)S(1)}, u32[]{:S(2)}, u32[]{:S(2)}) async-start(bf16[4,128,1024]{2,1,0:T(8,128)(2,1)} %bitcast.62), calls=%async_computation.7 | async-start | bytes 2097152 | tf_op jit(solution)/shard_map/all_to_all | solution.py:184
  240.5 2.6 %copy-start.5 = (f32[32,4096]{1,0:T(8,128)}, f32[32,4096]{1,0:T(8,128)S(1)}, u32[]{:S(2)}) copy-start(f32[32,4096]{1,0:T(8,128)S(1)} %convert_element_type.165) | copy-start | bytes 1572868
Sparse Core Ops, SparseCore 0:
  94.5 30.7 all-gather.5
Sparse Core Ops, SparseCore 1:
  146.0 23.9 all-gather.3
where the time goes:
time: 252 us; the launch traced here: 251 us
  waiting for transfers between devices  95.8 us (38%)
  starting transfers between devices  60.4 us (24%)
  blocking collectives  37.7 us (15%)
  Pallas kernels  24.1 us (10%)
  between operations  15.7 us (6%)
  matrix products  8.27 us (3%)
  other arithmetic  5.58 us (2%)
  local copies, waits for them, and re-layouts  3.78 us (2%)
    all_to_all x7, waiting for transfers between devices, swap(): return lax.all_to_all(values, axes, split_axis=0, concat_axis=0, tiled=True)  94.5 us
    all_to_all x7, starting transfers between devices, swap(): return lax.all_to_all(values, axes, split_axis=0, concat_axis=0, tiled=True)  60.4 us
    all_to_all x1, blocking collectives, swap(): return lax.all_to_all(values, axes, split_axis=0, concat_axis=0, tiled=True)  21.1 us
    all_gather x1, blocking collectives, per_device(): filter_grad = lax.all_gather(fgrad, 'dp', axis=0, tiled=True).astype(f32)  16.6 us
    pallas_call x1, Pallas kernels, late(): pl.pallas_call(late_kernel, grid=(GROUP,), in_specs=[taps_spec, smem, who...  14.7 us
    pallas_call x1, Pallas kernels, early(): pl.pallas_call(early_kernel, grid=(GROUP,), in_specs=[whole((GROUP, TAPS)...  9.45 us
  transfers between devices with their start and end apart: 9, of which 6 were waited for; matrix products, arithmetic and copies ran while one was open for 4% of the time, Pallas kernels for 10%

commit v1 on v0

--- a/solution.py
+++ b/solution.py
@@ -69,31 +69,56 @@
             )
 
 
-def late_kernel(taps_ref, skip_ref, pair_ref, value_ref, dmix_ref, out_ref, fgrad_ref, mixes, grads, behind, ahead, corr, sums, result, kgrad):
+def conv_kernel(taps_ref, skip_ref, place_ref, pair_ref, value_ref, dmix_ref, out_ref, mix_ref, mixes, values, behind, result):
     chan = pl.program_id(0)
 
     @pl.when(chan == 0)
     def _():
-        dconv, key = load_pair(pair_ref)
-        grads[0:SIGNAL, :] = dconv
-        grads[SIGNAL:, :] = jnp.zeros((SIGNAL, LANES), f32)
-        value = value_ref[...].astype(f32)
-        parts = [
-            value[:, seq * LANES : (seq + 1) * LANES].reshape(BLOCKS, 1, GROUP, LANES) for seq in range(SEQS)
-        ]
-        value = jnp.concatenate(parts, axis=1).reshape(SIGNAL, LANES)
+        _, key = load_pair(pair_ref)
+        for piece in range(2 * SEQS):
+            core, high, side = piece // 4, piece // 2 % 2, piece % 2
+            seq = (high ^ place_ref[1]) * 2 + (core ^ place_ref[2])
+            start = (side ^ place_ref[0]) * (SEQS * GROUP) + seq * GROUP
+            part = value_ref[:, piece * LANES : (piece + 1) * LANES].astype(f32)
+            for two in range(BLOCKS // 2):
+                row = pl.multiple_of(two * (2 * SEQS * GROUP) + start, GROUP)
+                values[pl.ds(row, GROUP), :] = part[two * GROUP : (two + 1) * GROUP, :]
+        mix = (key * values[...]).astype(bf16)
+        mix_ref[...] = mix
         mixes[0:SIGNAL, :] = jnp.zeros((SIGNAL, LANES), f32)
-        mixes[SIGNAL:, :] = (key * value).astype(bf16).astype(f32)
-        kgrad[...] = dmix_ref[...].astype(f32) * value
-        corr[:, TAPS:] = jnp.zeros((LANES, LANES), f32)
+        mixes[SIGNAL:, :] = mix.astype(f32)
 
     for block in range(BLOCKS):
-        lanes = slice(block * LANES, (block + 1) * LANES)
-        behind[:, lanes] = mixes[pl.ds(SIGNAL - block * SEQS * GROUP + chan, ROWS, stride=GROUP), :].astype(bf16)
-        ahead[:, lanes] = grads[pl.ds(block * SEQS * GROUP + chan, ROWS, stride=GROUP), :].astype(bf16)
+        behind[:, block * LANES : (block + 1) * LANES] = mixes[
+            pl.ds(SIGNAL - block * SEQS * GROUP + chan, ROWS, stride=GROUP), :
+        ].astype(bf16)
     own = mixes[pl.ds(SIGNAL + chan, ROWS, stride=GROUP), :]
     total = jnp.dot(behind[...], taps_ref[0], preferred_element_type=f32)
     result[pl.ds(chan, ROWS, stride=GROUP), :] = total + skip_ref[chan] * own
+
+    @pl.when(chan == GROUP - 1)
+    def _():
+        kgrad = dmix_ref[...].astype(f32) * values[...]
+        both = [result[...].reshape(ROWS, 1, GROUP, LANES), kgrad.reshape(ROWS, 1, GROUP, LANES)]
+        out_ref[...] = jnp.concatenate(both, axis=1).reshape(2 * SIGNAL, LANES).astype(bf16)
+
+
+def fgrad_kernel(pair_ref, mix_ref, fgrad_ref, mixes, grads, ahead, corr, sums):
+    chan = pl.program_id(0)
+
+    @pl.when(chan == 0)
+    def _():
+        dconv, _ = load_pair(pair_ref)
+        grads[0:SIGNAL, :] = dconv
+        grads[SIGNAL:, :] = jnp.zeros((SIGNAL, LANES), f32)
+        mixes[...] = mix_ref[...].astype(f32)
+        corr[:, TAPS:] = jnp.zeros((LANES, LANES), f32)
+
+    for block in range(BLOCKS):
+        ahead[:, block * LANES : (block + 1) * LANES] = grads[
+            pl.ds(block * SEQS * GROUP + chan, ROWS, stride=GROUP), :
+        ].astype(bf16)
+    own = mixes[pl.ds(chan, ROWS, stride=GROUP), :]
     corr[:, :TAPS] = jnp.dot(own.T.astype(bf16), ahead[...], preferred_element_type=f32)
     acc = corr[0:GROUP, :]
     for group in range(1, LANES // GROUP):
@@ -103,11 +128,6 @@
 
     @pl.when(chan == GROUP - 1)
     def _():
-        both = [
-            result[...].reshape(ROWS, 1, GROUP, LANES),
-            kgrad[...].reshape(ROWS, 1, GROUP, LANES),
-        ]
-        out_ref[...] = jnp.concatenate(both, axis=1).reshape(2 * SIGNAL, LANES).astype(bf16)
         fgrad = None
         for row in range(GROUP):
             part = jnp.concatenate(
@@ -149,92 +169,160 @@
     )(filters, skip, pair)
 
 
-def late(taps, skip, pair, value, dmix):
+def late_conv(taps, skip, place, pair, value, dmix):
     return pl.pallas_call(
-        late_kernel,
+        conv_kernel,
         grid=(GROUP,),
         in_specs=[
             taps_spec,
             smem,
+            smem,
             whole((2 * SIGNAL, LANES)),
-            whole((BLOCKS * GROUP, SEQS * LANES)),
+            whole((BLOCKS * GROUP // 2, 2 * SEQS * LANES)),
             whole((SIGNAL, LANES)),
         ],
-        out_specs=[whole((2 * SIGNAL, LANES)), whole((GROUP, TAPS))],
+        out_specs=[whole((2 * SIGNAL, LANES)), whole((SIGNAL, LANES))],
         out_shape=[
             jax.ShapeDtypeStruct((2 * SIGNAL, LANES), bf16),
-            jax.ShapeDtypeStruct((GROUP, TAPS), bf16),
+            jax.ShapeDtypeStruct((SIGNAL, LANES), bf16),
         ],
         scratch_shapes=[
             pltpu.VMEM((2 * SIGNAL, LANES), f32),
+            pltpu.VMEM((SIGNAL, LANES), f32),
+            pltpu.VMEM((ROWS, TAPS), bf16),
+            pltpu.VMEM((SIGNAL, LANES), f32),
+        ],
+        compiler_params=params,
+        name="late_conv",
+    )(taps, skip, place, pair, value, dmix)
+
+
+def late_fgrad(pair, mix):
+    return pl.pallas_call(
+        fgrad_kernel,
+        grid=(GROUP,),
+        in_specs=[whole((2 * SIGNAL, LANES)), whole((SIGNAL, LANES))],
+        out_specs=whole((GROUP, TAPS)),
+        out_shape=jax.ShapeDtypeStruct((GROUP, TAPS), bf16),
+        scratch_shapes=[
+            pltpu.VMEM((SIGNAL, LANES), f32),
             pltpu.VMEM((2 * SIGNAL, LANES), f32),
-            pltpu.VMEM((ROWS, TAPS), bf16),
             pltpu.VMEM((ROWS, TAPS), bf16),
             pltpu.VMEM((LANES, WIDE), f32),
             pltpu.VMEM((BLOCKS + 1, GROUP * GROUP, LANES), f32),
-            pltpu.VMEM((SIGNAL, LANES), f32),
-            pltpu.VMEM((SIGNAL, LANES), f32),
         ],
         compiler_params=params,
-        name="late",
-    )(taps, skip, pair, value, dmix)
-
-
-def swap(values, axes):
-    return lax.all_to_all(values, axes, split_axis=0, concat_axis=0, tiled=True)
+        name="late_fgrad",
+    )(pair, mix)
+
+
+def swap(values, axes, groups=None):
+    return lax.all_to_all(values, axes, split_axis=0, concat_axis=0, tiled=True, axis_index_groups=groups)
+
+
+def flip(values, axis, bit, extent):
+    return lax.ppermute(values, axis, [(i, i ^ bit) for i in range(extent)])
+
+
+def shift(values, step):
+    return lax.ppermute(values, "tensor", [(i, (i + step) % 4) for i in range(4)])
 
 
 def pick_columns(weight, quarter):
-    span = 512
-    source = lax.broadcasted_iota(jnp.int32, (span, LANES), 0)
-    target = lax.broadcasted_iota(jnp.int32, (span, LANES), 1)
-    chosen = (source == (target // GROUP) * (GROUP * SEQS) + quarter * GROUP + target % GROUP).astype(bf16)
+    span = 1024
+    source = lax.broadcasted_iota(jnp.int32, (span, 2 * LANES), 0)
+    target = lax.broadcasted_iota(jnp.int32, (span, 2 * LANES), 1)
+    wanted = (target % LANES // GROUP) * 64 + (target // LANES) * 32 + quarter * GROUP + target % GROUP
+    chosen = (source == wanted).astype(bf16)
     parts = [
         jnp.dot(weight[:, start : start + span], chosen, preferred_element_type=f32).astype(bf16)
         for start in range(0, weight.shape[1], span)
     ]
-    return jnp.concatenate(parts, axis=1)
+    return jnp.stack([jnp.concatenate([part[:, side * LANES : (side + 1) * LANES] for part in parts], axis=1) for side in (0, 1)])
 
 
 def per_device(inputs, value_weight, query, key, filters, skip, cotangent):
     quarter = lax.axis_index("dp")
-    rows = value_weight.shape[0]
+    column = lax.axis_index("tensor")
+    side = lax.axis_index("context") % 2
+    place = jnp.stack([side, quarter // 2, quarter % 2]).astype(jnp.int32)
+    depth = value_weight.shape[0] * BLOCKS
+    half = value_weight.shape[1] // 8
+
     picked = pick_columns(value_weight, quarter)
-    half = picked.shape[1] // 2
-    halves = [
-        swap(jnp.broadcast_to(part[None], (BLOCKS,) + part.shape), "context").reshape(BLOCKS * rows, half)
-        for part in (picked[:, :half], picked[:, half:])
-    ]
-    tokens = lax.all_gather(inputs[0], "dp", axis=0, tiled=True)
+    weight = swap(
+        jnp.broadcast_to(picked[None], (BLOCKS // 2,) + picked.shape).reshape((BLOCKS,) + picked.shape[1:]),
+        "context",
+    ).reshape(depth, half)
+
+    tokens = jnp.concatenate([inputs[0], flip(inputs[0], "context", 1, BLOCKS)], axis=0)
+    tokens_y = flip(tokens, "dp", 2, SEQS)
+    tokens = jnp.concatenate([tokens, tokens_y, flip(tokens, "dp", 1, SEQS), flip(tokens_y, "dp", 1, SEQS)], axis=0)
+
+    partial = lax.dot_general(weight, tokens, (((0,), (1,)), ((), ())), preferred_element_type=f32).astype(bf16)
+    partial = partial.reshape(4, half // 4, partial.shape[1])
+
+    def block_of(values, index):
+        return lax.dynamic_index_in_dim(values, index % 4, 0, keepdims=False)
+
+    received = [shift(block_of(partial, column + step), step) for step in (1, 2, 3)]
+    value = block_of(partial, column).astype(f32)
+    for part in received:
+        value = value + part.astype(f32)
+    value = value.astype(bf16)
 
     query_part = query[0].astype(f32)
     upstream = cotangent[0].astype(f32)
     dconv = (upstream * query_part).astype(bf16)
     pair = jnp.concatenate([dconv.reshape(ROWS, 1, GROUP, LANES), key[0].reshape(ROWS, 1, GROUP, LANES)], axis=1)
-    pair = swap(pair, ("context", "dp")).reshape(2 * SIGNAL, LANES)
+    pair, weight_done = lax.optimization_barrier((pair, weight))
+    pair = swap(pair, ("context", "dp"))
+
+    value = value.reshape(BLOCKS // 2, GROUP, 2 * SEQS * LANES)
+    value, pair = lax.optimization_barrier((value, pair))
+    pair = pair.reshape(2 * SIGNAL, LANES)
+    groups = [[2 * k + s for k in range(BLOCKS // 2)] for s in (0, 1)]
+    value = swap(value, "context", groups)
+
     own_filters = lax.dynamic_slice_in_dim(filters, quarter * GROUP, GROUP, 0)
     own_skip = lax.dynamic_slice_in_dim(skip, quarter * GROUP, GROUP, 0)
     dmix, dvalue, taps = early(own_filters, own_skip, pair)
-    dvalue = swap(dvalue.reshape(BLOCKS, GROUP, SEQS * LANES), "context").reshape(BLOCKS * GROUP, SEQS * LANES)
-    dvalue = lax.all_gather(dvalue, "tensor", axis=0, tiled=True)
-
-    weight = jnp.concatenate(halves, axis=1)
-    partial = lax.dot_general(weight, tokens, (((0,), (1,)), ((), ())), preferred_element_type=f32).astype(bf16)
-    partial = swap(partial.reshape(4, BLOCKS * GROUP, SEQS * LANES), "tensor").astype(f32)
-    value = (partial[0] + partial[1] + partial[2] + partial[3]).astype(bf16)
-    value = swap(value.reshape(BLOCKS, GROUP, SEQS * LANES), "context").reshape(BLOCKS * GROUP, SEQS * LANES)
-    out, fgrad = late(taps, own_skip, pair, value, dmix)
+    dvalue, value = lax.optimization_barrier((dvalue, value))
+    dvalue = swap(dvalue.reshape(BLOCKS, GROUP, SEQS * LANES), "context")
+
+    value = value.reshape(BLOCKS * GROUP // 2, 2 * SEQS * LANES)
+    out, mix = late_conv(taps, own_skip, place, pair, value, dmix)
+    out, dvalue = lax.optimization_barrier((out, dvalue))
     out = swap(out.reshape(ROWS, 2, GROUP, LANES), ("context", "dp"))
+    fgrad = late_fgrad(pair, mix)
+    filter_grad = lax.all_gather(fgrad, "dp", axis=0, tiled=True).astype(f32)
+    skip_grad = filter_grad[:, 0]
+
+    dvalue = dvalue.reshape(BLOCKS // 2, 2, GROUP, SEQS * LANES)
+    sides = [
+        lax.dynamic_index_in_dim(dvalue, index, 1, keepdims=False).reshape(LANES, SEQS * LANES)
+        for index in (side, 1 - side)
+    ]
+    dvalue = jnp.concatenate(sides, axis=0)
+    dvalue = jnp.concatenate([dvalue] + [shift(dvalue, -step) for step in (1, 2, 3)], axis=0)
+    other = flip(weight_done, "context", 1, BLOCKS)
+    columns = []
+    for step in range(4):
+        for part in (weight_done, other):
+            columns.append(lax.dynamic_slice_in_dim(part, (column + step) % 4 * LANES, LANES, 1))
+    weight_all = jnp.concatenate(columns, axis=1)
+    grad = lax.dot_general(dvalue, weight_all, (((0,), (1,)), ((), ())), preferred_element_type=f32).astype(bf16)
+    grad = grad.reshape(SEQS, LANES, depth)
+    received = [flip(block_of(grad, quarter ^ step), "dp", step, SEQS) for step in (1, 2, 3)]
+    input_grad = block_of(grad, quarter).astype(f32)
+    for part in received:
+        input_grad = input_grad + part.astype(f32)
+    input_grad = input_grad.astype(bf16)
+
     conv = out[:, 0].reshape(SIGNAL, LANES).astype(f32)
     key_grad = out[:, 1].reshape(SIGNAL, LANES)
     gated = (query_part * conv).astype(bf16)
     query_grad = (upstream * conv).astype(bf16)
-    filter_grad = lax.all_gather(fgrad, "dp", axis=0, tiled=True).astype(f32)
-    skip_grad = filter_grad[:, 0]
-
-    grad = lax.dot_general(dvalue, weight, (((0,), (1,)), ((), ())), preferred_element_type=f32).astype(bf16)
-    grad = swap(grad.reshape(SEQS, LANES, grad.shape[1]), "dp").astype(f32)
-    input_grad = (grad[0] + grad[1] + grad[2] + grad[3]).astype(bf16)
     return (gated[None], query_grad[None], key_grad[None], input_grad[None], filter_grad, skip_grad)
 
 

time: 252 us -> 233 us (0.925)
  waiting for transfers between devices: 95.8 us -> 43.3 us
  starting transfers between devices: 60.4 us -> 110 us
  blocking collectives: 37.7 us -> 6.13 us
  local copies, waits for them, and re-layouts: 3.78 us -> 25.5 us
  between operations: 15.7 us -> 1.26 us
    all_to_all x7 -> x5, waiting for transfers between devices: 94.5 us -> 3.22 us  [swap(): lax.all_to_all(values, axes, split_axis=0, concat_axis=0, tiled=True, axi...]
    ppermute x0 -> x14, starting transfers between devices: none -> 44 us  [the longest x8 27.5 us: flip(): return lax.ppermute(values, axis, [(i, i ^ bit) for i in range(extent)])]
    ppermute x0 -> x14, waiting for transfers between devices: none -> 40.1 us  [the longest x8 31 us: flip(): return lax.ppermute(values, axis, [(i, i ^ bit) for i in range(extent)])]
    all_to_all x1 -> x0, blocking collectives: 21.1 us -> none  [swap(): return lax.all_to_all(values, axes, split_axis=0, concat_axis=0, tiled=True)]
    unnamed x16 -> x33, local copies, waits for them, and re-layouts: 0.04 us -> 16.9 us
    all_gather x1, blocking collectives: 16.6 us -> 6.13 us  [per_device(): filter_grad = lax.all_gather(fgrad, 'dp', axis=0, tiled=True).astype(f32)]
    all_to_all x7 -> x5, starting transfers between devices: 60.4 us -> 66.5 us  [swap(): lax.all_to_all(values, axes, split_axis=0, concat_axis=0, tiled=True, axi...]
    concatenate x0 -> x3, local copies, waits for them, and re-layouts: none -> 4.28 us  [the longest x1 1.88 us: per_device(): jnp.concatenate([tokens, tokens_y, flip(tokens, 'dp', 1, SEQS), flip(toke...]
  transfers between devices with their start and end apart: 9 -> 19, of which waited for: 6 -> 5; matrix products, arithmetic and copies ran while one was open for 4% -> 13% of each run, Pallas kernels for 10% -> 11%
where the time goes in v1:
time: 233 us; the launch traced here: 232 us
  starting transfers between devices  110 us (47%)
  waiting for transfers between devices  43.3 us (19%)
  Pallas kernels  26.5 us (11%)
  local copies, waits for them, and re-layouts  25.5 us (11%)
  matrix products  10.5 us (5%)
  other arithmetic  7.98 us (3%)
  blocking collectives  6.13 us (3%)
    all_to_all x5, starting transfers between devices, swap(): lax.all_to_all(values, axes, split_axis=0, concat_axis=0, tiled=True, axi...  66.5 us
    ppermute x8, waiting for transfers between devices, flip(): return lax.ppermute(values, axis, [(i, i ^ bit) for i in range(extent)])  31 us
    ppermute x8, starting transfers between devices, flip(): return lax.ppermute(values, axis, [(i, i ^ bit) for i in range(extent)])  27.5 us
    unnamed x33, local copies, waits for them, and re-layouts  16.9 us
    ppermute x6, starting transfers between devices, shift(): lax.ppermute(values, 'tensor', [(i, (i + step) % 4) for i in range(4)])  16.5 us
    pallas_call x1, Pallas kernels, early(): pl.pallas_call(early_kernel, grid=(GROUP,), in_specs=[whole((GROUP, TAPS)...  9.38 us
    pallas_call x1, Pallas kernels, late_conv(): pl.pallas_call(conv_kernel, grid=(GROUP,), in_specs=[taps_spec, smem, sme...  9.33 us
    ppermute x6, waiting for transfers between devices, shift(): lax.ppermute(values, 'tensor', [(i, (i + step) % 4) for i in range(4)])  9.02 us
  transfers between devices with their start and end apart: 19, of which 5 were waited for; matrix products, arithmetic and copies ran while one was open for 13% of the time, Pallas kernels for 11%

profile of v1, /device:TPU:1, one launch (start us, length us, event | category | flops | bytes accessed | tf_op | source)
XLA Modules:
  0.0 231.6 jit_solution(4971599421066815829)
XLA Ops:
  0.7 0.2 fusion.9
  0.9 1.1 fusion.3
  2.0 1.1 fusion.2
  3.1 1.1 fusion.1
  4.2 1.1 fusion
  5.4 1.1 broadcast_in_dim.4
  6.6 16.5 %all-to-all-start = ((bf16[32,32,512]{2,1,0:T(8,128)(2,1)}), bf16[32,32,512]{2,1,0:T(8,128)(2,1)S(1)}, u32[]{:S(2)}, u32[]{:S(2)}) async-start(bf16[32,32,512]{2,1,0:T(8,128)(2,1)} %bitcast.6), calls=%async_computation | async-start | bytes 2097152 | tf_op jit(solution)/shard_map/all_to_all | solution.py:220
  23.1 3.1 %collective-permute-start = (bf16[128,1024]{1,0:T(8,128)(2,1)S(1)}, bf16[128,1024]{1,0:T(8,128)(2,1)S(1)}, u32[]{:S(2)}, u32[]{:S(2)}) collective-permute-start(bf16[128,1024]{1,0:T(8,128)(2,1)S(1)} %bitcast.92), channel_id=1, source_target_pairs={{0,1},{1,0},{2,3},{3,2},{4,5},{5,4},{6,7},{7,6},{8,9},{9,8},{10,11... | collective-permute-start | bytes 786440 | tf_op jit(solution)/shard_map/ppermute | solution.py:224
  26.2 24.3 %collective-permute-done = bf16[128,1024]{1,0:T(8,128)(2,1)S(1)} collective-permute-done((bf16[128,1024]{1,0:T(8,128)(2,1)S(1)}, bf16[128,1024]{1,0:T(8,128)(2,1)S(1)}, u32[]{:S(2)}, u32[]{:S(2)}) %collective-permute-start) | collective-permute-done | bytes 262176 | tf_op jit(solution)/shard_map/ppermute | solution.py:224
  50.5 0.8 pad_maximum_fusion
  51.4 4.8 %collective-permute-start.1 = (bf16[256,1024]{1,0:T(8,128)(2,1)}, bf16[256,1024]{1,0:T(8,128)(2,1)S(1)}, u32[]{:S(2)}, u32[]{:S(2)}) collective-permute-start(bf16[256,1024]{1,0:T(8,128)(2,1)} %pad_maximum_fusion), channel_id=1, source_target_pairs={{0,256},{128,384},{256,0},{384,128},{1,257},{129,385},{257,1},{385... | collective-permute-start | bytes 1572872 | tf_op jit(solution)/shard_map/ppermute | solution.py:224
  56.2 3.5 %collective-permute-start.2 = (bf16[256,1024]{1,0:T(8,128)(2,1)}, bf16[256,1024]{1,0:T(8,128)(2,1)}, u32[]{:S(2)}, u32[]{:S(2)}) collective-permute-start(bf16[256,1024]{1,0:T(8,128)(2,1)} %pad_maximum_fusion), channel_id=1, source_target_pairs={{0,128},{128,0},{256,384},{384,256},{1,129},{129,1},{257,385},{385... | collective-permute-start | bytes 1572872 | tf_op jit(solution)/shard_map/ppermute | solution.py:224
  59.8 6.7 %collective-permute-done.1 = bf16[256,1024]{1,0:T(8,128)(2,1)S(1)} collective-permute-done((bf16[256,1024]{1,0:T(8,128)(2,1)}, bf16[256,1024]{1,0:T(8,128)(2,1)S(1)}, u32[]{:S(2)}, u32[]{:S(2)}) %collective-permute-start.1) | collective-permute-done | bytes 524320 | tf_op jit(solution)/shard_map/ppermute | solution.py:224
  66.5 4.6 %collective-permute-start.3 = (bf16[256,1024]{1,0:T(8,128)(2,1)S(1)}, bf16[256,1024]{1,0:T(8,128)(2,1)}, u32[]{:S(2)}, u32[]{:S(2)}) collective-permute-start(bf16[256,1024]{1,0:T(8,128)(2,1)S(1)} %collective-permute-done.1), channel_id=1, source_target_pairs={{0,128},{128,0},{256,384},{384,256},{1,129},{129,1},{257,385},{385... | collective-permute-start | bytes 1572872 | tf_op jit(solution)/shard_map/ppermute | solution.py:224
  71.1 0.7 constant_dynamic-update-slice_fusion.4
  71.8 1.8 pad_maximum_fusion.1
  73.7 0.7 constant_dynamic-update-slice_fusion.3
  74.4 0.9 constant_dynamic-update-slice_fusion.2
  75.3 1.9 constant_dynamic-update-slice_fusion.1
  77.2 14.2 %all-to-all-start.1 = ((bf16[128,2,8,128]{3,2,1,0:T(8,128)(2,1)}), bf16[128,2,8,128]{3,2,1,0:T(8,128)(2,1)S(1)}, u32[]{:S(2)}, u32[]{:S(2)}) async-start(bf16[128,2,8,128]{3,2,1,0:T(8,128)(2,1)} %pad_maximum_fusion.1), calls=%async_computation.1 | async-start | bytes 1048576 | tf_op jit(solution)/shard_map/all_to_all | solution.py:220
  91.4 1.9 constant_dynamic-update-slice_fusion
  93.3 2.9 %convolution_convert_fusion.1 = bf16[512,1024]{1,0:T(8,128)(2,1)S(1)} fusion(bf16[1024,512]{1,0:T(8,128)(2,1)S(1)} %bitcast.82, bf16[1024,1024]{1,0:T(8,128)(2,1)} %constant_dynamic-update-slice_fusion), kind=kOutput, calls=%fused_computation.8 | convolution fusion | flops 1074266112 | bytes 4194304 | tf_op jit(solution)/shard_map/dot_general | solution.py:262
  96.2 0.9 dynamic-slice_bitcast_fusion.5
  97.0 4.4 %collective-permute-start.6 = (bf16[128,1024]{1,0:T(8,128)(2,1)}, bf16[128,1024]{1,0:T(8,128)(2,1)S(1)}, u32[]{:S(2)}, u32[]{:S(2)}) collective-permute-start(bf16[128,1024]{1,0:T(8,128)(2,1)} %get-tuple-element.40), channel_id=1, source_target_pairs={{0,96},{32,0},{64,32},{96,64},{1,97},{33,1},{65,33},{97,65},{2,98}... | collective-permute-start | bytes 786440 | tf_op jit(solution)/shard_map/ppermute | solution.py:228
  101.4 2.4 %collective-permute-start.5 = (bf16[128,1024]{1,0:T(8,128)(2,1)S(1)}, bf16[128,1024]{1,0:T(8,128)(2,1)}, u32[]{:S(2)}, u32[]{:S(2)}) collective-permute-start(bf16[128,1024]{1,0:T(8,128)(2,1)S(1)} %get-tuple-element.41), channel_id=1, source_target_pairs={{0,64},{32,96},{64,0},{96,32},{1,65},{33,97},{65,1},{97,33},{2,66}... | collective-permute-start | bytes 786440 | tf_op jit(solution)/shard_map/ppermute | solution.py:228
  103.9 2.5 %collective-permute-start.4 = (bf16[128,1024]{1,0:T(8,128)(2,1)S(1)}, bf16[128,1024]{1,0:T(8,128)(2,1)}, u32[]{:S(2)}, u32[]{:S(2)}) collective-permute-start(bf16[128,1024]{1,0:T(8,128)(2,1)S(1)} %get-tuple-element.39), channel_id=1, source_target_pairs={{0,32},{32,64},{64,96},{96,0},{1,33},{33,65},{65,97},{97,1},{2,34}... | collective-permute-start | bytes 786440 | tf_op jit(solution)/shard_map/ppermute | solution.py:228
  106.4 3.3 %collective-permute-start.10 = (bf16[1024,512]{1,0:T(8,128)(2,1)S(1)}, bf16[1024,512]{1,0:T(8,128)(2,1)}, u32[]{:S(2)}, u32[]{:S(2)}) collective-permute-start(bf16[1024,512]{1,0:T(8,128)(2,1)S(1)} %bitcast.83), channel_id=1, source_target_pairs={{0,1},{1,0},{2,3},{3,2},{4,5},{5,4},{6,7},{7,6},{8,9},{9,8},{10,11... | collective-permute-start | bytes 3145736 | tf_op jit(solution)/shard_map/ppermute | solution.py:224
  109.8 1.8 collective-permute-done.5
  111.6 7.2 %collective-permute-done.4 = bf16[128,1024]{1,0:T(8,128)(2,1)} collective-permute-done((bf16[128,1024]{1,0:T(8,128)(2,1)S(1)}, bf16[128,1024]{1,0:T(8,128)(2,1)}, u32[]{:S(2)}, u32[]{:S(2)}) %collective-permute-start.4) | collective-permute-done | bytes 262176 | tf_op jit(solution)/shard_map/ppermute | solution.py:228
  118.8 2.0 fusion.23
  120.8 11.9 %all-to-all-start.2 = ((bf16[16,8,1024]{2,1,0:T(8,128)(2,1)}), bf16[16,8,1024]{2,1,0:T(8,128)(2,1)S(1)}, u32[]{:S(2)}, u32[]{:S(2)}) async-start(bf16[16,8,1024]{2,1,0:T(8,128)(2,1)} %fusion.23), calls=%async_computation.2 | async-start | bytes 524288 | tf_op jit(solution)/shard_map/all_to_all | solution.py:220
  132.9 9.4 %early.1 = (bf16[1024,128]{1,0:T(8,128)(2,1)S(1)}, bf16[256,512]{1,0:T(8,128)(2,1)}, bf16[8,4096,128]{2,1,0:T(8,128)(2,1)}) custom-call(f32[8,4096]{1,0:T(8,128)S(1)} %constant_dynamic-slice_fusion.filters_ref, f32[8]{0:T(128)S(1)} %dynamic_slice.63.skip_ref, bf16[2048,128]{1,0:T(8,128)(2,1)S(1)} %bitcast.78), custom_call_target="tpu_custom_call" | custom-call | tf_op jit(solution)/shard_map/early/pallas_call | solution.py:150
  142.3 3.2 %all-to-all-done.2 = bf16[16,8,1024]{2,1,0:T(8,128)(2,1)S(1)} async-done(((bf16[16,8,1024]{2,1,0:T(8,128)(2,1)}), bf16[16,8,1024]{2,1,0:T(8,128)(2,1)S(1)}, u32[]{:S(2)}, u32[]{:S(2)}) %all-to-all-start.2) | async-done | bytes 262176 | tf_op jit(solution)/shard_map/all_to_all | solution.py:220
  145.5 8.7 %all-to-all-start.3 = ((bf16[32,8,512]{2,1,0:T(8,128)(2,1)}), bf16[32,8,512]{2,1,0:T(8,128)(2,1)}, u32[]{:S(2)}, u32[]{:S(2)}) async-start(bf16[32,8,512]{2,1,0:T(8,128)(2,1)} %bitcast.24), calls=%async_computation.3 | async-start | bytes 524288 | tf_op jit(solution)/shard_map/all_to_all | solution.py:220
  154.3 1.0 dynamic-slice_dynamic-update-slice_fusion.6
  155.4 0.1 dynamic-slice_dynamic-update-slice_fusion.5
  155.5 1.0 dynamic-slice_dynamic-update-slice_fusion.4
  156.5 0.1 dynamic-slice_dynamic-update-slice_fusion.3
  156.6 1.3 copy-done.7
  158.0 9.3 %late_conv.1 = (bf16[2048,128]{1,0:T(8,128)(2,1)}, bf16[1024,128]{1,0:T(8,128)(2,1)S(1)}) custom-call(bf16[8,4096,128]{2,1,0:T(8,128)(2,1)} %get-tuple-element.21.taps_ref, f32[8]{0:T(128)S(1)} %dynamic_slice.63.skip_ref, s32[3]{0:T(128)S(1)} %pad_add_fusion.place_ref, bf16[2048,128]{1,0:T(8,128)(2,1)S(1)} %bitcast.79, bf16[128,1024]{1,0:T(8,128)(2,1)S(1)} %bitcast.81, ...), custom_call_target="tpu_custom_call" | custom-call | tf_op jit(solution)/shard_map/late_conv/pallas_call | solution.py:173
  167.3 1.6 constant_dynamic-update-slice_fusion.9
  168.8 1.6 constant_dynamic-update-slice_fusion.8
  170.4 1.9 collective-permute-start.7
  172.4 1.7 dynamic-slice_dynamic-update-slice_fusion.2
  174.1 2.4 %collective-permute-start.8 = (bf16[256,512]{1,0:T(8,128)(2,1)S(1)}, bf16[256,512]{1,0:T(8,128)(2,1)}, u32[]{:S(2)}, u32[]{:S(2)}) collective-permute-start(bf16[256,512]{1,0:T(8,128)(2,1)S(1)} %pad_maximum_fusion.2), channel_id=1, source_target_pairs={{0,64},{32,96},{64,0},{96,32},{1,65},{33,97},{65,1},{97,33},{2,66}... | collective-permute-start | bytes 786440 | tf_op jit(solution)/shard_map/ppermute | solution.py:228
  176.5 0.8 dynamic-slice_dynamic-update-slice_fusion.1
  177.2 2.9 %collective-permute-start.9 = (bf16[256,512]{1,0:T(8,128)(2,1)S(1)}, bf16[256,512]{1,0:T(8,128)(2,1)S(1)}, u32[]{:S(2)}, u32[]{:S(2)}) collective-permute-start(bf16[256,512]{1,0:T(8,128)(2,1)S(1)} %pad_maximum_fusion.2), channel_id=1, source_target_pairs={{0,32},{32,64},{64,96},{96,0},{1,33},{33,65},{65,97},{97,1},{2,34}... | collective-permute-start | bytes 786440 | tf_op jit(solution)/shard_map/ppermute | solution.py:228
  180.1 1.7 dynamic-slice_dynamic-update-slice_fusion
  181.8 15.1 %all-to-all-start.4 = ((bf16[128,2,8,128]{3,2,1,0:T(8,128)(2,1)}), bf16[128,2,8,128]{3,2,1,0:T(8,128)(2,1)S(1)}, u32[]{:S(2)}, u32[]{:S(2)}) async-start(bf16[128,2,8,128]{3,2,1,0:T(8,128)(2,1)} %bitcast.25), calls=%async_computation.4 | async-start | bytes 1048576 | tf_op jit(solution)/shard_map/all_to_all | solution.py:220
  196.9 0.7 constant_dynamic-update-slice_fusion.7
  197.7 1.7 constant_dynamic-update-slice_fusion.6
  199.3 0.7 constant_dynamic-update-slice_fusion.5
  200.1 3.2 %convolution_convert_fusion = bf16[512,1024]{1,0:T(8,128)(2,1)S(1)} fusion(bf16[1024,512]{1,0:T(8,128)(2,1)} %constant_dynamic-update-slice_fusion.5, bf16[1024,1024]{1,0:T(8,128)(2,1)} %dynamic-slice_dynamic-update-slice_fusion), kind=kOutput, calls=%fused_computation.7 | convolution fusion | flops 1074266112 | bytes 4194304 | tf_op jit(solution)/shard_map/dot_general | solution.py:314
  203.3 1.0 copy-done.4
  204.3 0.8 dynamic-slice_bitcast_fusion.2
  205.1 3.5 %collective-permute-start.13 = (bf16[128,1024]{1,0:T(8,128)(2,1)}, bf16[128,1024]{1,0:T(8,128)(2,1)S(1)}, u32[]{:S(2)}, u32[]{:S(2)}) collective-permute-start(bf16[128,1024]{1,0:T(8,128)(2,1)} %get-tuple-element.37), channel_id=1, source_target_pairs={{0,384},{128,256},{256,128},{384,0},{1,385},{129,257},{257,129},{3... | collective-permute-start | bytes 786440 | tf_op jit(solution)/shard_map/ppermute | solution.py:224
  208.7 2.7 %collective-permute-start.12 = (bf16[128,1024]{1,0:T(8,128)(2,1)}, bf16[128,1024]{1,0:T(8,128)(2,1)}, u32[]{:S(2)}, u32[]{:S(2)}) collective-permute-start(bf16[128,1024]{1,0:T(8,128)(2,1)} %get-tuple-element.38), channel_id=1, source_target_pairs={{0,256},{128,384},{256,0},{384,128},{1,257},{129,385},{257,1},{385... | collective-permute-start | bytes 786440 | tf_op jit(solution)/shard_map/ppermute | solution.py:224
  211.4 1.9 collective-permute-start.11
  213.3 7.8 %late_fgrad.1 = bf16[8,4096]{1,0:T(8,128)(2,1)S(1)} custom-call(bf16[2048,128]{1,0:T(8,128)(2,1)S(1)} %bitcast.80, bf16[1024,128]{1,0:T(8,128)(2,1)S(1)} %get-tuple-element.31.mix_ref), custom_call_target="tpu_custom_call" | custom-call | tf_op jit(solution)/shard_map/late_fgrad/pallas_call | solution.py:201
  221.1 6.1 %all_gather.3 = bf16[32,4096]{1,0:T(8,128)(2,1)S(1)} all-gather(bf16[8,4096]{1,0:T(8,128)(2,1)S(1)} %late_fgrad.1), channel_id=1, replica_groups=mesh['dp'=4,'tensor'=4,'context'=32] {'dp'}, dimensions={0}, use_global_device_ids=true | all-gather | bytes 327680 | tf_op jit(solution)/shard_map/all_gather | solution.py:298
  227.3 0.7 slice_reduce_fusion
  228.0 2.0 fusion.24
  230.0 0.9 fusion.16
  230.9 0.7 slice_bitcast_fusion
  (49 shorter events, 0.5 us)
Async XLA Ops:
  0.6 132.3 %copy-start = (f32[32,4096]{1,0:T(8,128)S(1)}, f32[32,4096]{1,0:T(8,128)}, u32[]{:S(2)}) copy-start(f32[32,4096]{1,0:T(8,128)} %param.11) | copy-start | bytes 1572868
  3.1 20.0 %copy-start.5 = (bf16[1,128,1024]{2,1,0:T(8,128)(2,1)S(1)}, bf16[1,128,1024]{2,1,0:T(8,128)(2,1)}, u32[]{:S(2)}) copy-start(bf16[1,128,1024]{2,1,0:T(8,128)(2,1)} %param.7) | copy-start | bytes 786436
  5.4 50.7 %copy-start.1 = (bf16[1,1024,128]{2,1,0:T(8,128)(2,1)S(1)}, bf16[1,1024,128]{2,1,0:T(8,128)(2,1)}, u32[]{:S(2)}) copy-start(bf16[1,1024,128]{2,1,0:T(8,128)(2,1)} %param.13) | copy-start | bytes 786436
  5.4 50.7 %copy-start.2 = (bf16[1,1024,128]{2,1,0:T(8,128)(2,1)S(1)}, bf16[1,1024,128]{2,1,0:T(8,128)(2,1)}, u32[]{:S(2)}) copy-start(bf16[1,1024,128]{2,1,0:T(8,128)(2,1)} %param.9) | copy-start | bytes 786436
  6.6 70.6 %all-to-all-start = ((bf16[32,32,512]{2,1,0:T(8,128)(2,1)}), bf16[32,32,512]{2,1,0:T(8,128)(2,1)S(1)}, u32[]{:S(2)}, u32[]{:S(2)}) async-start(bf16[32,32,512]{2,1,0:T(8,128)(2,1)} %bitcast.6), calls=%async_computation | async-start | bytes 2097152 | tf_op jit(solution)/shard_map/all_to_all | solution.py:220
  23.1 27.5 %collective-permute-start = (bf16[128,1024]{1,0:T(8,128)(2,1)S(1)}, bf16[128,1024]{1,0:T(8,128)(2,1)S(1)}, u32[]{:S(2)}, u32[]{:S(2)}) collective-permute-start(bf16[128,1024]{1,0:T(8,128)(2,1)S(1)} %bitcast.92), channel_id=1, source_target_pairs={{0,1},{1,0},{2,3},{3,2},{4,5},{5,4},{6,7},{7,6},{8,9},{9,8},{10,11... | collective-permute-start | bytes 786440 | tf_op jit(solution)/shard_map/ppermute | solution.py:224
  51.4 15.1 %collective-permute-start.1 = (bf16[256,1024]{1,0:T(8,128)(2,1)}, bf16[256,1024]{1,0:T(8,128)(2,1)S(1)}, u32[]{:S(2)}, u32[]{:S(2)}) collective-permute-start(bf16[256,1024]{1,0:T(8,128)(2,1)} %pad_maximum_fusion), channel_id=1, source_target_pairs={{0,256},{128,384},{256,0},{384,128},{1,257},{129,385},{257,1},{385... | collective-permute-start | bytes 1572872 | tf_op jit(solution)/shard_map/ppermute | solution.py:224
  56.2 19.0 %collective-permute-start.2 = (bf16[256,1024]{1,0:T(8,128)(2,1)}, bf16[256,1024]{1,0:T(8,128)(2,1)}, u32[]{:S(2)}, u32[]{:S(2)}) collective-permute-start(bf16[256,1024]{1,0:T(8,128)(2,1)} %pad_maximum_fusion), channel_id=1, source_target_pairs={{0,128},{128,0},{256,384},{384,256},{1,129},{129,1},{257,385},{385... | collective-permute-start | bytes 1572872 | tf_op jit(solution)/shard_map/ppermute | solution.py:224
  66.5 24.9 %collective-permute-start.3 = (bf16[256,1024]{1,0:T(8,128)(2,1)S(1)}, bf16[256,1024]{1,0:T(8,128)(2,1)}, u32[]{:S(2)}, u32[]{:S(2)}) collective-permute-start(bf16[256,1024]{1,0:T(8,128)(2,1)S(1)} %collective-permute-done.1), channel_id=1, source_target_pairs={{0,128},{128,0},{256,384},{384,256},{1,129},{129,1},{257,385},{385... | collective-permute-start | bytes 1572872 | tf_op jit(solution)/shard_map/ppermute | solution.py:224
  77.2 43.6 %all-to-all-start.1 = ((bf16[128,2,8,128]{3,2,1,0:T(8,128)(2,1)}), bf16[128,2,8,128]{3,2,1,0:T(8,128)(2,1)S(1)}, u32[]{:S(2)}, u32[]{:S(2)}) async-start(bf16[128,2,8,128]{3,2,1,0:T(8,128)(2,1)} %pad_maximum_fusion.1), calls=%async_computation.1 | async-start | bytes 1048576 | tf_op jit(solution)/shard_map/all_to_all | solution.py:220
  96.2 7.7 %copy-start.3 = (bf16[512,1024]{1,0:T(8,128)(2,1)}, bf16[512,1024]{1,0:T(8,128)(2,1)S(1)}, u32[]{:S(2)}) copy-start(bf16[512,1024]{1,0:T(8,128)(2,1)S(1)} %convolution_convert_fusion.1) | copy-start | bytes 3145732
  96.2 36.6 %copy-start.8 = (f32[32]{0:T(128)S(1)}, f32[32]{0:T(128)}, u32[]{:S(2)}) copy-start(f32[32]{0:T(128)} %param.12) | copy-start | bytes 388
  97.0 12.7 %collective-permute-start.6 = (bf16[128,1024]{1,0:T(8,128)(2,1)}, bf16[128,1024]{1,0:T(8,128)(2,1)S(1)}, u32[]{:S(2)}, u32[]{:S(2)}) collective-permute-start(bf16[128,1024]{1,0:T(8,128)(2,1)} %get-tuple-element.40), channel_id=1, source_target_pairs={{0,96},{32,0},{64,32},{96,64},{1,97},{33,1},{65,33},{97,65},{2,98}... | collective-permute-start | bytes 786440 | tf_op jit(solution)/shard_map/ppermute | solution.py:228
  101.4 10.2 %collective-permute-start.5 = (bf16[128,1024]{1,0:T(8,128)(2,1)S(1)}, bf16[128,1024]{1,0:T(8,128)(2,1)}, u32[]{:S(2)}, u32[]{:S(2)}) collective-permute-start(bf16[128,1024]{1,0:T(8,128)(2,1)S(1)} %get-tuple-element.41), channel_id=1, source_target_pairs={{0,64},{32,96},{64,0},{96,32},{1,65},{33,97},{65,1},{97,33},{2,66}... | collective-permute-start | bytes 786440 | tf_op jit(solution)/shard_map/ppermute | solution.py:228
  103.9 14.9 %collective-permute-start.4 = (bf16[128,1024]{1,0:T(8,128)(2,1)S(1)}, bf16[128,1024]{1,0:T(8,128)(2,1)}, u32[]{:S(2)}, u32[]{:S(2)}) collective-permute-start(bf16[128,1024]{1,0:T(8,128)(2,1)S(1)} %get-tuple-element.39), channel_id=1, source_target_pairs={{0,32},{32,64},{64,96},{96,0},{1,33},{33,65},{65,97},{97,1},{2,34}... | collective-permute-start | bytes 786440 | tf_op jit(solution)/shard_map/ppermute | solution.py:228
  106.4 47.9 %collective-permute-start.10 = (bf16[1024,512]{1,0:T(8,128)(2,1)S(1)}, bf16[1024,512]{1,0:T(8,128)(2,1)}, u32[]{:S(2)}, u32[]{:S(2)}) collective-permute-start(bf16[1024,512]{1,0:T(8,128)(2,1)S(1)} %bitcast.83), channel_id=1, source_target_pairs={{0,1},{1,0},{2,3},{3,2},{4,5},{5,4},{6,7},{7,6},{8,9},{9,8},{10,11... | collective-permute-start | bytes 3145736 | tf_op jit(solution)/shard_map/ppermute | solution.py:224
  120.8 24.7 %all-to-all-start.2 = ((bf16[16,8,1024]{2,1,0:T(8,128)(2,1)}), bf16[16,8,1024]{2,1,0:T(8,128)(2,1)S(1)}, u32[]{:S(2)}, u32[]{:S(2)}) async-start(bf16[16,8,1024]{2,1,0:T(8,128)(2,1)} %fusion.23), calls=%async_computation.2 | async-start | bytes 524288 | tf_op jit(solution)/shard_map/all_to_all | solution.py:220
  145.5 21.8 %all-to-all-start.3 = ((bf16[32,8,512]{2,1,0:T(8,128)(2,1)}), bf16[32,8,512]{2,1,0:T(8,128)(2,1)}, u32[]{:S(2)}, u32[]{:S(2)}) async-start(bf16[32,8,512]{2,1,0:T(8,128)(2,1)} %bitcast.24), calls=%async_computation.3 | async-start | bytes 524288 | tf_op jit(solution)/shard_map/all_to_all | solution.py:220
  156.6 1.3 copy-start.7
  170.4 26.5 %collective-permute-start.7 = (bf16[256,512]{1,0:T(8,128)(2,1)S(1)}, bf16[256,512]{1,0:T(8,128)(2,1)S(1)}, u32[]{:S(2)}, u32[]{:S(2)}) collective-permute-start(bf16[256,512]{1,0:T(8,128)(2,1)S(1)} %pad_maximum_fusion.2), channel_id=1, source_target_pairs={{0,96},{32,0},{64,32},{96,64},{1,97},{33,1},{65,33},{97,65},{2,98}... | collective-permute-start | bytes 786440 | tf_op jit(solution)/shard_map/ppermute | solution.py:228
  174.1 23.6 %collective-permute-start.8 = (bf16[256,512]{1,0:T(8,128)(2,1)S(1)}, bf16[256,512]{1,0:T(8,128)(2,1)}, u32[]{:S(2)}, u32[]{:S(2)}) collective-permute-start(bf16[256,512]{1,0:T(8,128)(2,1)S(1)} %pad_maximum_fusion.2), channel_id=1, source_target_pairs={{0,64},{32,96},{64,0},{96,32},{1,65},{33,97},{65,1},{97,33},{2,66}... | collective-permute-start | bytes 786440 | tf_op jit(solution)/shard_map/ppermute | solution.py:228
  177.2 22.1 %collective-permute-start.9 = (bf16[256,512]{1,0:T(8,128)(2,1)S(1)}, bf16[256,512]{1,0:T(8,128)(2,1)S(1)}, u32[]{:S(2)}, u32[]{:S(2)}) collective-permute-start(bf16[256,512]{1,0:T(8,128)(2,1)S(1)} %pad_maximum_fusion.2), channel_id=1, source_target_pairs={{0,32},{32,64},{64,96},{96,0},{1,33},{33,65},{65,97},{97,1},{2,34}... | collective-permute-start | bytes 786440 | tf_op jit(solution)/shard_map/ppermute | solution.py:228
  181.8 48.2 %all-to-all-start.4 = ((bf16[128,2,8,128]{3,2,1,0:T(8,128)(2,1)}), bf16[128,2,8,128]{3,2,1,0:T(8,128)(2,1)S(1)}, u32[]{:S(2)}, u32[]{:S(2)}) async-start(bf16[128,2,8,128]{3,2,1,0:T(8,128)(2,1)} %bitcast.25), calls=%async_computation.4 | async-start | bytes 1048576 | tf_op jit(solution)/shard_map/all_to_all | solution.py:220
  203.3 1.0 copy-start.4
  205.1 22.9 %collective-permute-start.13 = (bf16[128,1024]{1,0:T(8,128)(2,1)}, bf16[128,1024]{1,0:T(8,128)(2,1)S(1)}, u32[]{:S(2)}, u32[]{:S(2)}) collective-permute-start(bf16[128,1024]{1,0:T(8,128)(2,1)} %get-tuple-element.37), channel_id=1, source_target_pairs={{0,384},{128,256},{256,128},{384,0},{1,385},{129,257},{257,129},{3... | collective-permute-start | bytes 786440 | tf_op jit(solution)/shard_map/ppermute | solution.py:224
  208.7 19.4 %collective-permute-start.12 = (bf16[128,1024]{1,0:T(8,128)(2,1)}, bf16[128,1024]{1,0:T(8,128)(2,1)}, u32[]{:S(2)}, u32[]{:S(2)}) collective-permute-start(bf16[128,1024]{1,0:T(8,128)(2,1)} %get-tuple-element.38), channel_id=1, source_target_pairs={{0,256},{128,384},{256,0},{384,128},{1,257},{129,385},{257,1},{385... | collective-permute-start | bytes 786440 | tf_op jit(solution)/shard_map/ppermute | solution.py:224
  211.4 16.7 %collective-permute-start.11 = (bf16[128,1024]{1,0:T(8,128)(2,1)S(1)}, bf16[128,1024]{1,0:T(8,128)(2,1)}, u32[]{:S(2)}, u32[]{:S(2)}) collective-permute-start(bf16[128,1024]{1,0:T(8,128)(2,1)S(1)} %get-tuple-element.36), channel_id=1, source_target_pairs={{0,128},{128,0},{256,384},{384,256},{1,129},{129,1},{257,385},{385... | collective-permute-start | bytes 786440 | tf_op jit(solution)/shard_map/ppermute | solution.py:224
  227.3 4.3 %copy-start.6 = (f32[32,4096]{1,0:T(8,128)}, f32[32,4096]{1,0:T(8,128)S(1)}, u32[]{:S(2)}) copy-start(f32[32,4096]{1,0:T(8,128)S(1)} %convert_element_type.159) | copy-start | bytes 1572868

commit v2 on v0

v2 whole, which is shorter than its diff:
```python
import jax
import jax.numpy as jnp
from jax import lax
from jax.experimental import pallas as pl
from jax.experimental.pallas import tpu as pltpu
from jax.sharding import PartitionSpec as P

f32 = jnp.float32
bf16 = jnp.bfloat16

LANES = 128
GROUP = 8
SEQS = 4
BLOCKS = 32
ROWS = BLOCKS * SEQS
SIGNAL = ROWS * GROUP
TAPS = BLOCKS * LANES
WIDE = TAPS + LANES
NEAR = ((0, 0), (1, 0), (3, 0), (2, 0), (2, 1), (3, 1), (1, 1), (0, 1))
HALF = 16
SPAN = 1024


def pack_kernel(quarter_ref, weight_ref, query_ref, upstream_ref, key_ref, out_ref, picks):
    step = pl.program_id(0)

    @pl.when(step == 0)
    def _():
        quarter = quarter_ref[0]
        source = lax.broadcasted_iota(jnp.int32, (SPAN, SPAN), 0)
        target = lax.broadcasted_iota(jnp.int32, (SPAN, SPAN), 1)
        wanted = (target % LANES // 4) * 32 + (target // LANES % SEQS) * GROUP + (target // LANES // SEQS) * 4 + target % 4
        chosen = (source == wanted).astype(f32).astype(bf16)
        row = pl.multiple_of(quarter // 2 * HALF, HALF)
        for slot in range(2):
            lane = pl.multiple_of((quarter % 2 * 2 + slot) * SPAN, SPAN)
            part = weight_ref[pl.ds(row, HALF), pl.ds(lane, SPAN)]
            picked = jnp.dot(part, chosen, preferred_element_type=f32).astype(bf16)
            for kind in range(GROUP):
                start = (kind * 2 + slot) * HALF
                picks[start : start + HALF, :] = picked[:, kind * LANES : (kind + 1) * LANES]

    dconv = upstream_ref[...].astype(f32) * query_ref[...].astype(f32)
    count = dconv.shape[0] // GROUP
    both = [dconv.reshape(count, 1, GROUP, LANES), key_ref[...].astype(f32).reshape(count, 1, GROUP, LANES)]
    both = jnp.concatenate(both, axis=1).reshape(count * HALF, LANES).astype(bf16)
    for dest in range(count):
        kind = dest % GROUP
        out_ref[dest * 48 : dest * 48 + 32, :] = picks[kind * 32 : kind * 32 + 32, :]
        out_ref[dest * 48 + 32 : dest * 48 + 48, :] = both[dest * HALF : (dest + 1) * HALF, :]


def load_pair(pair_ref):
    both = pair_ref[...].astype(f32).reshape(ROWS, 2, GROUP, LANES)
    return both[:, 0].reshape(SIGNAL, LANES), both[:, 1].reshape(SIGNAL, LANES)


def taps_kernel(filters_ref, taps_ref, rolled):
    chan = pl.program_id(0)

    @pl.when(chan == 0)
    def _():
        padded = jnp.concatenate([filters_ref[...], jnp.zeros((GROUP, LANES), f32)], axis=1)
        for row in range(GROUP):
            turned = pltpu.roll(padded, row, 1) if row else padded
            for block in range(BLOCKS + 1):
                rolled[block, row * GROUP : (row + 1) * GROUP, :] = turned[:, block * LANES : (block + 1) * LANES]

    base = jnp.concatenate(
        [rolled[block, pl.ds(chan, GROUP, stride=GROUP), :] for block in range(BLOCKS + 1)], axis=1
    )
    for pair in range(LANES // 16):
        low = pltpu.roll(base, 16 * pair, 1) if pair else base
        high = pltpu.roll(base, 16 * pair + 8, 1)
        tile = jnp.concatenate([low[:, :TAPS], high[:, :TAPS]], axis=0).astype(bf16)
        for block in range(BLOCKS):
            taps_ref[0, block * LANES + 16 * pair : block * LANES + 16 * pair + 16, :] = tile[
                :, block * LANES : (block + 1) * LANES
            ]


def fill_ahead(grads, copies, chan):
    for part in range(SEQS):
        copies[part, 0:ROWS, :] = grads[pl.ds(part * SEQS * GROUP + chan, ROWS, stride=GROUP), :].astype(bf16)


def ahead_of(copies, block):
    return copies[block % 4, block // 4 * 16 : block // 4 * 16 + ROWS, :]


def clear_ahead(grads, copies, dconv):
    grads[0:SIGNAL, :] = dconv
    grads[SIGNAL:, :] = jnp.zeros((LANES, LANES), f32)
    for part in range(SEQS):
        copies[part, ROWS:, :] = jnp.zeros((ROWS, LANES), bf16)


def dmix_kernel(taps0, taps1, taps2, taps3, skip_ref, pair_ref, dmix_ref, dvalue_ref, grads, copies, result):
    chan = pl.program_id(0)

    @pl.when(chan == 0)
    def _():
        clear_ahead(grads, copies, load_pair(pair_ref)[0])

    fill_ahead(grads, copies, chan)
    ahead = jnp.concatenate([ahead_of(copies, block) for block in range(BLOCKS)], axis=1)
    refs = (taps0, taps1, taps2, taps3)
    wide = jnp.concatenate(
        [refs[block // 8][0, block % 8 * LANES : (block % 8 + 1) * LANES, :] for block in range(BLOCKS)], axis=1
    )
    total = lax.dot_general(ahead, wide, (((1,), (1,)), ((), ())), preferred_element_type=f32)
    own = grads[pl.ds(chan, ROWS, stride=GROUP), :]
    result[pl.ds(chan, ROWS, stride=GROUP), :] = total + skip_ref[chan] * own

    @pl.when(chan == GROUP - 1)
    def _():
        _, key = load_pair(pair_ref)
        dmix = result[...].astype(bf16)
        dmix_ref[...] = dmix
        dvalue = (dmix.astype(f32) * key).reshape(BLOCKS, SEQS, GROUP, LANES)
        for seq in range(SEQS):
            dvalue_ref[:, seq * LANES : (seq + 1) * LANES] = (
                dvalue[:, seq].reshape(BLOCKS * GROUP, LANES).astype(bf16)
            )


def project_kernel(column_ref, packed_ref, tokens_ref, out0, out1, out2, out3, low_ref, high_ref):
    part = packed_ref[...].reshape(SPAN, LANES)
    index = (column_ref[0] + pl.program_id(0)) % 4
    lanes = pl.ds(pl.multiple_of(index % 2 * LANES, LANES), LANES)

    @pl.when(index < 2)
    def _():
        low_ref[:, lanes] = part

    @pl.when(index >= 2)
    def _():
        high_ref[:, lanes] = part

    product = lax.dot_general(part, tokens_ref[...], (((0,), (1,)), ((), ())), preferred_element_type=f32)
    product = product.astype(bf16)
    for step, out_ref in enumerate((out0, out1, out2, out3)):

        @pl.when(pl.program_id(0) == step)
        def _():
            out_ref[...] = product


def halves_of(even, odd):
    upper = lax.broadcasted_iota(jnp.int32, even.shape, 0) < 4
    return jnp.where(upper, even, pltpu.roll(odd, 4, 0)), jnp.where(upper, pltpu.roll(even, 4, 0), odd)


def join_kernel(part0, part1, part2, part3, dvalue_ref, out_ref):
    value = part0[...].astype(f32) + part1[...].astype(f32) + part2[...].astype(f32) + part3[...].astype(f32)
    value = value.astype(bf16).astype(f32)
    dvalue = dvalue_ref[...].astype(f32)
    lanes = SEQS * LANES
    for two in range(BLOCKS // 2):
        rows = value[two * GROUP : (two + 1) * GROUP, :]
        for place, tile in enumerate(halves_of(rows[:, :lanes], rows[:, lanes:])):
            index = 2 * two + place
            tile = jnp.concatenate([tile, dvalue[index * GROUP : (index + 1) * GROUP, :]], axis=0)
            out_ref[index * HALF : (index + 1) * HALF, :] = tile.astype(bf16)


def back_kernel(place_ref, dvalue_ref, low, high, other_low, other_high, fgrad_ref, sent_ref, kept_ref, total):
    first = place_ref[0] == 0
    for index in range(4):
        dvalue = dvalue_ref[index * BLOCKS * GROUP : (index + 1) * BLOCKS * GROUP, :].astype(f32)
        tiles = [[], []]
        for two in range(BLOCKS // 2):
            start = two * HALF
            pair = halves_of(dvalue[start : start + GROUP, :], dvalue[start + GROUP : start + HALF, :])
            for half in range(2):
                tiles[half].append(pair[half])
        upper, lower = [jnp.concatenate(part, axis=0).astype(bf16) for part in tiles]
        rows = jnp.concatenate([jnp.where(first, upper, lower), jnp.where(first, lower, upper)], axis=0)
        lanes = slice(index % 2 * LANES, (index % 2 + 1) * LANES)
        columns = [ref[:, lanes] for ref in ((low, other_low) if index < 2 else (high, other_high))]
        columns = jnp.concatenate(columns, axis=1)
        term = lax.dot_general(rows, columns, (((0,), (1,)), ((), ())), preferred_element_type=f32)
        total[...] = term if index == 0 else total[...] + term
    core = place_ref[1]
    for chip in range(2):
        rows = slice(chip * LANES, (chip + 1) * LANES)
        sent_ref[rows, :] = total[pl.ds((2 * chip + 1 - core) * LANES, LANES), :].astype(bf16)
        kept_ref[rows, :] = total[pl.ds((2 * chip + core) * LANES, LANES), :]
    for part in range(4):
        rows = slice(2 * LANES + part * GROUP, 2 * LANES + (part + 1) * GROUP)
        sent_ref[rows, :] = fgrad_ref[:, part * SPAN : (part + 1) * SPAN].astype(bf16)


def middle_kernel(place_ref, kept_ref, received_ref, fgrad_ref, sent_ref, rest_ref):
    chip, core = place_ref[2], place_ref[1]
    for target, index in ((sent_ref, 1 - chip), (rest_ref, chip)):
        rows = pl.ds(pl.multiple_of(index * LANES, LANES), LANES)
        target[0:LANES, :] = (kept_ref[rows, :] + received_ref[rows, :].astype(f32)).astype(bf16)
    own = fgrad_ref[...]
    for part in range(4):
        theirs = received_ref[2 * LANES :, :][part * GROUP : (part + 1) * GROUP, :].astype(f32)
        ours = own[:, part * SPAN : (part + 1) * SPAN]
        both = jnp.concatenate([jnp.where(core == 0, ours, theirs), jnp.where(core == 0, theirs, ours)], axis=0)
        for target in (sent_ref, rest_ref):
            target[LANES + part * HALF : LANES + (part + 1) * HALF, :] = both.astype(bf16)


def last_kernel(place_ref, rest_ref, received_ref, grad_ref, fgrad_ref):
    first = place_ref[2] == 0
    rest, received = rest_ref[...].astype(f32), received_ref[...].astype(f32)
    grad_ref[...] = (rest[0:LANES, :] + received[0:LANES, :]).astype(bf16)
    for part in range(4):
        rows = slice(LANES + part * HALF, LANES + (part + 1) * HALF)
        lanes = slice(part * SPAN, (part + 1) * SPAN)
        fgrad_ref[0:HALF, lanes] = jnp.where(first, rest[rows, :], received[rows, :])
        fgrad_ref[HALF:, lanes] = jnp.where(first, received[rows, :], rest[rows, :])


def conv_kernel(taps0, taps1, taps2, taps3, skip_ref, pair_ref, value_ref, dmix_ref, out_ref, mix_ref, mixes, values, copies, result):
    chan = pl.program_id(0)

    @pl.when(chan == 0)
    def _():
        _, key = load_pair(pair_ref)
        value = value_ref[...].astype(f32)
        for two in range(BLOCKS // 2):
            start = two * 2 * HALF
            pair = halves_of(value[start : start + GROUP, :], value[start + HALF : start + HALF + GROUP, :])
            for side in range(2):
                for piece, (seq, _) in enumerate(NEAR[side * SEQS : (side + 1) * SEQS]):
                    row = ((2 * two + side) * SEQS + seq) * GROUP
                    values[row : row + GROUP, :] = pair[side][:, piece * LANES : (piece + 1) * LANES]
        mix = (key * values[...]).astype(bf16)
        mix_ref[...] = mix
        mixes[0:LANES, :] = jnp.zeros((LANES, LANES), f32)
        mixes[LANES:, :] = mix.astype(f32)
        for part in range(SEQS):
            copies[part, 0:ROWS, :] = jnp.zeros((ROWS, LANES), bf16)

    for part in range(SEQS):
        copies[part, ROWS:, :] = mixes[
            pl.ds(LANES - part * SEQS * GROUP + chan, ROWS, stride=GROUP), :
        ].astype(bf16)
    behind = [
        copies[block % 4, ROWS - block // 4 * 16 : 2 * ROWS - block // 4 * 16, :] for block in range(BLOCKS)
    ]
    own = mixes[pl.ds(LANES + chan, ROWS, stride=GROUP), :]
    taps = jnp.concatenate([ref[0] for ref in (taps0, taps1, taps2, taps3)], axis=0)
    total = jnp.dot(jnp.concatenate(behind, axis=1), taps, preferred_element_type=f32)
    result[pl.ds(chan, ROWS, stride=GROUP), :] = total + skip_ref[chan] * own

    @pl.when(chan == GROUP - 1)
    def _():
        kgrad = dmix_ref[...].astype(f32) * values[...]
        both = [result[...].reshape(ROWS, 1, GROUP, LANES), kgrad.reshape(ROWS, 1, GROUP, LANES)]
        out_ref[...] = jnp.concatenate(both, axis=1).reshape(2 * SIGNAL, LANES).astype(bf16)


def fgrad_kernel(pair_ref, mix_ref, fgrad_ref, mixes, grads, copies, corr, sums):
    chan = pl.program_id(0)

    @pl.when(chan == 0)
    def _():
        clear_ahead(grads, copies, load_pair(pair_ref)[0])
        mixes[...] = mix_ref[...].astype(f32)
        corr[:, TAPS:] = jnp.zeros((LANES, LANES), f32)

    fill_ahead(grads, copies, chan)
    own = mixes[pl.ds(chan, ROWS, stride=GROUP), :].T.astype(bf16)
    for block in range(0, BLOCKS, 2):
        two = jnp.concatenate([ahead_of(copies, block), ahead_of(copies, block + 1)], axis=1)
        corr[:, block * LANES : (block + 2) * LANES] = jnp.dot(own, two, preferred_element_type=f32)
    acc = corr[0:GROUP, :]
    for group in range(1, LANES // GROUP):
        acc = acc + pltpu.roll(corr[group * GROUP : (group + 1) * GROUP, :], WIDE - group * GROUP, 1)
    for block in range(BLOCKS + 1):
        sums[block, pl.ds(pl.multiple_of(chan * GROUP, GROUP), GROUP), :] = acc[:, block * LANES : (block + 1) * LANES]

    @pl.when(chan == GROUP - 1)
    def _():
        fgrad = None
        for row in range(GROUP):
            part = jnp.concatenate(
                [sums[block, pl.ds(row, GROUP, stride=GROUP), :] for block in range(BLOCKS + 1)], axis=1
            )
            fgrad = part if row == 0 else fgrad + pltpu.roll(part, WIDE - row, 1)
        fgrad_ref[...] = fgrad[:, :TAPS]


def whole(shape):
    return pl.BlockSpec(shape, lambda chan: (0,) * len(shape))


params = pltpu.CompilerParams(vmem_limit_bytes=24 * 1024 * 1024)
smem = pl.BlockSpec(memory_space=pltpu.SMEM)
taps_spec = pl.BlockSpec((1, TAPS, LANES), lambda chan: (chan, 0, 0))
CUTS = 4
CUT = TAPS // CUTS
taps_specs = [pl.BlockSpec((1, CUT, LANES), lambda chan, cut=cut: (chan, cut, 0)) for cut in range(CUTS)]
pair_spec = pl.BlockSpec((ROWS, 1, HALF, LANES), lambda chan: (0, 2, 0, 0))


def pack(quarter, weight, query, upstream, key):
    steps = 4
    block = pl.BlockSpec((SIGNAL // steps, LANES), lambda step: (step, 0))
    return pl.pallas_call(
        pack_kernel,
        grid=(steps,),
        in_specs=[smem, pl.BlockSpec(weight.shape, lambda step: (0, 0)), block, block, block],
        out_specs=pl.BlockSpec((ROWS * 48 // steps, LANES), lambda step: (step, 0)),
        out_shape=jax.ShapeDtypeStruct((ROWS * 48, LANES), bf16),
        scratch_shapes=[pltpu.VMEM((2 * GROUP * HALF, LANES), bf16)],
        compiler_params=params,
        name="pack",
    )(quarter, *[pltpu.with_memory_space_constraint(x, pltpu.HBM) for x in (weight, query, upstream, key)])


def build_taps(filters):
    return pl.pallas_call(
        taps_kernel,
        grid=(GROUP,),
        in_specs=[whole((GROUP, TAPS))],
        out_specs=taps_spec,
        out_shape=jax.ShapeDtypeStruct((GROUP, TAPS, LANES), bf16),
        scratch_shapes=[pltpu.VMEM((BLOCKS + 1, GROUP * GROUP, LANES), f32)],
        compiler_params=params,
        name="build_taps",
    )(filters)


def early_dmix(taps, skip, pair):
    return pl.pallas_call(
        dmix_kernel,
        grid=(GROUP,),
        in_specs=taps_specs + [smem, pair_spec],
        out_specs=[whole((SIGNAL, LANES)), whole((BLOCKS * GROUP, SEQS * LANES))],
        out_shape=[
            jax.ShapeDtypeStruct((SIGNAL, LANES), bf16),
            jax.ShapeDtypeStruct((BLOCKS * GROUP, SEQS * LANES), bf16),
        ],
        scratch_shapes=[
            pltpu.VMEM((SIGNAL + LANES, LANES), f32),
            pltpu.VMEM((SEQS, 2 * ROWS, LANES), bf16),
            pltpu.VMEM((SIGNAL, LANES), f32),
        ],
        compiler_params=params,
        name="early_dmix",
    )(taps, taps, taps, taps, skip, pair)


def project(column, packed, tokens):
    slots = packed.reshape(2 * BLOCKS, 2, 3, HALF, LANES)

    def slot(step, column_ref):
        part = (column_ref[0] + step) % 4
        return (0, part // 2, part % 2, 0, 0)

    out_spec = pl.BlockSpec((LANES, tokens.shape[0]), lambda step, column_ref: (0, 0))
    return pl.pallas_call(
        project_kernel,
        grid_spec=pltpu.PrefetchScalarGridSpec(
            num_scalar_prefetch=1,
            grid=(4,),
            in_specs=[
                pl.BlockSpec((2 * BLOCKS, 1, 1, HALF, LANES), slot),
                pl.BlockSpec(tokens.shape, lambda step, column_ref: (0, 0)),
            ],
            out_specs=[out_spec] * 4 + [pl.BlockSpec((SPAN, 2 * LANES), lambda step, column_ref: (0, 0))] * 2,
        ),
        out_shape=[jax.ShapeDtypeStruct((LANES, tokens.shape[0]), bf16)] * 4
        + [jax.ShapeDtypeStruct((SPAN, 2 * LANES), bf16)] * 2,
        compiler_params=params,
        name="project",
    )(column, slots, tokens)


def join(parts, dvalue):
    return pl.pallas_call(
        join_kernel,
        out_shape=jax.ShapeDtypeStruct((BLOCKS * HALF, SEQS * LANES), bf16),
        compiler_params=params,
        name="join",
    )(*parts, dvalue)


def vmem_specs(count):
    return [smem] + [pl.BlockSpec(memory_space=pltpu.VMEM)] * count


def back(place, dvalue, weights, fgrad):
    return pl.pallas_call(
        back_kernel,
        in_specs=vmem_specs(6),
        out_shape=[
            jax.ShapeDtypeStruct((2 * LANES + 4 * GROUP, SPAN), bf16),
            jax.ShapeDtypeStruct((2 * LANES, SPAN), f32),
        ],
        scratch_shapes=[pltpu.VMEM((SEQS * LANES, SPAN), f32)],
        compiler_params=params,
        name="back",
    )(place, dvalue, *weights, fgrad)


def middle(place, kept, received, fgrad):
    return pl.pallas_call(
        middle_kernel,
        in_specs=vmem_specs(3),
        out_shape=[jax.ShapeDtypeStruct((LANES + 4 * HALF, SPAN), bf16)] * 2,
        compiler_params=params,
        name="middle",
    )(place, kept, received, fgrad)


def last(place, rest, received):
    return pl.pallas_call(
        last_kernel,
        in_specs=vmem_specs(2),
        out_shape=[jax.ShapeDtypeStruct((LANES, SPAN), bf16), jax.ShapeDtypeStruct((2 * HALF, TAPS), f32)],
        compiler_params=params,
        name="last",
    )(place, rest, received)


def late_conv(taps, skip, pair, value, dmix):
    return pl.pallas_call(
        conv_kernel,
        grid=(GROUP,),
        in_specs=taps_specs
        + [
            smem,
            pair_spec,
            whole((BLOCKS * HALF, SEQS * LANES)),
            whole((SIGNAL, LANES)),
        ],
        out_specs=[whole((2 * SIGNAL, LANES)), whole((SIGNAL, LANES))],
        out_shape=[
            jax.ShapeDtypeStruct((2 * SIGNAL, LANES), bf16),
            jax.ShapeDtypeStruct((SIGNAL, LANES), bf16),
        ],
        scratch_shapes=[
            pltpu.VMEM((SIGNAL + LANES, LANES), f32),
            pltpu.VMEM((SIGNAL, LANES), f32),
            pltpu.VMEM((SEQS, 2 * ROWS, LANES), bf16),
            pltpu.VMEM((SIGNAL, LANES), f32),
        ],
        compiler_params=params,
        name="late_conv",
    )(taps, taps, taps, taps, skip, pair, value, dmix)


def late_fgrad(pair, mix):
    return pl.pallas_call(
        fgrad_kernel,
        grid=(GROUP,),
        in_specs=[pair_spec, whole((SIGNAL, LANES))],
        out_specs=whole((GROUP, TAPS)),
        out_shape=jax.ShapeDtypeStruct((GROUP, TAPS), f32),
        scratch_shapes=[
            pltpu.VMEM((SIGNAL, LANES), f32),
            pltpu.VMEM((SIGNAL + LANES, LANES), f32),
            pltpu.VMEM((SEQS, 2 * ROWS, LANES), bf16),
            pltpu.VMEM((LANES, WIDE), f32),
            pltpu.VMEM((BLOCKS + 1, GROUP * GROUP, LANES), f32),
        ],
        compiler_params=params,
        name="late_fgrad",
    )(pair, mix)


def swap(values, axes, groups=None):
    return lax.all_to_all(values, axes, split_axis=0, concat_axis=0, tiled=True, axis_index_groups=groups)


def per_device(inputs, value_weight, query, key, filters, skip, cotangent):
    quarter = lax.axis_index("dp")
    side = lax.axis_index("context") % 2

    near = [[seq * BLOCKS + 2 * k + place for seq, place in NEAR] for k in range(BLOCKS // 2)]
    tokens = lax.all_gather(inputs[0], ("dp", "context"), axis=0, tiled=True, axis_index_groups=near)
    own_filters = lax.dynamic_slice_in_dim(filters, quarter * GROUP, GROUP, 0)
    own_skip = lax.dynamic_slice_in_dim(skip, quarter * GROUP, GROUP, 0)
    taps = build_taps(own_filters)

    packed = pack(quarter.astype(jnp.int32)[None], value_weight, query[0], cotangent[0], key[0])
    packed = swap(packed.reshape(ROWS, 3 * HALF, LANES), ("context", "dp"))
    packed, taps = lax.optimization_barrier((packed, taps))
    pair = packed.reshape(ROWS, 3, HALF, LANES)

    column = lax.axis_index("tensor").astype(jnp.int32)[None]
    *parts, low, high = project(column, packed, tokens)
    parts = [parts[0]] + [
        lax.ppermute(parts[step], "tensor", [(i, (i + step) % 4) for i in range(4)]) for step in (1, 2, 3)
    ]
    twins = [(k, k ^ 1) for k in range(BLOCKS)]
    other_low = lax.ppermute(low, "context", twins)
    dmix, dvalue = early_dmix(taps, own_skip, pair)
    dvalue, other_low = lax.optimization_barrier((dvalue, other_low))

    both, high = lax.optimization_barrier((join(parts, dvalue), high))
    other_high = lax.ppermute(high, "context", twins)
    both = swap(both.reshape(BLOCKS, HALF, SEQS * LANES), "context")
    dvalue = lax.all_gather(both[:, GROUP:].reshape(BLOCKS * GROUP, SEQS * LANES), "tensor", axis=0, tiled=True)
    out, mix = late_conv(taps, own_skip, pair, both.reshape(BLOCKS * HALF, SEQS * LANES), dmix)
    out = swap(out.reshape(ROWS, 2, GROUP, LANES), ("context", "dp"))
    fgrad = late_fgrad(pair, mix)
    dvalue, fgrad = lax.optimization_barrier((dvalue, fgrad))

    place = jnp.stack([side, quarter % 2, quarter // 2]).astype(jnp.int32)
    sent, kept = back(place, dvalue, (low, high, other_low, other_high), fgrad)
    received = lax.ppermute(sent, "dp", [(i, i ^ 1) for i in range(SEQS)])
    sent, rest = middle(place, kept, received, fgrad)
    received = lax.ppermute(sent, "dp", [(i, i ^ 2) for i in range(SEQS)])
    input_grad, filter_grad = last(place, rest, received)
    skip_grad = filter_grad[:, 0]

    query_part = query[0].astype(f32)
    upstream = cotangent[0].astype(f32)
    conv = out[:, 0].reshape(SIGNAL, LANES).astype(f32)
    key_grad = out[:, 1].reshape(SIGNAL, LANES)
    gated = (query_part * conv).astype(bf16)
    query_grad = (upstream * conv).astype(bf16)
    return (gated[None], query_grad[None], key_grad[None], input_grad[None], filter_grad, skip_grad)


def solution(mesh):
    by_channel = P("dp", "tensor", "context")
    by_row = P(("tensor", "context"), None)
    in_specs = (
        P("dp", "context", "tensor"),
        by_row,
        by_channel,
        by_channel,
        by_row,
        P(("tensor", "context")),
        by_channel,
    )
    out_specs = (
        by_channel,
        by_channel,
        by_channel,
        P("dp", "context", "tensor"),
        by_row,
        P(("tensor", "context")),
    )
    return jax.shard_map(
        per_device, mesh=mesh, in_specs=in_specs, out_specs=out_specs, check_vma=False
    )
```

time: 252 us -> 204 us (0.81)
  waiting for transfers between devices: 95.8 us -> 49.8 us
  local copies, waits for them, and re-layouts: 3.78 us -> 21.3 us
  starting transfers between devices: 60.4 us -> 47 us
  Pallas kernels: 24.1 us -> 32.7 us
  matrix products: 8.27 us -> 0 us
  other arithmetic: 5.58 us -> 2.01 us
  blocking collectives: 37.7 us -> 35 us
    all_to_all x7 -> x2, waiting for transfers between devices: 94.5 us -> 39.2 us  [swap(): lax.all_to_all(values, axes, split_axis=0, concat_axis=0, tiled=True, axi...]
    all_to_all x7 -> x2, starting transfers between devices: 60.4 us -> 27 us  [swap(): lax.all_to_all(values, axes, split_axis=0, concat_axis=0, tiled=True, axi...]
    ppermute x0 -> x7, starting transfers between devices: none -> 20 us  [the longest x3 10.6 us: per_device(): lax.ppermute(parts[step], 'tensor', [(i, (i + step) % 4) for i in range(4)])]
    unnamed x16 -> x30, local copies, waits for them, and re-layouts: 0.04 us -> 17.5 us
    all_gather x1 -> x0, blocking collectives: 16.6 us -> none  [per_device(): filter_grad = lax.all_gather(fgrad, 'dp', axis=0, tiled=True).astype(f32)]
    all_to_all x1, blocking collectives: 21.1 us -> 35 us  [swap(): lax.all_to_all(values, axes, split_axis=0, concat_axis=0, tiled=True, axi...]
    pallas_call x2 -> x10, Pallas kernels: 24.1 us -> 32.7 us  [the longest x1 7.43 us: late_fgrad(): pl.pallas_call(fgrad_kernel, grid=(GROUP,), in_specs=[pair_spec, whole((S...]
    dot_general x10 -> x0, matrix products: 8.27 us -> none  [the longest x1 3.52 us: per_device(): lax.dot_general(dvalue, weight, (((0,), (1,)), ((), ())), preferred_eleme...]
  transfers between devices with their start and end apart: 9 -> 11, of which waited for: 6 -> 5; matrix products, arithmetic and copies ran while one was open for 4% -> 2% of each run, Pallas kernels for 10% -> 13%
where the time goes in v2:
time: 204 us; the launch traced here: 202 us
  waiting for transfers between devices  49.8 us (24%)
  starting transfers between devices  47 us (23%)
  blocking collectives  35 us (17%)
  Pallas kernels  32.7 us (16%)
  local copies, waits for them, and re-layouts  21.3 us (10%)
  between operations  14.4 us (7%)
    all_to_all x2, waiting for transfers between devices, swap(): lax.all_to_all(values, axes, split_axis=0, concat_axis=0, tiled=True, axi...  39.2 us
    all_to_all x1, blocking collectives, swap(): lax.all_to_all(values, axes, split_axis=0, concat_axis=0, tiled=True, axi...  35 us
    all_to_all x2, starting transfers between devices, swap(): lax.all_to_all(values, axes, split_axis=0, concat_axis=0, tiled=True, axi...  27 us
    unnamed x30, local copies, waits for them, and re-layouts  17.5 us
    ppermute x3, starting transfers between devices, per_device(): lax.ppermute(parts[step], 'tensor', [(i, (i + step) % 4) for i in range(4)])  10.6 us
    pallas_call x1, Pallas kernels, late_fgrad(): pl.pallas_call(fgrad_kernel, grid=(GROUP,), in_specs=[pair_spec, whole((S...  7.43 us
    ppermute x1, waiting for transfers between devices, per_device(): received = lax.ppermute(sent, 'dp', [(i, i ^ 2) for i in range(SEQS)])  5.89 us
    pallas_call x1, Pallas kernels, late_conv(): pl.pallas_call(conv_kernel, grid=(GROUP,), in_specs=taps_specs + [smem, p...  5.39 us
  transfers between devices with their start and end apart: 11, of which 5 were waited for; matrix products, arithmetic and copies ran while one was open for 2% of the time, Pallas kernels for 13%

profile of v2, /device:TPU:1, one launch (start us, length us, event | category | flops | bytes accessed | tf_op | source)
XLA Modules:
  0.0 202.2 jit_solution(1854687046032446265)
XLA Ops:
  7.2 0.0 copy-start
  7.2 0.0 all-gather.6.cloned.1.call-start
  7.2 0.7 all-gather.6.cloned.1.call-update
  7.9 3.2 %pack.1 = bf16[6144,128]{1,0:T(8,128)(2,1)S(1)} custom-call(s32[1]{0:T(128)} %bitcast.quarter_ref, bf16[32,4096]{1,0:T(8,128)(2,1)} %weight_ref.1, bf16[1024,128]{1,0:T(8,128)(2,1)} %bitcast.36, bf16[1024,128]{1,0:T(8,128)(2,1)} %bitcast.35, bf16[1024,128]{1,0:T(8,128)(2,1)} %bitcast.37), custom_call_target="tpu_custom_call" | custom-call | tf_op jit(solution)/shard_map/pack/pallas_call | solution.py:306
  11.2 0.0 copy-start.4
  11.2 1.1 copy-done.4
  12.3 18.4 %all-to-all-start = ((bf16[128,48,128]{2,1,0:T(8,128)(2,1)}), bf16[128,48,128]{2,1,0:T(8,128)(2,1)S(1)}, u32[]{:S(2)}, u32[]{:S(2)}) async-start(bf16[128,48,128]{2,1,0:T(8,128)(2,1)} %bitcast.31), calls=%async_computation | async-start | bytes 3145728 | tf_op jit(solution)/shard_map/all_to_all | solution.py:471
  30.7 0.0 all-gather.4.cloned.1.call-start
  30.8 0.0 copy-done
  30.8 3.5 %build_taps.1.taps0.taps1.taps2.taps3 = bf16[8,4096,128]{2,1,0:T(8,128)(2,1)S(1)} custom-call(f32[8,4096]{1,0:T(8,128)S(1)} %constant_dynamic-slice_fusion.filters_ref), custom_call_target="tpu_custom_call" | custom-call | tf_op jit(solution)/shard_map/build_taps/pallas_call | solution.py:319
  34.3 0.0 copy-start.1
  34.3 3.3 %copy-done.1 = bf16[8,4096,128]{2,1,0:T(8,128)(2,1)} copy-done((bf16[8,4096,128]{2,1,0:T(8,128)(2,1)}, bf16[8,4096,128]{2,1,0:T(8,128)(2,1)S(1)}, u32[]{:S(2)}) %copy-start.1) | copy-done | bytes 8388632
  37.6 0.0 copy-start.14
  37.6 39.2 %all-to-all-done = bf16[128,48,128]{2,1,0:T(8,128)(2,1)S(1)} async-done(((bf16[128,48,128]{2,1,0:T(8,128)(2,1)}), bf16[128,48,128]{2,1,0:T(8,128)(2,1)S(1)}, u32[]{:S(2)}, u32[]{:S(2)}) %all-to-all-start) | async-done | bytes 1572896 | tf_op jit(solution)/shard_map/all_to_all | solution.py:471
  76.8 2.0 all-gather.6.cloned.1.call-done
  78.8 1.6 copy-done.5
  80.4 4.0 %project.1 = (bf16[128,1024]{1,0:T(8,128)(2,1)S(1)}, bf16[128,1024]{1,0:T(8,128)(2,1)S(1)}, bf16[128,1024]{1,0:T(8,128)(2,1)S(1)}, bf16[128,1024]{1,0:T(8,128)(2...) custom-call(s32[1]{0:T(128)} %bitcast.6.column_ref, bf16[64,2,3,16,128]{4,3,2,1,0:T(8,128)(2,1)S(1)} %bitcast.27, ...), custom_call_target="tpu_custom_call" | custom-call | tf_op jit(solution)/shard_map/project/pallas_call | solution.py:359
  84.4 0.0 copy-start.7
  84.4 0.8 copy-done.7
  85.2 1.9 collective-permute-start.3
  87.1 3.1 %collective-permute-start = (bf16[128,1024]{1,0:T(8,128)(2,1)S(1)}, bf16[128,1024]{1,0:T(8,128)(2,1)S(1)}, u32[]{:S(2)}, u32[]{:S(2)}) collective-permute-start(bf16[128,1024]{1,0:T(8,128)(2,1)S(1)} %get-tuple-element.33), channel_id=1, source_target_pairs={{0,32},{32,64},{64,96},{96,0},{1,33},{33,65},{65,97},{97,1},{2,34}... | collective-permute-start | bytes 786440 | tf_op jit(solution)/shard_map/ppermute | solution.py:492
  90.2 4.3 %collective-permute-start.1 = (bf16[128,1024]{1,0:T(8,128)(2,1)S(1)}, bf16[128,1024]{1,0:T(8,128)(2,1)S(1)}, u32[]{:S(2)}, u32[]{:S(2)}) collective-permute-start(bf16[128,1024]{1,0:T(8,128)(2,1)S(1)} %get-tuple-element.34), channel_id=1, source_target_pairs={{0,64},{32,96},{64,0},{96,32},{1,65},{33,97},{65,1},{97,33},{2,66}... | collective-permute-start | bytes 786440 | tf_op jit(solution)/shard_map/ppermute | solution.py:492
  94.6 3.1 %collective-permute-start.2 = (bf16[128,1024]{1,0:T(8,128)(2,1)S(1)}, bf16[128,1024]{1,0:T(8,128)(2,1)S(1)}, u32[]{:S(2)}, u32[]{:S(2)}) collective-permute-start(bf16[128,1024]{1,0:T(8,128)(2,1)S(1)} %get-tuple-element.35), channel_id=1, source_target_pairs={{0,96},{32,0},{64,32},{96,64},{1,97},{33,1},{65,33},{97,65},{2,98}... | collective-permute-start | bytes 786440 | tf_op jit(solution)/shard_map/ppermute | solution.py:492
  97.7 0.0 copy-done.14
  97.7 0.1 dynamic_slice.7.skip_ref
  97.8 3.4 %copy-done.2 = bf16[8,4096,128]{2,1,0:T(8,128)(2,1)S(1)} copy-done((bf16[8,4096,128]{2,1,0:T(8,128)(2,1)S(1)}, bf16[8,4096,128]{2,1,0:T(8,128)(2,1)}, u32[]{:S(2)}) %copy-start.2) | copy-done | bytes 8388632
  101.1 4.5 %early_dmix.1 = (bf16[1024,128]{1,0:T(8,128)(2,1)S(1)}, bf16[256,512]{1,0:T(8,128)(2,1)S(1)}) custom-call(bf16[8,4096,128]{2,1,0:T(8,128)(2,1)S(1)} %copy-done.2, bf16[8,4096,128]{2,1,0:T(8,128)(2,1)S(1)} %copy-done.2, bf16[8,4096,128]{2,1,0:T(8,128)(2,1)S(1)} %copy-done.2, bf16[8,4096,128]{2,1,0:T(8,128)(2,1)S(1)} %copy-done.2, ...), custom_call_target="tpu_custom_call" | custom-call | tf_op jit(solution)/shard_map/early_dmix/pallas_call | solution.py:332
  105.6 0.0 collective-permute-done.3.other_low
  105.7 0.0 copy-start.9
  105.7 0.0 collective-permute-done.part1
  105.7 0.0 collective-permute-done.1.part2
  105.7 0.3 collective-permute-done.2.part3
  106.0 0.2 join.1
  106.2 35.0 %all_to_all.15 = bf16[32,16,512]{2,1,0:T(8,128)(2,1)S(1)} all-to-all(bf16[32,16,512]{2,1,0:T(8,128)(2,1)S(1)} %bitcast.33), channel_id=1, replica_groups=mesh['dp'=4,'tensor'=4,'context'=32] {'context'}, dimensions={0} | all-to-all | bytes 1048576 | tf_op jit(solution)/shard_map/all_to_all | solution.py:471
  141.2 0.0 copy-done.9
  141.2 0.7 slice_bitcast_fusion
  141.9 0.0 all-gather.4.cloned.1.call-update
  141.9 1.9 collective-permute-start.4
  143.9 0.0 copy-start.3
  143.9 3.4 %copy-done.3 = bf16[8,4096,128]{2,1,0:T(8,128)(2,1)S(1)} copy-done((bf16[8,4096,128]{2,1,0:T(8,128)(2,1)S(1)}, bf16[8,4096,128]{2,1,0:T(8,128)(2,1)}, u32[]{:S(2)}) %copy-start.3) | copy-done | bytes 8388632
  147.2 5.4 %late_conv.1 = (bf16[2048,128]{1,0:T(8,128)(2,1)}, bf16[1024,128]{1,0:T(8,128)(2,1)S(1)}) custom-call(bf16[8,4096,128]{2,1,0:T(8,128)(2,1)S(1)} %copy-done.3, bf16[8,4096,128]{2,1,0:T(8,128)(2,1)S(1)} %copy-done.3, bf16[8,4096,128]{2,1,0:T(8,128)(2,1)S(1)} %copy-done.3, bf16[8,4096,128]{2,1,0:T(8,128)(2,1)S(1)} %copy-done.3, f32[8]{0:T(128)S(1)} %dynamic_slice.7.skip_ref, ...), custom_call_target="tpu_custom_call" | custom-call | tf_op jit(solution)/shard_map/late_conv/pallas_call | solution.py:425
  152.6 0.7 copy-done.11
  153.3 8.6 %all-to-all-start.2 = ((bf16[128,2,8,128]{3,2,1,0:T(8,128)(2,1)}), bf16[128,2,8,128]{3,2,1,0:T(8,128)(2,1)}, u32[]{:S(2)}, u32[]{:S(2)}) async-start(bf16[128,2,8,128]{3,2,1,0:T(8,128)(2,1)} %bitcast.11), calls=%async_computation.2 | async-start | bytes 1048576 | tf_op jit(solution)/shard_map/all_to_all | solution.py:471
  161.9 0.1 pad_add_fusion.place_ref
  162.0 0.9 copy-done.12
  163.0 7.4 %late_fgrad.1.fgrad_ref = f32[8,4096]{1,0:T(8,128)S(1)} custom-call(bf16[128,3,16,128]{3,2,1,0:T(8,128)(2,1)S(1)} %bitcast.30, bf16[1024,128]{1,0:T(8,128)(2,1)S(1)} %copy-done.12), custom_call_target="tpu_custom_call" | custom-call | tf_op jit(solution)/shard_map/late_fgrad/pallas_call | solution.py:452
  170.4 0.0 all-gather.4.cloned.1.call-done.dvalue_ref
  170.4 0.0 collective-permute-done.4.other_high
  170.4 0.0 copy-done.8
  170.4 0.0 copy-start.6
  170.4 1.2 copy-done.6
  171.7 1.0 copy-done.10
  172.7 2.5 %back.1 = (bf16[288,1024]{1,0:T(8,128)(2,1)S(1)}, f32[256,1024]{1,0:T(8,128)S(1)}) custom-call(s32[3]{0:T(128)S(1)} %pad_add_fusion.place_ref, bf16[1024,512]{1,0:T(8,128)(2,1)S(1)} %copy-done.6, bf16[1024,256]{1,0:T(8,128)(2,1)S(1)} %get-tuple-element.37.low, bf16[1024,256]{1,0:T(8,128)(2,1)S(1)} %copy-done.8, bf16[1024,256]{1,0:T(8,128)(2,1)S(1)} %copy-done.10, ...), custom_call_target="tpu_custom_call" | custom-call | tf_op jit(solution)/shard_map/back/pallas_call | solution.py:391
  175.2 2.9 %collective-permute-start.5 = (bf16[288,1024]{1,0:T(8,128)(2,1)S(1)}, bf16[288,1024]{1,0:T(8,128)(2,1)S(1)}, u32[]{:S(2)}, u32[]{:S(2)}) collective-permute-start(bf16[288,1024]{1,0:T(8,128)(2,1)S(1)} %get-tuple-element.49), channel_id=1, source_target_pairs={{0,128},{128,0},{256,384},{384,256},{1,129},{129,1},{257,385},{385... | collective-permute-start | bytes 1769480 | tf_op jit(solution)/shard_map/ppermute | solution.py:510
  178.1 1.6 collective-permute-done.5.received_ref
  179.7 0.7 middle.1
  180.3 2.7 %collective-permute-start.6 = (bf16[192,1024]{1,0:T(8,128)(2,1)S(1)}, bf16[192,1024]{1,0:T(8,128)(2,1)S(1)}, u32[]{:S(2)}, u32[]{:S(2)}) collective-permute-start(bf16[192,1024]{1,0:T(8,128)(2,1)S(1)} %get-tuple-element.51), channel_id=1, source_target_pairs={{0,256},{128,384},{256,0},{384,128},{1,257},{129,385},{257,1},{385... | collective-permute-start | bytes 1179656 | tf_op jit(solution)/shard_map/ppermute | solution.py:512
  183.0 0.0 all-to-all-done.2
  183.0 1.7 slice_bitcast_fusion.1
  184.7 0.0 copy-done.13
  184.7 1.9 fusion.1
  186.7 5.9 %collective-permute-done.6.received_ref = bf16[192,1024]{1,0:T(8,128)(2,1)S(1)} collective-permute-done((bf16[192,1024]{1,0:T(8,128)(2,1)S(1)}, bf16[192,1024]{1,0:T(8,128)(2,1)S(1)}, u32[]{:S(2)}, u32[]{:S(2)}) %collective-permute-start.6) | collective-permute-done | bytes 393248 | tf_op jit(solution)/shard_map/ppermute | solution.py:512
  192.5 1.5 last.1
  194.0 1.3 slice_reduce_fusion
  (8 shorter events, 0.0 us)
Async XLA Ops:
  7.2 23.6 %copy-start = (f32[32,4096]{1,0:T(8,128)S(1)}, f32[32,4096]{1,0:T(8,128)}, u32[]{:S(2)}) copy-start(f32[32,4096]{1,0:T(8,128)} %param.11) | copy-start | bytes 1572868
  7.2 71.6 %all-gather.6.cloned.1.call-start = ((), (), s32[]{:S(2)}) async-start(), calls=%async_computation.4 | async-start | bytes 2359296 | tf_op jit(solution)/shard_map/all_gather | solution.py:479
  11.2 1.1 copy-start.4
  12.3 64.5 %all-to-all-start = ((bf16[128,48,128]{2,1,0:T(8,128)(2,1)}), bf16[128,48,128]{2,1,0:T(8,128)(2,1)S(1)}, u32[]{:S(2)}, u32[]{:S(2)}) async-start(bf16[128,48,128]{2,1,0:T(8,128)(2,1)} %bitcast.31), calls=%async_computation | async-start | bytes 3145728 | tf_op jit(solution)/shard_map/all_to_all | solution.py:471
  30.7 139.7 %all-gather.4.cloned.1.call-start = ((), (), s32[]{:S(2)}) async-start(), calls=%async_computation.3 | async-start | bytes 1310720 | tf_op jit(solution)/shard_map/all_gather | solution.py:502
  34.3 3.3 %copy-start.1 = (bf16[8,4096,128]{2,1,0:T(8,128)(2,1)}, bf16[8,4096,128]{2,1,0:T(8,128)(2,1)S(1)}, u32[]{:S(2)}) copy-start(bf16[8,4096,128]{2,1,0:T(8,128)(2,1)S(1)} %build_taps.1.taps0.taps1.taps2.taps3) | copy-start | bytes 25165828
  37.6 60.1 %copy-start.14 = (f32[32]{0:T(128)S(1)}, f32[32]{0:T(128)}, u32[]{:S(2)}) copy-start(f32[32]{0:T(128)} %param.12) | copy-start | bytes 388
  78.8 1.6 copy-start.5
  84.4 0.8 copy-start.7
  85.2 20.5 %collective-permute-start.3 = (bf16[1024,256]{1,0:T(8,128)(2,1)S(1)}, bf16[1024,256]{1,0:T(8,128)(2,1)S(1)}, u32[]{:S(2)}, u32[]{:S(2)}) collective-permute-start(bf16[1024,256]{1,0:T(8,128)(2,1)S(1)} %get-tuple-element.37.low), channel_id=1, source_target_pairs={{0,1},{1,0},{2,3},{3,2},{4,5},{5,4},{6,7},{7,6},{8,9},{9,8},{10,11... | collective-permute-start | bytes 1572872 | tf_op jit(solution)/shard_map/ppermute | solution.py:495
  87.1 18.6 %collective-permute-start = (bf16[128,1024]{1,0:T(8,128)(2,1)S(1)}, bf16[128,1024]{1,0:T(8,128)(2,1)S(1)}, u32[]{:S(2)}, u32[]{:S(2)}) collective-permute-start(bf16[128,1024]{1,0:T(8,128)(2,1)S(1)} %get-tuple-element.33), channel_id=1, source_target_pairs={{0,32},{32,64},{64,96},{96,0},{1,33},{33,65},{65,97},{97,1},{2,34}... | collective-permute-start | bytes 786440 | tf_op jit(solution)/shard_map/ppermute | solution.py:492
  90.2 15.4 %collective-permute-start.1 = (bf16[128,1024]{1,0:T(8,128)(2,1)S(1)}, bf16[128,1024]{1,0:T(8,128)(2,1)S(1)}, u32[]{:S(2)}, u32[]{:S(2)}) collective-permute-start(bf16[128,1024]{1,0:T(8,128)(2,1)S(1)} %get-tuple-element.34), channel_id=1, source_target_pairs={{0,64},{32,96},{64,0},{96,32},{1,65},{33,97},{65,1},{97,33},{2,66}... | collective-permute-start | bytes 786440 | tf_op jit(solution)/shard_map/ppermute | solution.py:492
  94.6 11.5 %collective-permute-start.2 = (bf16[128,1024]{1,0:T(8,128)(2,1)S(1)}, bf16[128,1024]{1,0:T(8,128)(2,1)S(1)}, u32[]{:S(2)}, u32[]{:S(2)}) collective-permute-start(bf16[128,1024]{1,0:T(8,128)(2,1)S(1)} %get-tuple-element.35), channel_id=1, source_target_pairs={{0,96},{32,0},{64,32},{96,64},{1,97},{33,1},{65,33},{97,65},{2,98}... | collective-permute-start | bytes 786440 | tf_op jit(solution)/shard_map/ppermute | solution.py:492
  97.8 3.4 %copy-start.2 = (bf16[8,4096,128]{2,1,0:T(8,128)(2,1)S(1)}, bf16[8,4096,128]{2,1,0:T(8,128)(2,1)}, u32[]{:S(2)}) copy-start(bf16[8,4096,128]{2,1,0:T(8,128)(2,1)} %copy-done.1) | copy-start | bytes 25165828
  105.7 35.5 %copy-start.9 = (bf16[1024,256]{1,0:T(8,128)(2,1)}, bf16[1024,256]{1,0:T(8,128)(2,1)S(1)}, u32[]{:S(2)}) copy-start(bf16[1024,256]{1,0:T(8,128)(2,1)S(1)} %collective-permute-done.3.other_low) | copy-start | bytes 1572868
  141.9 28.5 %collective-permute-start.4 = (bf16[1024,256]{1,0:T(8,128)(2,1)}, bf16[1024,256]{1,0:T(8,128)(2,1)}, u32[]{:S(2)}, u32[]{:S(2)}) collective-permute-start(bf16[1024,256]{1,0:T(8,128)(2,1)} %copy-done.7), channel_id=1, source_target_pairs={{0,1},{1,0},{2,3},{3,2},{4,5},{5,4},{6,7},{7,6},{8,9},{9,8},{10,11... | collective-permute-start | bytes 1572872 | tf_op jit(solution)/shard_map/ppermute | solution.py:500
  143.9 3.4 %copy-start.3 = (bf16[8,4096,128]{2,1,0:T(8,128)(2,1)S(1)}, bf16[8,4096,128]{2,1,0:T(8,128)(2,1)}, u32[]{:S(2)}) copy-start(bf16[8,4096,128]{2,1,0:T(8,128)(2,1)} %copy-done.1) | copy-start | bytes 25165828
  152.6 0.7 copy-start.11
  153.3 17.1 %copy-start.8 = (bf16[1024,256]{1,0:T(8,128)(2,1)S(1)}, bf16[1024,256]{1,0:T(8,128)(2,1)}, u32[]{:S(2)}) copy-start(bf16[1024,256]{1,0:T(8,128)(2,1)} %copy-done.7) | copy-start | bytes 1572868
  153.3 29.7 %all-to-all-start.2 = ((bf16[128,2,8,128]{3,2,1,0:T(8,128)(2,1)}), bf16[128,2,8,128]{3,2,1,0:T(8,128)(2,1)}, u32[]{:S(2)}, u32[]{:S(2)}) async-start(bf16[128,2,8,128]{3,2,1,0:T(8,128)(2,1)} %bitcast.11), calls=%async_computation.2 | async-start | bytes 1048576 | tf_op jit(solution)/shard_map/all_to_all | solution.py:471
  162.0 1.0 copy-start.12
  163.0 21.8 %copy-start.13 = (bf16[1,1024,128]{2,1,0:T(8,128)(2,1)S(1)}, bf16[1,1024,128]{2,1,0:T(8,128)(2,1)}, u32[]{:S(2)}) copy-start(bf16[1,1024,128]{2,1,0:T(8,128)(2,1)} %param.13) | copy-start | bytes 786436
  170.4 1.2 copy-start.6
  171.7 1.0 copy-start.10
  175.2 4.5 %collective-permute-start.5 = (bf16[288,1024]{1,0:T(8,128)(2,1)S(1)}, bf16[288,1024]{1,0:T(8,128)(2,1)S(1)}, u32[]{:S(2)}, u32[]{:S(2)}) collective-permute-start(bf16[288,1024]{1,0:T(8,128)(2,1)S(1)} %get-tuple-element.49), channel_id=1, source_target_pairs={{0,128},{128,0},{256,384},{384,256},{1,129},{129,1},{257,385},{385... | collective-permute-start | bytes 1769480 | tf_op jit(solution)/shard_map/ppermute | solution.py:510
  180.3 12.2 %collective-permute-start.6 = (bf16[192,1024]{1,0:T(8,128)(2,1)S(1)}, bf16[192,1024]{1,0:T(8,128)(2,1)S(1)}, u32[]{:S(2)}, u32[]{:S(2)}) collective-permute-start(bf16[192,1024]{1,0:T(8,128)(2,1)S(1)} %get-tuple-element.51), channel_id=1, source_target_pairs={{0,256},{128,384},{256,0},{384,128},{1,257},{129,385},{257,1},{385... | collective-permute-start | bytes 1179656 | tf_op jit(solution)/shard_map/ppermute | solution.py:512
Sparse Core Ops, SparseCore 0:
  10.1 68.6 all-gather.5
  142.0 22.0 all-gather.3

commit v3 on v2

--- a/solution.py
+++ b/solution.py
@@ -21,33 +21,22 @@
 SPAN = 1024
 
 
-def pack_kernel(quarter_ref, weight_ref, query_ref, upstream_ref, key_ref, out_ref, picks):
-    step = pl.program_id(0)
-
-    @pl.when(step == 0)
-    def _():
-        quarter = quarter_ref[0]
-        source = lax.broadcasted_iota(jnp.int32, (SPAN, SPAN), 0)
-        target = lax.broadcasted_iota(jnp.int32, (SPAN, SPAN), 1)
-        wanted = (target % LANES // 4) * 32 + (target // LANES % SEQS) * GROUP + (target // LANES // SEQS) * 4 + target % 4
+def pack_kernel(quarter_ref, weight_ref, out_ref, picks):
+    @pl.when(pl.program_id(0) == 0)
+    def _():
+        source = lax.broadcasted_iota(jnp.int32, (SPAN, 2 * LANES), 0)
+        target = lax.broadcasted_iota(jnp.int32, (SPAN, 2 * LANES), 1)
+        wanted = (target % LANES // 4) * 32 + quarter_ref[0] * GROUP + (target // LANES) * 4 + target % 4
         chosen = (source == wanted).astype(f32).astype(bf16)
-        row = pl.multiple_of(quarter // 2 * HALF, HALF)
-        for slot in range(2):
-            lane = pl.multiple_of((quarter % 2 * 2 + slot) * SPAN, SPAN)
-            part = weight_ref[pl.ds(row, HALF), pl.ds(lane, SPAN)]
-            picked = jnp.dot(part, chosen, preferred_element_type=f32).astype(bf16)
-            for kind in range(GROUP):
-                start = (kind * 2 + slot) * HALF
-                picks[start : start + HALF, :] = picked[:, kind * LANES : (kind + 1) * LANES]
-
-    dconv = upstream_ref[...].astype(f32) * query_ref[...].astype(f32)
-    count = dconv.shape[0] // GROUP
-    both = [dconv.reshape(count, 1, GROUP, LANES), key_ref[...].astype(f32).reshape(count, 1, GROUP, LANES)]
-    both = jnp.concatenate(both, axis=1).reshape(count * HALF, LANES).astype(bf16)
-    for dest in range(count):
-        kind = dest % GROUP
-        out_ref[dest * 48 : dest * 48 + 32, :] = picks[kind * 32 : kind * 32 + 32, :]
-        out_ref[dest * 48 + 32 : dest * 48 + 48, :] = both[dest * HALF : (dest + 1) * HALF, :]
+        for part in range(4):
+            columns = weight_ref[:, part * SPAN : (part + 1) * SPAN]
+            picked = jnp.dot(columns, chosen, preferred_element_type=f32).astype(bf16)
+            for side in range(2):
+                picks[side, :, part * LANES : (part + 1) * LANES] = picked[:, side * LANES : (side + 1) * LANES]
+
+    count = picks.shape[1]
+    for dest in range(out_ref.shape[0] // count):
+        out_ref[dest * count : (dest + 1) * count, :] = picks[dest % 2]
 
 
 def load_pair(pair_ref):
@@ -95,19 +84,27 @@
         copies[part, ROWS:, :] = jnp.zeros((ROWS, LANES), bf16)
 
 
-def dmix_kernel(taps0, taps1, taps2, taps3, skip_ref, pair_ref, dmix_ref, dvalue_ref, grads, copies, result):
+def start_taps(taps_ref, taps, done):
+    for chan in range(GROUP):
+        pltpu.make_async_copy(taps_ref.at[chan], taps.at[chan], done.at[chan]).start()
+
+
+def wait_taps(taps_ref, taps, done, chan):
+    pltpu.make_async_copy(taps_ref.at[chan], taps.at[chan], done.at[chan]).wait()
+
+
+def dmix_kernel(taps_ref, skip_ref, pair_ref, dmix_ref, dvalue_ref, taps, done, grads, copies, result):
     chan = pl.program_id(0)
 
     @pl.when(chan == 0)
     def _():
+        start_taps(taps_ref, taps, done)
         clear_ahead(grads, copies, load_pair(pair_ref)[0])
 
     fill_ahead(grads, copies, chan)
     ahead = jnp.concatenate([ahead_of(copies, block) for block in range(BLOCKS)], axis=1)
-    refs = (taps0, taps1, taps2, taps3)
-    wide = jnp.concatenate(
-        [refs[block // 8][0, block % 8 * LANES : (block % 8 + 1) * LANES, :] for block in range(BLOCKS)], axis=1
-    )
+    wait_taps(taps_ref, taps, done, chan)
+    wide = jnp.concatenate([taps[chan, block * LANES : (block + 1) * LANES, :] for block in range(BLOCKS)], axis=1)
     total = lax.dot_general(ahead, wide, (((1,), (1,)), ((), ())), preferred_element_type=f32)
     own = grads[pl.ds(chan, ROWS, stride=GROUP), :]
     result[pl.ds(chan, ROWS, stride=GROUP), :] = total + skip_ref[chan] * own
@@ -124,8 +121,8 @@
             )
 
 
-def project_kernel(column_ref, packed_ref, tokens_ref, out0, out1, out2, out3, low_ref, high_ref):
-    part = packed_ref[...].reshape(SPAN, LANES)
+def project_kernel(column_ref, weight_ref, tokens_ref, out0, out1, out2, out3, low_ref, high_ref):
+    part = weight_ref[...]
     index = (column_ref[0] + pl.program_id(0)) % 4
     lanes = pl.ds(pl.multiple_of(index % 2 * LANES, LANES), LANES)
 
@@ -155,10 +152,13 @@
     value = part0[...].astype(f32) + part1[...].astype(f32) + part2[...].astype(f32) + part3[...].astype(f32)
     value = value.astype(bf16).astype(f32)
     dvalue = dvalue_ref[...].astype(f32)
-    lanes = SEQS * LANES
+    sides = []
+    for side in range(2):
+        order = [NEAR.index((seq, side)) for seq in range(SEQS)]
+        sides.append(jnp.concatenate([value[:, piece * LANES : (piece + 1) * LANES] for piece in order], axis=1))
     for two in range(BLOCKS // 2):
-        rows = value[two * GROUP : (two + 1) * GROUP, :]
-        for place, tile in enumerate(halves_of(rows[:, :lanes], rows[:, lanes:])):
+        rows = [part[two * GROUP : (two + 1) * GROUP, :] for part in sides]
+        for place, tile in enumerate(halves_of(*rows)):
             index = 2 * two + place
             tile = jnp.concatenate([tile, dvalue[index * GROUP : (index + 1) * GROUP, :]], axis=0)
             out_ref[index * HALF : (index + 1) * HALF, :] = tile.astype(bf16)
@@ -216,20 +216,21 @@
         fgrad_ref[HALF:, lanes] = jnp.where(first, received[rows, :], rest[rows, :])
 
 
-def conv_kernel(taps0, taps1, taps2, taps3, skip_ref, pair_ref, value_ref, dmix_ref, out_ref, mix_ref, mixes, values, copies, result):
+def conv_kernel(taps_ref, skip_ref, pair_ref, value_ref, dmix_ref, out_ref, mix_ref, taps, done, mixes, values, copies, result):
     chan = pl.program_id(0)
 
     @pl.when(chan == 0)
     def _():
+        start_taps(taps_ref, taps, done)
         _, key = load_pair(pair_ref)
         value = value_ref[...].astype(f32)
         for two in range(BLOCKS // 2):
             start = two * 2 * HALF
             pair = halves_of(value[start : start + GROUP, :], value[start + HALF : start + HALF + GROUP, :])
             for side in range(2):
-                for piece, (seq, _) in enumerate(NEAR[side * SEQS : (side + 1) * SEQS]):
+                for seq in range(SEQS):
                     row = ((2 * two + side) * SEQS + seq) * GROUP
-                    values[row : row + GROUP, :] = pair[side][:, piece * LANES : (piece + 1) * LANES]
+                    values[row : row + GROUP, :] = pair[side][:, seq * LANES : (seq + 1) * LANES]
         mix = (key * values[...]).astype(bf16)
         mix_ref[...] = mix
         mixes[0:LANES, :] = jnp.zeros((LANES, LANES), f32)
@@ -245,8 +246,8 @@
         copies[block % 4, ROWS - block // 4 * 16 : 2 * ROWS - block // 4 * 16, :] for block in range(BLOCKS)
     ]
     own = mixes[pl.ds(LANES + chan, ROWS, stride=GROUP), :]
-    taps = jnp.concatenate([ref[0] for ref in (taps0, taps1, taps2, taps3)], axis=0)
-    total = jnp.dot(jnp.concatenate(behind, axis=1), taps, preferred_element_type=f32)
+    wait_taps(taps_ref, taps, done, chan)
+    total = jnp.dot(jnp.concatenate(behind, axis=1), taps[chan], preferred_element_type=f32)
     result[pl.ds(chan, ROWS, stride=GROUP), :] = total + skip_ref[chan] * own
 
     @pl.when(chan == GROUP - 1)
@@ -294,25 +295,23 @@
 params = pltpu.CompilerParams(vmem_limit_bytes=24 * 1024 * 1024)
 smem = pl.BlockSpec(memory_space=pltpu.SMEM)
 taps_spec = pl.BlockSpec((1, TAPS, LANES), lambda chan: (chan, 0, 0))
-CUTS = 4
-CUT = TAPS // CUTS
-taps_specs = [pl.BlockSpec((1, CUT, LANES), lambda chan, cut=cut: (chan, cut, 0)) for cut in range(CUTS)]
-pair_spec = pl.BlockSpec((ROWS, 1, HALF, LANES), lambda chan: (0, 2, 0, 0))
-
-
-def pack(quarter, weight, query, upstream, key):
-    steps = 4
-    block = pl.BlockSpec((SIGNAL // steps, LANES), lambda step: (step, 0))
+any_spec = pl.BlockSpec(memory_space=pl.ANY)
+taps_scratch = [pltpu.VMEM((GROUP, TAPS, LANES), bf16), pltpu.SemaphoreType.DMA((GROUP,))]
+pair_spec = whole((2 * SIGNAL, LANES))
+
+
+def pack(quarter, weight):
+    steps, rows = 4, weight.shape[0]
     return pl.pallas_call(
         pack_kernel,
         grid=(steps,),
-        in_specs=[smem, pl.BlockSpec(weight.shape, lambda step: (0, 0)), block, block, block],
-        out_specs=pl.BlockSpec((ROWS * 48 // steps, LANES), lambda step: (step, 0)),
-        out_shape=jax.ShapeDtypeStruct((ROWS * 48, LANES), bf16),
-        scratch_shapes=[pltpu.VMEM((2 * GROUP * HALF, LANES), bf16)],
+        in_specs=[smem, pl.BlockSpec(weight.shape, lambda step: (0, 0))],
+        out_specs=pl.BlockSpec((rows * BLOCKS // steps, 4 * LANES), lambda step: (step, 0)),
+        out_shape=jax.ShapeDtypeStruct((rows * BLOCKS, 4 * LANES), bf16),
+        scratch_shapes=[pltpu.VMEM((2, rows, 4 * LANES), bf16)],
         compiler_params=params,
         name="pack",
-    )(quarter, *[pltpu.with_memory_space_constraint(x, pltpu.HBM) for x in (weight, query, upstream, key)])
+    )(quarter, pltpu.with_memory_space_constraint(weight, pltpu.HBM))
 
 
 def build_taps(filters):
@@ -332,46 +331,46 @@
     return pl.pallas_call(
         dmix_kernel,
         grid=(GROUP,),
-        in_specs=taps_specs + [smem, pair_spec],
+        in_specs=[any_spec, smem, pair_spec],
         out_specs=[whole((SIGNAL, LANES)), whole((BLOCKS * GROUP, SEQS * LANES))],
         out_shape=[
             jax.ShapeDtypeStruct((SIGNAL, LANES), bf16),
             jax.ShapeDtypeStruct((BLOCKS * GROUP, SEQS * LANES), bf16),
         ],
-        scratch_shapes=[
+        scratch_shapes=taps_scratch
+        + [
             pltpu.VMEM((SIGNAL + LANES, LANES), f32),
             pltpu.VMEM((SEQS, 2 * ROWS, LANES), bf16),
             pltpu.VMEM((SIGNAL, LANES), f32),
         ],
         compiler_params=params,
         name="early_dmix",
-    )(taps, taps, taps, taps, skip, pair)
-
-
-def project(column, packed, tokens):
-    slots = packed.reshape(2 * BLOCKS, 2, 3, HALF, LANES)
-
-    def slot(step, column_ref):
-        part = (column_ref[0] + step) % 4
-        return (0, part // 2, part % 2, 0, 0)
-
-    out_spec = pl.BlockSpec((LANES, tokens.shape[0]), lambda step, column_ref: (0, 0))
+    )(pltpu.with_memory_space_constraint(taps, pltpu.HBM), skip, pair)
+
+
+def project(column, weight, tokens):
+    count = tokens.shape[0]
+    out_spec = pl.BlockSpec((LANES, count), lambda step, column_ref: (0, 0))
     return pl.pallas_call(
         project_kernel,
         grid_spec=pltpu.PrefetchScalarGridSpec(
             num_scalar_prefetch=1,
             grid=(4,),
             in_specs=[
-                pl.BlockSpec((2 * BLOCKS, 1, 1, HALF, LANES), slot),
+                pl.BlockSpec((SPAN, LANES), lambda step, column_ref: (0, (column_ref[0] + step) % 4)),
                 pl.BlockSpec(tokens.shape, lambda step, column_ref: (0, 0)),
             ],
             out_specs=[out_spec] * 4 + [pl.BlockSpec((SPAN, 2 * LANES), lambda step, column_ref: (0, 0))] * 2,
         ),
-        out_shape=[jax.ShapeDtypeStruct((LANES, tokens.shape[0]), bf16)] * 4
+        out_shape=[jax.ShapeDtypeStruct((LANES, count), bf16)] * 4
         + [jax.ShapeDtypeStruct((SPAN, 2 * LANES), bf16)] * 2,
         compiler_params=params,
         name="project",
-    )(column, slots, tokens)
+    )(column, weight, tokens)
+
+
+def vmem_specs(count):
+    return [smem] + [pl.BlockSpec(memory_space=pltpu.VMEM)] * count
 
 
 def join(parts, dvalue):
@@ -381,10 +380,6 @@
         compiler_params=params,
         name="join",
     )(*parts, dvalue)
-
-
-def vmem_specs(count):
-    return [smem] + [pl.BlockSpec(memory_space=pltpu.VMEM)] * count
 
 
 def back(place, dvalue, weights, fgrad):
@@ -425,8 +420,8 @@
     return pl.pallas_call(
         conv_kernel,
         grid=(GROUP,),
-        in_specs=taps_specs
-        + [
+        in_specs=[
+            any_spec,
             smem,
             pair_spec,
             whole((BLOCKS * HALF, SEQS * LANES)),
@@ -437,7 +432,8 @@
             jax.ShapeDtypeStruct((2 * SIGNAL, LANES), bf16),
             jax.ShapeDtypeStruct((SIGNAL, LANES), bf16),
         ],
-        scratch_shapes=[
+        scratch_shapes=taps_scratch
+        + [
             pltpu.VMEM((SIGNAL + LANES, LANES), f32),
             pltpu.VMEM((SIGNAL, LANES), f32),
             pltpu.VMEM((SEQS, 2 * ROWS, LANES), bf16),
@@ -445,7 +441,7 @@
         ],
         compiler_params=params,
         name="late_conv",
-    )(taps, taps, taps, taps, skip, pair, value, dmix)
+    )(pltpu.with_memory_space_constraint(taps, pltpu.HBM), skip, pair, value, dmix)
 
 
 def late_fgrad(pair, mix):
@@ -475,19 +471,26 @@
     quarter = lax.axis_index("dp")
     side = lax.axis_index("context") % 2
 
+    place = jnp.stack([side, quarter % 2, quarter // 2]).astype(jnp.int32)
+
     near = [[seq * BLOCKS + 2 * k + place for seq, place in NEAR] for k in range(BLOCKS // 2)]
     tokens = lax.all_gather(inputs[0], ("dp", "context"), axis=0, tiled=True, axis_index_groups=near)
     own_filters = lax.dynamic_slice_in_dim(filters, quarter * GROUP, GROUP, 0)
     own_skip = lax.dynamic_slice_in_dim(skip, quarter * GROUP, GROUP, 0)
     taps = build_taps(own_filters)
 
-    packed = pack(quarter.astype(jnp.int32)[None], value_weight, query[0], cotangent[0], key[0])
-    packed = swap(packed.reshape(ROWS, 3 * HALF, LANES), ("context", "dp"))
-    packed, taps = lax.optimization_barrier((packed, taps))
-    pair = packed.reshape(ROWS, 3, HALF, LANES)
+    packed = pack(quarter.astype(jnp.int32)[None], value_weight)
+    weight = swap(packed.reshape(BLOCKS, value_weight.shape[0], 4 * LANES), "context").reshape(SPAN, 4 * LANES)
+
+    query_part = query[0].astype(f32)
+    upstream = cotangent[0].astype(f32)
+    dconv = (upstream * query_part).astype(bf16)
+    pair = jnp.concatenate([dconv.reshape(ROWS, 1, GROUP, LANES), key[0].reshape(ROWS, 1, GROUP, LANES)], axis=1)
+    pair, weight, taps = lax.optimization_barrier((pair, weight, taps))
+    pair = swap(pair, ("context", "dp")).reshape(2 * SIGNAL, LANES)
 
     column = lax.axis_index("tensor").astype(jnp.int32)[None]
-    *parts, low, high = project(column, packed, tokens)
+    *parts, low, high = project(column, weight, tokens)
     parts = [parts[0]] + [
         lax.ppermute(parts[step], "tensor", [(i, (i + step) % 4) for i in range(4)]) for step in (1, 2, 3)
     ]
@@ -505,7 +508,6 @@
     fgrad = late_fgrad(pair, mix)
     dvalue, fgrad = lax.optimization_barrier((dvalue, fgrad))
 
-    place = jnp.stack([side, quarter % 2, quarter // 2]).astype(jnp.int32)
     sent, kept = back(place, dvalue, (low, high, other_low, other_high), fgrad)
     received = lax.ppermute(sent, "dp", [(i, i ^ 1) for i in range(SEQS)])
     sent, rest = middle(place, kept, received, fgrad)
@@ -513,8 +515,6 @@
     input_grad, filter_grad = last(place, rest, received)
     skip_grad = filter_grad[:, 0]
 
-    query_part = query[0].astype(f32)
-    upstream = cotangent[0].astype(f32)
     conv = out[:, 0].reshape(SIGNAL, LANES).astype(f32)
     key_grad = out[:, 1].reshape(SIGNAL, LANES)
     gated = (query_part * conv).astype(bf16)

time: 204 us -> 191 us (0.936)
  waiting for transfers between devices: 49.8 us -> 33 us
  starting transfers between devices: 47 us -> 60.4 us
  local copies, waits for them, and re-layouts: 21.3 us -> 10.9 us
  blocking collectives: 35 us -> 29.3 us
  Pallas kernels: 32.7 us -> 37.2 us
    all_to_all x2 -> x3, waiting for transfers between devices: 39.2 us -> 23.7 us  [swap(): lax.all_to_all(values, axes, split_axis=0, concat_axis=0, tiled=True, axi...]
    all_to_all x2 -> x3, starting transfers between devices: 27 us -> 37.5 us  [swap(): lax.all_to_all(values, axes, split_axis=0, concat_axis=0, tiled=True, axi...]
    unnamed x30 -> x20, local copies, waits for them, and re-layouts: 17.5 us -> 7.05 us
    all_to_all x1, blocking collectives: 35 us -> 29.3 us  [swap(): lax.all_to_all(values, axes, split_axis=0, concat_axis=0, tiled=True, axi...]
    pallas_call x2, Pallas kernels: 9.89 us -> 12.7 us  [the longest x1 6.77 us: late_conv(): pl.pallas_call(conv_kernel, grid=(GROUP,), in_specs=[any_spec, smem, pair...]
  transfers between devices with their start and end apart: 11 -> 12, of which waited for: 5 -> 7; matrix products, arithmetic and copies ran while one was open for 2% -> 3% of each run, Pallas kernels for 13% -> 18%
where the time goes in v3:
time: 191 us; the launch traced here: 188 us
  starting transfers between devices  60.4 us (32%)
  Pallas kernels  37.2 us (19%)
  waiting for transfers between devices  33 us (17%)
  blocking collectives  29.3 us (15%)
  between operations  14.4 us (8%)
  local copies, waits for them, and re-layouts  10.9 us (6%)
  other arithmetic  3.05 us (2%)
    all_to_all x3, starting transfers between devices, swap(): lax.all_to_all(values, axes, split_axis=0, concat_axis=0, tiled=True, axi...  37.5 us
    all_to_all x1, blocking collectives, swap(): lax.all_to_all(values, axes, split_axis=0, concat_axis=0, tiled=True, axi...  29.3 us
    all_to_all x3, waiting for transfers between devices, swap(): lax.all_to_all(values, axes, split_axis=0, concat_axis=0, tiled=True, axi...  23.7 us
    ppermute x3, starting transfers between devices, per_device(): lax.ppermute(parts[step], 'tensor', [(i, (i + step) % 4) for i in range(4)])  10.6 us
    pallas_call x1, Pallas kernels, late_fgrad(): pl.pallas_call(fgrad_kernel, grid=(GROUP,), in_specs=[pair_spec, whole((S...  7.37 us
    unnamed x20, local copies, waits for them, and re-layouts  7.05 us
    pallas_call x1, Pallas kernels, late_conv(): pl.pallas_call(conv_kernel, grid=(GROUP,), in_specs=[any_spec, smem, pair...  6.77 us
    pallas_call x1, Pallas kernels, early_dmix(): pl.pallas_call(dmix_kernel, grid=(GROUP,), in_specs=[any_spec, smem, pair...  5.92 us
  transfers between devices with their start and end apart: 12, of which 7 were waited for; matrix products, arithmetic and copies ran while one was open for 3% of the time, Pallas kernels for 18%

profile of v3, /device:TPU:1, one launch (start us, length us, event | category | flops | bytes accessed | tf_op | source)
XLA Modules:
  0.0 188.2 jit_solution(17690990079349797453)
XLA Ops:
  7.2 0.0 copy-start
  7.2 0.0 copy-start.6
  7.2 0.0 copy-start.7
  7.2 0.0 copy-start.8
  7.2 0.0 all-gather.6.cloned.1.call-start
  7.3 0.7 all-gather.6.cloned.1.call-update
  8.0 3.0 %pack.1 = bf16[1024,512]{1,0:T(8,128)(2,1)} custom-call(s32[1]{0:T(128)} %bitcast.4.quarter_ref, bf16[32,4096]{1,0:T(8,128)(2,1)} %weight_ref.1), custom_call_target="tpu_custom_call" | custom-call | tf_op jit(solution)/shard_map/pack/pallas_call | solution.py:305
  11.0 16.6 %all-to-all-start = ((bf16[32,32,512]{2,1,0:T(8,128)(2,1)}), bf16[32,32,512]{2,1,0:T(8,128)(2,1)S(1)}, u32[]{:S(2)}, u32[]{:S(2)}) async-start(bf16[32,32,512]{2,1,0:T(8,128)(2,1)} %bitcast.5), calls=%async_computation | async-start | bytes 2097152 | tf_op jit(solution)/shard_map/all_to_all | solution.py:467
  27.6 0.0 copy-done
  27.6 3.5 %build_taps.1.taps_ref = bf16[8,4096,128]{2,1,0:T(8,128)(2,1)S(1)} custom-call(f32[8,4096]{1,0:T(8,128)S(1)} %constant_dynamic-slice_fusion.filters_ref), custom_call_target="tpu_custom_call" | custom-call | tf_op jit(solution)/shard_map/build_taps/pallas_call | solution.py:318
  31.1 0.0 copy-start.1
  31.1 3.3 %copy-done.1 = bf16[8,4096,128]{2,1,0:T(8,128)(2,1)} copy-done((bf16[8,4096,128]{2,1,0:T(8,128)(2,1)}, bf16[8,4096,128]{2,1,0:T(8,128)(2,1)S(1)}, u32[]{:S(2)}) %copy-start.1) | copy-done | bytes 8388632
  34.4 0.0 copy-done.6
  34.4 0.0 copy-done.7
  34.4 0.1 fusion.3
  34.5 0.0 copy-done.8
  34.5 0.9 pad_maximum_fusion
  35.4 23.1 %all-to-all-done = bf16[32,32,512]{2,1,0:T(8,128)(2,1)S(1)} async-done(((bf16[32,32,512]{2,1,0:T(8,128)(2,1)}), bf16[32,32,512]{2,1,0:T(8,128)(2,1)S(1)}, u32[]{:S(2)}, u32[]{:S(2)}) %all-to-all-start) | async-done | bytes 1048608 | tf_op jit(solution)/shard_map/all_to_all | solution.py:467
  58.4 11.2 %all-to-all-start.1 = ((bf16[128,2,8,128]{3,2,1,0:T(8,128)(2,1)}), bf16[128,2,8,128]{3,2,1,0:T(8,128)(2,1)S(1)}, u32[]{:S(2)}, u32[]{:S(2)}) async-start(bf16[128,2,8,128]{3,2,1,0:T(8,128)(2,1)} %pad_maximum_fusion), calls=%async_computation.1 | async-start | bytes 1048576 | tf_op jit(solution)/shard_map/all_to_all | solution.py:467
  69.6 0.0 all-gather.4.cloned.1.call-start
  69.7 0.0 all-gather.6.cloned.1.call-done
  69.7 0.0 copy-start.2
  69.7 1.6 copy-done.2
  71.3 4.9 %project.1 = (bf16[128,1024]{1,0:T(8,128)(2,1)S(1)}, bf16[128,1024]{1,0:T(8,128)(2,1)}, bf16[128,1024]{1,0:T(8,128)(2,1)}, bf16[128,1024]{1,0:T(8,128)(2,1)}, bf...) custom-call(s32[1]{0:T(128)} %bitcast.8.column_ref, bf16[1024,512]{1,0:T(8,128)(2,1)S(1)} %bitcast.34, ...), custom_call_target="tpu_custom_call" | custom-call | tf_op jit(solution)/shard_map/project/pallas_call | solution.py:354
  76.2 3.3 %collective-permute-start.3 = (bf16[1024,256]{1,0:T(8,128)(2,1)S(1)}, bf16[1024,256]{1,0:T(8,128)(2,1)S(1)}, u32[]{:S(2)}, u32[]{:S(2)}) collective-permute-start(bf16[1024,256]{1,0:T(8,128)(2,1)S(1)} %get-tuple-element.39.low), channel_id=1, source_target_pairs={{0,1},{1,0},{2,3},{3,2},{4,5},{5,4},{6,7},{7,6},{8,9},{9,8},{10,11... | collective-permute-start | bytes 1572872 | tf_op jit(solution)/shard_map/ppermute | solution.py:498
  79.5 3.1 %collective-permute-start = (bf16[128,1024]{1,0:T(8,128)(2,1)}, bf16[128,1024]{1,0:T(8,128)(2,1)S(1)}, u32[]{:S(2)}, u32[]{:S(2)}) collective-permute-start(bf16[128,1024]{1,0:T(8,128)(2,1)} %get-tuple-element.35), channel_id=1, source_target_pairs={{0,32},{32,64},{64,96},{96,0},{1,33},{33,65},{65,97},{97,1},{2,34}... | collective-permute-start | bytes 786440 | tf_op jit(solution)/shard_map/ppermute | solution.py:495
  82.6 4.4 %collective-permute-start.1 = (bf16[128,1024]{1,0:T(8,128)(2,1)}, bf16[128,1024]{1,0:T(8,128)(2,1)}, u32[]{:S(2)}, u32[]{:S(2)}) collective-permute-start(bf16[128,1024]{1,0:T(8,128)(2,1)} %get-tuple-element.36), channel_id=1, source_target_pairs={{0,64},{32,96},{64,0},{96,32},{1,65},{33,97},{65,1},{97,33},{2,66}... | collective-permute-start | bytes 786440 | tf_op jit(solution)/shard_map/ppermute | solution.py:495
  87.0 3.1 %collective-permute-start.2 = (bf16[128,1024]{1,0:T(8,128)(2,1)}, bf16[128,1024]{1,0:T(8,128)(2,1)}, u32[]{:S(2)}, u32[]{:S(2)}) collective-permute-start(bf16[128,1024]{1,0:T(8,128)(2,1)} %get-tuple-element.37), channel_id=1, source_target_pairs={{0,96},{32,0},{64,32},{96,64},{1,97},{33,1},{65,33},{97,65},{2,98}... | collective-permute-start | bytes 786440 | tf_op jit(solution)/shard_map/ppermute | solution.py:495
  90.1 0.0 copy-done.9
  90.1 0.1 dynamic_slice.7.skip_ref
  90.2 0.0 all-to-all-done.1
  90.2 5.9 %early_dmix.1 = (bf16[1024,128]{1,0:T(8,128)(2,1)S(1)}, bf16[256,512]{1,0:T(8,128)(2,1)S(1)}) custom-call(bf16[8,4096,128]{2,1,0:T(8,128)(2,1)} %copy-done.1, f32[8]{0:T(128)S(1)} %dynamic_slice.7.skip_ref, bf16[2048,128]{1,0:T(8,128)(2,1)S(1)} %bitcast.31), custom_call_target="tpu_custom_call" | custom-call | tf_op jit(solution)/shard_map/early_dmix/pallas_call | solution.py:331
  96.1 0.0 copy-start.4
  96.1 0.2 collective-permute-done.3.other_low
  96.4 0.0 collective-permute-done.part1
  96.4 0.4 collective-permute-done.1.part2
  96.7 1.2 collective-permute-done.2.part3
  97.9 1.2 join.1
  99.1 0.0 copy-done.4
  99.1 29.3 %all_to_all.20 = bf16[32,16,512]{2,1,0:T(8,128)(2,1)S(1)} all-to-all(bf16[32,16,512]{2,1,0:T(8,128)(2,1)S(1)} %bitcast.36), channel_id=1, replica_groups=mesh['dp'=4,'tensor'=4,'context'=32] {'context'}, dimensions={0} | all-to-all | bytes 1048576 | tf_op jit(solution)/shard_map/all_to_all | solution.py:467
  128.4 0.7 slice_bitcast_fusion
  129.1 0.0 all-gather.4.cloned.1.call-update
  129.1 3.4 %collective-permute-start.4 = (bf16[1024,256]{1,0:T(8,128)(2,1)S(1)}, bf16[1024,256]{1,0:T(8,128)(2,1)}, u32[]{:S(2)}, u32[]{:S(2)}) collective-permute-start(bf16[1024,256]{1,0:T(8,128)(2,1)S(1)} %get-tuple-element.47.high), channel_id=1, source_target_pairs={{0,1},{1,0},{2,3},{3,2},{4,5},{5,4},{6,7},{7,6},{8,9},{9,8},{10,11... | collective-permute-start | bytes 1572872 | tf_op jit(solution)/shard_map/ppermute | solution.py:503
  132.5 0.0 copy-start.5
  132.5 0.9 copy-done.5
  133.5 6.8 %late_conv.1 = (bf16[2048,128]{1,0:T(8,128)(2,1)}, bf16[1024,128]{1,0:T(8,128)(2,1)S(1)}) custom-call(bf16[8,4096,128]{2,1,0:T(8,128)(2,1)} %copy-done.1, f32[8]{0:T(128)S(1)} %dynamic_slice.7.skip_ref, bf16[2048,128]{1,0:T(8,128)(2,1)S(1)} %bitcast.32, bf16[512,512]{1,0:T(8,128)(2,1)S(1)} %bitcast.35, bf16[1024,128]{1,0:T(8,128)(2,1)S(1)} %copy-done.5), custom_call_target="tpu_custom_call" | custom-call | tf_op jit(solution)/shard_map/late_conv/pallas_call | solution.py:420
  140.3 9.7 %all-to-all-start.3 = ((bf16[128,2,8,128]{3,2,1,0:T(8,128)(2,1)}), bf16[128,2,8,128]{3,2,1,0:T(8,128)(2,1)}, u32[]{:S(2)}, u32[]{:S(2)}) async-start(bf16[128,2,8,128]{3,2,1,0:T(8,128)(2,1)} %bitcast.12), calls=%async_computation.3 | async-start | bytes 1048576 | tf_op jit(solution)/shard_map/all_to_all | solution.py:467
  150.0 0.1 pad_add_fusion.place_ref
  150.0 7.4 %late_fgrad.1.fgrad_ref = f32[8,4096]{1,0:T(8,128)S(1)} custom-call(bf16[2048,128]{1,0:T(8,128)(2,1)S(1)} %bitcast.33, bf16[1024,128]{1,0:T(8,128)(2,1)S(1)} %get-tuple-element.45.mix_ref), custom_call_target="tpu_custom_call" | custom-call | tf_op jit(solution)/shard_map/late_fgrad/pallas_call | solution.py:448
  157.4 0.0 all-gather.4.cloned.1.call-done.dvalue_ref
  157.4 0.0 collective-permute-done.4.other_high
  157.4 0.0 copy-start.3
  157.5 1.2 copy-done.3
  158.7 2.5 %back.1 = (bf16[288,1024]{1,0:T(8,128)(2,1)S(1)}, f32[256,1024]{1,0:T(8,128)S(1)}) custom-call(s32[3]{0:T(128)S(1)} %pad_add_fusion.place_ref, bf16[1024,512]{1,0:T(8,128)(2,1)S(1)} %copy-done.3, bf16[1024,256]{1,0:T(8,128)(2,1)S(1)} %get-tuple-element.39.low, bf16[1024,256]{1,0:T(8,128)(2,1)S(1)} %get-tuple-element.47.high, ...), custom_call_target="tpu_custom_call" | custom-call | tf_op jit(solution)/shard_map/back/pallas_call | solution.py:386
  161.1 2.9 %collective-permute-start.5 = (bf16[288,1024]{1,0:T(8,128)(2,1)S(1)}, bf16[288,1024]{1,0:T(8,128)(2,1)S(1)}, u32[]{:S(2)}, u32[]{:S(2)}) collective-permute-start(bf16[288,1024]{1,0:T(8,128)(2,1)S(1)} %get-tuple-element.51), channel_id=1, source_target_pairs={{0,128},{128,0},{256,384},{384,256},{1,129},{129,1},{257,385},{385... | collective-permute-start | bytes 1769480 | tf_op jit(solution)/shard_map/ppermute | solution.py:512
  164.0 1.6 collective-permute-done.5.received_ref
  165.6 0.7 middle.1
  166.3 2.7 %collective-permute-start.6 = (bf16[192,1024]{1,0:T(8,128)(2,1)S(1)}, bf16[192,1024]{1,0:T(8,128)(2,1)S(1)}, u32[]{:S(2)}, u32[]{:S(2)}) collective-permute-start(bf16[192,1024]{1,0:T(8,128)(2,1)S(1)} %get-tuple-element.53), channel_id=1, source_target_pairs={{0,256},{128,384},{256,0},{384,128},{1,257},{129,385},{257,1},{385... | collective-permute-start | bytes 1179656 | tf_op jit(solution)/shard_map/ppermute | solution.py:514
  169.0 0.6 all-to-all-done.3
  169.6 1.7 slice_bitcast_fusion.1
  171.3 2.0 %fusion.2 = (bf16[1,1024,128]{2,1,0:T(8,128)(2,1)}, bf16[1,1024,128]{2,1,0:T(8,128)(2,1)}) fusion(bf16[1,1024,128]{2,1,0:T(8,128)(2,1)} %param.13, bf16[128,2,8,128]{3,2,1,0:T(8,128)(2,1)} %all-to-all-done.3, bf16[1,1024,128]{2,1,0:T(8,128)(2,1)} %param.9), kind=kLoop, calls=%fused_computation.5 | loop fusion | flops 917504 | bytes 1310720 | tf_op jit(solution)/shard_map/convert_element_type | solution.py:521
  173.3 5.2 %collective-permute-done.6.received_ref = bf16[192,1024]{1,0:T(8,128)(2,1)S(1)} collective-permute-done((bf16[192,1024]{1,0:T(8,128)(2,1)S(1)}, bf16[192,1024]{1,0:T(8,128)(2,1)S(1)}, u32[]{:S(2)}, u32[]{:S(2)}) %collective-permute-start.6) | collective-permute-done | bytes 393248 | tf_op jit(solution)/shard_map/ppermute | solution.py:514
  178.5 1.5 last.1
  180.0 1.3 slice_reduce_fusion
  (2 shorter events, 0.0 us)
Async XLA Ops:
  7.2 20.4 %copy-start = (f32[32,4096]{1,0:T(8,128)S(1)}, f32[32,4096]{1,0:T(8,128)}, u32[]{:S(2)}) copy-start(f32[32,4096]{1,0:T(8,128)} %param.11) | copy-start | bytes 1572868
  7.2 27.2 %copy-start.6 = (bf16[1,1024,128]{2,1,0:T(8,128)(2,1)S(1)}, bf16[1,1024,128]{2,1,0:T(8,128)(2,1)}, u32[]{:S(2)}) copy-start(bf16[1,1024,128]{2,1,0:T(8,128)(2,1)} %param.13) | copy-start | bytes 786436
  7.2 27.2 %copy-start.7 = (bf16[1,1024,128]{2,1,0:T(8,128)(2,1)S(1)}, bf16[1,1024,128]{2,1,0:T(8,128)(2,1)}, u32[]{:S(2)}) copy-start(bf16[1,1024,128]{2,1,0:T(8,128)(2,1)} %param.9) | copy-start | bytes 786436
  7.2 27.3 %copy-start.8 = (bf16[1,1024,128]{2,1,0:T(8,128)(2,1)S(1)}, bf16[1,1024,128]{2,1,0:T(8,128)(2,1)}, u32[]{:S(2)}) copy-start(bf16[1,1024,128]{2,1,0:T(8,128)(2,1)} %param.10) | copy-start | bytes 786436
  7.2 62.5 %all-gather.6.cloned.1.call-start = ((), (), s32[]{:S(2)}) async-start(), calls=%async_computation.5 | async-start | bytes 2359296 | tf_op jit(solution)/shard_map/all_gather | solution.py:477
  11.0 79.1 %copy-start.9 = (f32[32]{0:T(128)S(1)}, f32[32]{0:T(128)}, u32[]{:S(2)}) copy-start(f32[32]{0:T(128)} %param.12) | copy-start | bytes 388
  11.0 47.5 %all-to-all-start = ((bf16[32,32,512]{2,1,0:T(8,128)(2,1)}), bf16[32,32,512]{2,1,0:T(8,128)(2,1)S(1)}, u32[]{:S(2)}, u32[]{:S(2)}) async-start(bf16[32,32,512]{2,1,0:T(8,128)(2,1)} %bitcast.5), calls=%async_computation | async-start | bytes 2097152 | tf_op jit(solution)/shard_map/all_to_all | solution.py:467
  31.1 3.3 %copy-start.1 = (bf16[8,4096,128]{2,1,0:T(8,128)(2,1)}, bf16[8,4096,128]{2,1,0:T(8,128)(2,1)S(1)}, u32[]{:S(2)}) copy-start(bf16[8,4096,128]{2,1,0:T(8,128)(2,1)S(1)} %build_taps.1.taps_ref) | copy-start | bytes 25165828
  58.4 31.8 %all-to-all-start.1 = ((bf16[128,2,8,128]{3,2,1,0:T(8,128)(2,1)}), bf16[128,2,8,128]{3,2,1,0:T(8,128)(2,1)S(1)}, u32[]{:S(2)}, u32[]{:S(2)}) async-start(bf16[128,2,8,128]{3,2,1,0:T(8,128)(2,1)} %pad_maximum_fusion), calls=%async_computation.1 | async-start | bytes 1048576 | tf_op jit(solution)/shard_map/all_to_all | solution.py:467
  69.6 87.8 %all-gather.4.cloned.1.call-start = ((), (), s32[]{:S(2)}) async-start(), calls=%async_computation.4 | async-start | bytes 1310720 | tf_op jit(solution)/shard_map/all_gather | solution.py:505
  69.7 1.6 copy-start.2
  76.2 20.2 %collective-permute-start.3 = (bf16[1024,256]{1,0:T(8,128)(2,1)S(1)}, bf16[1024,256]{1,0:T(8,128)(2,1)S(1)}, u32[]{:S(2)}, u32[]{:S(2)}) collective-permute-start(bf16[1024,256]{1,0:T(8,128)(2,1)S(1)} %get-tuple-element.39.low), channel_id=1, source_target_pairs={{0,1},{1,0},{2,3},{3,2},{4,5},{5,4},{6,7},{7,6},{8,9},{9,8},{10,11... | collective-permute-start | bytes 1572872 | tf_op jit(solution)/shard_map/ppermute | solution.py:498
  79.5 16.9 %collective-permute-start = (bf16[128,1024]{1,0:T(8,128)(2,1)}, bf16[128,1024]{1,0:T(8,128)(2,1)S(1)}, u32[]{:S(2)}, u32[]{:S(2)}) collective-permute-start(bf16[128,1024]{1,0:T(8,128)(2,1)} %get-tuple-element.35), channel_id=1, source_target_pairs={{0,32},{32,64},{64,96},{96,0},{1,33},{33,65},{65,97},{97,1},{2,34}... | collective-permute-start | bytes 786440 | tf_op jit(solution)/shard_map/ppermute | solution.py:495
  82.6 14.1 %collective-permute-start.1 = (bf16[128,1024]{1,0:T(8,128)(2,1)}, bf16[128,1024]{1,0:T(8,128)(2,1)}, u32[]{:S(2)}, u32[]{:S(2)}) collective-permute-start(bf16[128,1024]{1,0:T(8,128)(2,1)} %get-tuple-element.36), channel_id=1, source_target_pairs={{0,64},{32,96},{64,0},{96,32},{1,65},{33,97},{65,1},{97,33},{2,66}... | collective-permute-start | bytes 786440 | tf_op jit(solution)/shard_map/ppermute | solution.py:495
  87.0 10.9 %collective-permute-start.2 = (bf16[128,1024]{1,0:T(8,128)(2,1)}, bf16[128,1024]{1,0:T(8,128)(2,1)}, u32[]{:S(2)}, u32[]{:S(2)}) collective-permute-start(bf16[128,1024]{1,0:T(8,128)(2,1)} %get-tuple-element.37), channel_id=1, source_target_pairs={{0,96},{32,0},{64,32},{96,64},{1,97},{33,1},{65,33},{97,65},{2,98}... | collective-permute-start | bytes 786440 | tf_op jit(solution)/shard_map/ppermute | solution.py:495
  96.1 3.0 %copy-start.4 = (bf16[1024,128]{1,0:T(8,128)(2,1)}, bf16[1024,128]{1,0:T(8,128)(2,1)S(1)}, u32[]{:S(2)}) copy-start(bf16[1024,128]{1,0:T(8,128)(2,1)S(1)} %get-tuple-element.43.dmix_ref) | copy-start | bytes 786436
  129.1 28.3 %collective-permute-start.4 = (bf16[1024,256]{1,0:T(8,128)(2,1)S(1)}, bf16[1024,256]{1,0:T(8,128)(2,1)}, u32[]{:S(2)}, u32[]{:S(2)}) collective-permute-start(bf16[1024,256]{1,0:T(8,128)(2,1)S(1)} %get-tuple-element.47.high), channel_id=1, source_target_pairs={{0,1},{1,0},{2,3},{3,2},{4,5},{5,4},{6,7},{7,6},{8,9},{9,8},{10,11... | collective-permute-start | bytes 1572872 | tf_op jit(solution)/shard_map/ppermute | solution.py:503
  132.5 1.0 copy-start.5
  140.3 29.4 %all-to-all-start.3 = ((bf16[128,2,8,128]{3,2,1,0:T(8,128)(2,1)}), bf16[128,2,8,128]{3,2,1,0:T(8,128)(2,1)}, u32[]{:S(2)}, u32[]{:S(2)}) async-start(bf16[128,2,8,128]{3,2,1,0:T(8,128)(2,1)} %bitcast.12), calls=%async_computation.3 | async-start | bytes 1048576 | tf_op jit(solution)/shard_map/all_to_all | solution.py:467
  157.4 1.2 copy-start.3
  161.1 4.5 %collective-permute-start.5 = (bf16[288,1024]{1,0:T(8,128)(2,1)S(1)}, bf16[288,1024]{1,0:T(8,128)(2,1)S(1)}, u32[]{:S(2)}, u32[]{:S(2)}) collective-permute-start(bf16[288,1024]{1,0:T(8,128)(2,1)S(1)} %get-tuple-element.51), channel_id=1, source_target_pairs={{0,128},{128,0},{256,384},{384,256},{1,129},{129,1},{257,385},{385... | collective-permute-start | bytes 1769480 | tf_op jit(solution)/shard_map/ppermute | solution.py:512
  166.3 12.2 %collective-permute-start.6 = (bf16[192,1024]{1,0:T(8,128)(2,1)S(1)}, bf16[192,1024]{1,0:T(8,128)(2,1)S(1)}, u32[]{:S(2)}, u32[]{:S(2)}) collective-permute-start(bf16[192,1024]{1,0:T(8,128)(2,1)S(1)} %get-tuple-element.53), channel_id=1, source_target_pairs={{0,256},{128,384},{256,0},{384,128},{1,257},{129,385},{257,1},{385... | collective-permute-start | bytes 1179656 | tf_op jit(solution)/shard_map/ppermute | solution.py:514
Sparse Core Ops, SparseCore 0:
  10.1 57.3 all-gather.5
  129.3 25.2 all-gather.3

commit v4 on v3

v4 whole, which is shorter than its diff:
```python
import jax
import jax.numpy as jnp
from jax import lax
from jax.experimental import pallas as pl
from jax.experimental.pallas import tpu as pltpu
from jax.sharding import PartitionSpec as P

f32 = jnp.float32
bf16 = jnp.bfloat16

LANES = 128
GROUP = 8
SEQS = 4
BLOCKS = 32
ROWS = BLOCKS * SEQS
SIGNAL = ROWS * GROUP
TAPS = BLOCKS * LANES
WIDE = TAPS + LANES
DMIX, CONV, FGRAD = 1, 2, 8
NEAR = ((0, 0), (1, 0), (3, 0), (2, 0), (2, 1), (3, 1), (1, 1), (0, 1))
HALF = 16
SPAN = 1024


def pack_kernel(quarter_ref, weight_ref, out_ref, picks):
    @pl.when(pl.program_id(0) == 0)
    def _():
        source = lax.broadcasted_iota(jnp.int32, (SPAN, 2 * LANES), 0)
        target = lax.broadcasted_iota(jnp.int32, (SPAN, 2 * LANES), 1)
        wanted = (target % LANES // 4) * 32 + quarter_ref[0] * GROUP + (target // LANES) * 4 + target % 4
        chosen = (source == wanted).astype(f32).astype(bf16)
        for part in range(4):
            columns = weight_ref[:, part * SPAN : (part + 1) * SPAN]
            picked = jnp.dot(columns, chosen, preferred_element_type=f32).astype(bf16)
            for side in range(2):
                picks[side, :, part * LANES : (part + 1) * LANES] = picked[:, side * LANES : (side + 1) * LANES]

    count = picks.shape[1]
    for dest in range(out_ref.shape[0] // count):
        out_ref[dest * count : (dest + 1) * count, :] = picks[dest % 2]


def load_pair(pair_ref):
    both = pair_ref[...].astype(f32).reshape(ROWS, 2, GROUP, LANES)
    return both[:, 0].reshape(SIGNAL, LANES), both[:, 1].reshape(SIGNAL, LANES)


def taps_kernel(filters_ref, taps_ref, rolled):
    chan = pl.program_id(0)

    @pl.when(chan == 0)
    def _():
        padded = jnp.concatenate([filters_ref[...], jnp.zeros((GROUP, LANES), f32)], axis=1)
        for row in range(GROUP):
            turned = pltpu.roll(padded, row, 1) if row else padded
            for block in range(BLOCKS + 1):
                rolled[block, row * GROUP : (row + 1) * GROUP, :] = turned[:, block * LANES : (block + 1) * LANES]

    base = jnp.concatenate(
        [rolled[block, pl.ds(chan, GROUP, stride=GROUP), :] for block in range(BLOCKS + 1)], axis=1
    )
    for pair in range(LANES // 16):
        low = pltpu.roll(base, 16 * pair, 1) if pair else base
        high = pltpu.roll(base, 16 * pair + 8, 1)
        tile = jnp.concatenate([low[:, :TAPS], high[:, :TAPS]], axis=0).astype(bf16)
        for block in range(BLOCKS):
            taps_ref[0, block * LANES + 16 * pair : block * LANES + 16 * pair + 16, :] = tile[
                :, block * LANES : (block + 1) * LANES
            ]


def fill_ahead(grads, copies, chan):
    for part in range(SEQS):
        copies[part, 0:ROWS, :] = grads[pl.ds(part * SEQS * GROUP + chan, ROWS, stride=GROUP), :].astype(bf16)


def ahead_of(copies, block):
    return copies[block % 4, block // 4 * 16 : block // 4 * 16 + ROWS, :]


def clear_ahead(grads, copies, dconv):
    grads[0:SIGNAL, :] = dconv
    grads[SIGNAL:, :] = jnp.zeros((LANES, LANES), f32)
    for copy in copies:
        for part in range(SEQS):
            copy[part, ROWS:, :] = jnp.zeros((ROWS, LANES), bf16)


def start_taps(taps_ref, taps, done):
    for chan in range(GROUP):
        pltpu.make_async_copy(taps_ref.at[chan], taps.at[chan], done.at[chan]).start()


def wait_taps(taps_ref, taps, done, chan):
    pltpu.make_async_copy(taps_ref.at[chan], taps.at[chan], done.at[chan]).wait()


def dmix_kernel(taps_ref, skip_ref, pair_ref, dmix_ref, dvalue_ref, taps, done, grads, result, *copies):
    step = pl.program_id(0)

    @pl.when(step == 0)
    def _():
        start_taps(taps_ref, taps, done)
        clear_ahead(grads, copies, load_pair(pair_ref)[0])

    for index, copy in enumerate(copies):
        chan = step * DMIX + index
        fill_ahead(grads, copy, chan)
        ahead = jnp.concatenate([ahead_of(copy, block) for block in range(BLOCKS)], axis=1)
        wait_taps(taps_ref, taps, done, chan)
        wide = jnp.concatenate([taps[chan, block * LANES : (block + 1) * LANES, :] for block in range(BLOCKS)], axis=1)
        total = lax.dot_general(ahead, wide, (((1,), (1,)), ((), ())), preferred_element_type=f32)
        own = grads[pl.ds(chan, ROWS, stride=GROUP), :]
        result[pl.ds(chan, ROWS, stride=GROUP), :] = total + skip_ref[chan] * own

    @pl.when(step == pl.num_programs(0) - 1)
    def _():
        _, key = load_pair(pair_ref)
        dmix = result[...].astype(bf16)
        dmix_ref[...] = dmix
        dvalue = (dmix.astype(f32) * key).reshape(BLOCKS, SEQS, GROUP, LANES)
        for seq in range(SEQS):
            dvalue_ref[:, seq * LANES : (seq + 1) * LANES] = (
                dvalue[:, seq].reshape(BLOCKS * GROUP, LANES).astype(bf16)
            )


def project_kernel(column_ref, weight_ref, tokens_ref, out0, out1, out2, out3, turned):
    @pl.when(pl.program_id(0) == 0)
    def _():
        for step in range(4):
            lanes = pl.ds(pl.multiple_of((column_ref[0] + step) % 4 * LANES, LANES), LANES)
            turned[step * LANES : (step + 1) * LANES, :] = weight_ref[:, lanes].T

    product = lax.dot_general(turned[...], tokens_ref[...], (((1,), (1,)), ((), ())), preferred_element_type=f32)
    product = product.astype(bf16)
    for step, out_ref in enumerate((out0, out1, out2, out3)):
        out_ref[...] = product[step * LANES : (step + 1) * LANES, :]


def halves_of(even, odd):
    upper = lax.broadcasted_iota(jnp.int32, even.shape, 0) < 4
    return jnp.where(upper, even, pltpu.roll(odd, 4, 0)), jnp.where(upper, pltpu.roll(even, 4, 0), odd)


def join_kernel(part0, part1, part2, part3, dvalue_ref, out_ref):
    value = part0[...].astype(f32) + part1[...].astype(f32) + part2[...].astype(f32) + part3[...].astype(f32)
    value = value.astype(bf16).astype(f32)
    dvalue = dvalue_ref[...].astype(f32)
    sides = []
    for side in range(2):
        order = [NEAR.index((seq, side)) for seq in range(SEQS)]
        sides.append(jnp.concatenate([value[:, piece * LANES : (piece + 1) * LANES] for piece in order], axis=1))
    for two in range(BLOCKS // 2):
        rows = [part[two * GROUP : (two + 1) * GROUP, :] for part in sides]
        for place, tile in enumerate(halves_of(*rows)):
            index = 2 * two + place
            tile = jnp.concatenate([tile, dvalue[index * GROUP : (index + 1) * GROUP, :]], axis=0)
            out_ref[index * HALF : (index + 1) * HALF, :] = tile.astype(bf16)


def back_kernel(place_ref, dvalue_ref, weights_ref, sent_ref, kept_ref, total):
    index = pl.program_id(0)
    dvalue = dvalue_ref[...].astype(f32)
    tiles = [[], []]
    for two in range(BLOCKS // 2):
        start = two * HALF
        pair = halves_of(dvalue[start : start + GROUP, :], dvalue[start + GROUP : start + HALF, :])
        for half in range(2):
            tiles[half].append(pair[half])
    rows = jnp.concatenate([jnp.concatenate(part, axis=0).astype(bf16) for part in tiles], axis=0)
    columns = jnp.concatenate([weights_ref[0:SPAN, :], weights_ref[SPAN:, :]], axis=1)
    term = lax.dot_general(rows, columns, (((0,), (1,)), ((), ())), preferred_element_type=f32)

    @pl.when(index == 0)
    def _():
        total[...] = term

    @pl.when(index > 0)
    def _():
        total[...] += term

    @pl.when(index == 3)
    def _():
        core = place_ref[1]
        for chip in range(2):
            rows = slice(chip * LANES, (chip + 1) * LANES)
            sent_ref[rows, :] = total[pl.ds((2 * chip + 1 - core) * LANES, LANES), :].astype(bf16)
            kept_ref[rows, :] = total[pl.ds((2 * chip + core) * LANES, LANES), :]


def middle_kernel(place_ref, kept_ref, received_ref, sent_ref, rest_ref):
    chip = place_ref[2]
    for target, index in ((sent_ref, 1 - chip), (rest_ref, chip)):
        rows = pl.ds(pl.multiple_of(index * LANES, LANES), LANES)
        target[...] = (kept_ref[rows, :] + received_ref[rows, :].astype(f32)).astype(bf16)


def last_kernel(place_ref, rest_ref, received_ref, near_ref, far_ref, grad_ref, fgrad_ref, skip_ref):
    grad_ref[...] = (rest_ref[...].astype(f32) + received_ref[...].astype(f32)).astype(bf16)
    pieces = []
    for ref in (near_ref, far_ref):
        both = ref[...].astype(f32)
        pieces += [both[0 : 4 * GROUP, :], both[4 * GROUP :, :]]
    for bit, flag in ((1, place_ref[1]), (2, place_ref[2])):
        pieces = [jnp.where(flag == 0, pieces[index], pieces[index ^ bit]) for index in range(SEQS)]
    for index, piece in enumerate(pieces):
        for part in range(4):
            rows = slice(part * GROUP, (part + 1) * GROUP)
            fgrad_ref[index * GROUP : (index + 1) * GROUP, part * SPAN : (part + 1) * SPAN] = piece[rows, :]
    shape = (SEQS * GROUP, LANES)
    diagonal = lax.broadcasted_iota(jnp.int32, shape, 0) == lax.broadcasted_iota(jnp.int32, shape, 1)
    lag0 = jnp.broadcast_to(fgrad_ref[:, 0:1], shape)
    skip_ref[...] = jnp.sum(jnp.where(diagonal, lag0, 0.0), axis=0, keepdims=True)


def conv_kernel(taps_ref, skip_ref, pair_ref, value_ref, dmix_ref, out_ref, mix_ref, taps, done, mixes, values, result, *copies):
    step = pl.program_id(0)

    @pl.when(step == 0)
    def _():
        start_taps(taps_ref, taps, done)
        _, key = load_pair(pair_ref)
        value = value_ref[...].astype(f32)
        for two in range(BLOCKS // 2):
            start = two * 2 * HALF
            pair = halves_of(value[start : start + GROUP, :], value[start + HALF : start + HALF + GROUP, :])
            for side in range(2):
                for seq in range(SEQS):
                    row = ((2 * two + side) * SEQS + seq) * GROUP
                    values[row : row + GROUP, :] = pair[side][:, seq * LANES : (seq + 1) * LANES]
        mix = (key * values[...]).astype(bf16)
        mix_ref[...] = mix
        mixes[0:LANES, :] = jnp.zeros((LANES, LANES), f32)
        mixes[LANES:, :] = mix.astype(f32)
        for copy in copies:
            for part in range(SEQS):
                copy[part, 0:ROWS, :] = jnp.zeros((ROWS, LANES), bf16)

    for index, copy in enumerate(copies):
        chan = step * CONV + index
        for part in range(SEQS):
            copy[part, ROWS:, :] = mixes[
                pl.ds(LANES - part * SEQS * GROUP + chan, ROWS, stride=GROUP), :
            ].astype(bf16)
        behind = [
            copy[block % 4, ROWS - block // 4 * 16 : 2 * ROWS - block // 4 * 16, :] for block in range(BLOCKS)
        ]
        own = mixes[pl.ds(LANES + chan, ROWS, stride=GROUP), :]
        wait_taps(taps_ref, taps, done, chan)
        total = jnp.dot(jnp.concatenate(behind, axis=1), taps[chan], preferred_element_type=f32)
        result[pl.ds(chan, ROWS, stride=GROUP), :] = total + skip_ref[chan] * own

    @pl.when(step == pl.num_programs(0) - 1)
    def _():
        kgrad = dmix_ref[...].astype(f32) * values[...]
        both = [result[...].reshape(ROWS, 1, GROUP, LANES), kgrad.reshape(ROWS, 1, GROUP, LANES)]
        out_ref[...] = jnp.concatenate(both, axis=1).reshape(2 * SIGNAL, LANES).astype(bf16)


def fgrad_kernel(pair_ref, mix_ref, fgrad_ref, mixes, grads, sums, *scratch):
    step = pl.program_id(0)
    copies, corrs = scratch[:FGRAD], scratch[FGRAD:]

    @pl.when(step == 0)
    def _():
        clear_ahead(grads, copies, load_pair(pair_ref)[0])
        mixes[...] = mix_ref[...].astype(f32)
        for corr in corrs:
            corr[:, TAPS:] = jnp.zeros((LANES, LANES), f32)

    for index, (copy, corr) in enumerate(zip(copies, corrs)):
        chan = step * FGRAD + index
        fill_ahead(grads, copy, chan)
        own = mixes[pl.ds(chan, ROWS, stride=GROUP), :].T.astype(bf16)
        for block in range(0, BLOCKS, 2):
            two = jnp.concatenate([ahead_of(copy, block), ahead_of(copy, block + 1)], axis=1)
            corr[:, block * LANES : (block + 2) * LANES] = jnp.dot(own, two, preferred_element_type=f32)
    for index, corr in enumerate(corrs):
        chan = step * FGRAD + index
        acc = corr[0:GROUP, :]
        for group in range(1, LANES // GROUP):
            acc = acc + pltpu.roll(corr[group * GROUP : (group + 1) * GROUP, :], WIDE - group * GROUP, 1)
        rows = pl.ds(pl.multiple_of(chan * GROUP, GROUP), GROUP)
        for block in range(BLOCKS + 1):
            sums[block, rows, :] = acc[:, block * LANES : (block + 1) * LANES]

    @pl.when(step == pl.num_programs(0) - 1)
    def _():
        fgrad = None
        for row in range(GROUP):
            part = jnp.concatenate(
                [sums[block, pl.ds(row, GROUP, stride=GROUP), :] for block in range(BLOCKS + 1)], axis=1
            )
            fgrad = part if row == 0 else fgrad + pltpu.roll(part, WIDE - row, 1)
        parts = [fgrad[:, part * SPAN : (part + 1) * SPAN] for part in range(4)]
        fgrad_ref[...] = jnp.concatenate(parts, axis=0).astype(bf16)


def whole(shape):
    return pl.BlockSpec(shape, lambda chan: (0,) * len(shape))


params = pltpu.CompilerParams(vmem_limit_bytes=24 * 1024 * 1024)
smem = pl.BlockSpec(memory_space=pltpu.SMEM)
taps_spec = pl.BlockSpec((1, TAPS, LANES), lambda chan: (chan, 0, 0))
any_spec = pl.BlockSpec(memory_space=pl.ANY)
taps_scratch = [pltpu.VMEM((GROUP, TAPS, LANES), bf16), pltpu.SemaphoreType.DMA((GROUP,))]
pair_spec = whole((2 * SIGNAL, LANES))


def pack(quarter, weight):
    steps, rows = 4, weight.shape[0]
    return pl.pallas_call(
        pack_kernel,
        grid=(steps,),
        in_specs=[smem, pl.BlockSpec(weight.shape, lambda step: (0, 0))],
        out_specs=pl.BlockSpec((rows * BLOCKS // steps, 4 * LANES), lambda step: (step, 0)),
        out_shape=jax.ShapeDtypeStruct((rows * BLOCKS, 4 * LANES), bf16),
        scratch_shapes=[pltpu.VMEM((2, rows, 4 * LANES), bf16)],
        compiler_params=params,
        name="pack",
    )(quarter, pltpu.with_memory_space_constraint(weight, pltpu.HBM))


def build_taps(filters):
    return pl.pallas_call(
        taps_kernel,
        grid=(GROUP,),
        in_specs=[whole((GROUP, TAPS))],
        out_specs=taps_spec,
        out_shape=jax.ShapeDtypeStruct((GROUP, TAPS, LANES), bf16),
        scratch_shapes=[pltpu.VMEM((BLOCKS + 1, GROUP * GROUP, LANES), f32)],
        compiler_params=params,
        name="build_taps",
    )(filters)


def early_dmix(taps, skip, pair):
    return pl.pallas_call(
        dmix_kernel,
        grid=(GROUP // DMIX,),
        in_specs=[any_spec, smem, pair_spec],
        out_specs=[whole((SIGNAL, LANES)), whole((BLOCKS * GROUP, SEQS * LANES))],
        out_shape=[
            jax.ShapeDtypeStruct((SIGNAL, LANES), bf16),
            jax.ShapeDtypeStruct((BLOCKS * GROUP, SEQS * LANES), bf16),
        ],
        scratch_shapes=taps_scratch
        + [
            pltpu.VMEM((SIGNAL + LANES, LANES), f32),
            pltpu.VMEM((SIGNAL, LANES), f32),
        ]
        + [pltpu.VMEM((SEQS, 2 * ROWS, LANES), bf16)] * DMIX,
        compiler_params=params,
        name="early_dmix",
    )(pltpu.with_memory_space_constraint(taps, pltpu.HBM), skip, pair)


def project(column, weight, tokens):
    count, steps = tokens.shape[0], 4
    return pl.pallas_call(
        project_kernel,
        grid=(steps,),
        in_specs=[smem, whole(weight.shape), pl.BlockSpec((count // steps, SPAN), lambda step: (step, 0))],
        out_specs=[pl.BlockSpec((LANES, count // steps), lambda step: (0, step))] * 4,
        out_shape=[jax.ShapeDtypeStruct((LANES, count), bf16)] * 4,
        scratch_shapes=[pltpu.VMEM((4 * LANES, SPAN), bf16)],
        compiler_params=params,
        name="project",
    )(column, *[pltpu.with_memory_space_constraint(x, pltpu.HBM) for x in (weight, tokens)])


def vmem_specs(count):
    return [smem] + [pl.BlockSpec(memory_space=pltpu.VMEM)] * count


def join(parts, dvalue):
    return pl.pallas_call(
        join_kernel,
        out_shape=jax.ShapeDtypeStruct((BLOCKS * HALF, SEQS * LANES), bf16),
        compiler_params=params,
        name="join",
    )(*parts, dvalue)


def back(place, dvalue, weights):
    return pl.pallas_call(
        back_kernel,
        grid=(4,),
        in_specs=[
            smem,
            pl.BlockSpec((BLOCKS * GROUP, SEQS * LANES), lambda step: (step, 0)),
            pl.BlockSpec((2 * SPAN, LANES), lambda step: (0, step)),
        ],
        out_specs=[whole((2 * LANES, SPAN)), whole((2 * LANES, SPAN))],
        out_shape=[
            jax.ShapeDtypeStruct((2 * LANES, SPAN), bf16),
            jax.ShapeDtypeStruct((2 * LANES, SPAN), f32),
        ],
        scratch_shapes=[pltpu.VMEM((SEQS * LANES, SPAN), f32)],
        compiler_params=params,
        name="back",
    )(place, *[pltpu.with_memory_space_constraint(x, pltpu.HBM) for x in (dvalue, weights)])


def middle(place, kept, received):
    return pl.pallas_call(
        middle_kernel,
        in_specs=vmem_specs(2),
        out_shape=[jax.ShapeDtypeStruct((LANES, SPAN), bf16)] * 2,
        compiler_params=params,
        name="middle",
    )(place, kept, received)


def last(place, rest, received, near, far):
    return pl.pallas_call(
        last_kernel,
        in_specs=vmem_specs(4),
        out_shape=[
            jax.ShapeDtypeStruct((LANES, SPAN), bf16),
            jax.ShapeDtypeStruct((2 * HALF, TAPS), f32),
            jax.ShapeDtypeStruct((1, LANES), f32),
        ],
        compiler_params=params,
        name="last",
    )(place, rest, received, near, far)


def late_conv(taps, skip, pair, value, dmix):
    return pl.pallas_call(
        conv_kernel,
        grid=(GROUP // CONV,),
        in_specs=[
            any_spec,
            smem,
            pair_spec,
            whole((BLOCKS * HALF, SEQS * LANES)),
            whole((SIGNAL, LANES)),
        ],
        out_specs=[whole((2 * SIGNAL, LANES)), whole((SIGNAL, LANES))],
        out_shape=[
            jax.ShapeDtypeStruct((2 * SIGNAL, LANES), bf16),
            jax.ShapeDtypeStruct((SIGNAL, LANES), bf16),
        ],
        scratch_shapes=taps_scratch
        + [
            pltpu.VMEM((SIGNAL + LANES, LANES), f32),
            pltpu.VMEM((SIGNAL, LANES), f32),
            pltpu.VMEM((SIGNAL, LANES), f32),
        ]
        + [pltpu.VMEM((SEQS, 2 * ROWS, LANES), bf16)] * CONV,
        compiler_params=params,
        name="late_conv",
    )(pltpu.with_memory_space_constraint(taps, pltpu.HBM), skip, pair, value, dmix)


def late_fgrad(pair, mix):
    return pl.pallas_call(
        fgrad_kernel,
        grid=(GROUP // FGRAD,),
        in_specs=[pair_spec, whole((SIGNAL, LANES))],
        out_specs=whole((4 * GROUP, SPAN)),
        out_shape=jax.ShapeDtypeStruct((4 * GROUP, SPAN), bf16),
        scratch_shapes=[
            pltpu.VMEM((SIGNAL, LANES), f32),
            pltpu.VMEM((SIGNAL + LANES, LANES), f32),
            pltpu.VMEM((BLOCKS + 1, GROUP * GROUP, LANES), f32),
        ]
        + [pltpu.VMEM((SEQS, 2 * ROWS, LANES), bf16)] * FGRAD
        + [pltpu.VMEM((LANES, WIDE), f32)] * FGRAD,
        compiler_params=params,
        name="late_fgrad",
    )(pair, mix)


def swap(values, axes, groups=None):
    return lax.all_to_all(values, axes, split_axis=0, concat_axis=0, tiled=True, axis_index_groups=groups)


def per_device(inputs, value_weight, query, key, filters, skip, cotangent):
    quarter = lax.axis_index("dp")
    side = lax.axis_index("context") % 2

    place = jnp.stack([side, quarter % 2, quarter // 2]).astype(jnp.int32)

    near = [[seq * BLOCKS + 2 * k + place for seq, place in NEAR] for k in range(BLOCKS // 2)]
    tokens = lax.all_gather(inputs[0], ("dp", "context"), axis=0, tiled=True, axis_index_groups=near)
    own_filters = lax.dynamic_slice_in_dim(filters, quarter * GROUP, GROUP, 0)
    own_skip = lax.dynamic_slice_in_dim(skip, quarter * GROUP, GROUP, 0)
    taps = build_taps(own_filters)

    packed = pack(quarter.astype(jnp.int32)[None], value_weight)
    weight = swap(packed.reshape(BLOCKS, value_weight.shape[0], 4 * LANES), "context").reshape(SPAN, 4 * LANES)

    query_part = query[0].astype(f32)
    upstream = cotangent[0].astype(f32)
    dconv = (upstream * query_part).astype(bf16)
    pair = jnp.concatenate([dconv.reshape(ROWS, 1, GROUP, LANES), key[0].reshape(ROWS, 1, GROUP, LANES)], axis=1)
    pair, weight, taps = lax.optimization_barrier((pair, weight, taps))
    pair = swap(pair, ("context", "dp")).reshape(2 * SIGNAL, LANES)

    column = lax.axis_index("tensor").astype(jnp.int32)[None]
    parts = project(column, weight, tokens)
    parts = [parts[0]] + [
        lax.ppermute(parts[step], "tensor", [(i, (i + step) % 4) for i in range(4)]) for step in (1, 2, 3)
    ]
    sides = [[2 * k, 2 * k + 1] for k in range(BLOCKS // 2)]
    weights = lax.all_gather(weight, "context", axis=0, tiled=True, axis_index_groups=sides)
    dmix, dvalue = early_dmix(taps, own_skip, pair)

    both = swap(join(parts, dvalue).reshape(BLOCKS, HALF, SEQS * LANES), "context")
    both, weights = lax.optimization_barrier((both, weights))
    dvalue = lax.all_gather(both[:, GROUP:].reshape(BLOCKS * GROUP, SEQS * LANES), "tensor", axis=0, tiled=True)
    out, mix = late_conv(taps, own_skip, pair, both.reshape(BLOCKS * HALF, SEQS * LANES), dmix)
    out = swap(out.reshape(ROWS, 2, GROUP, LANES), ("context", "dp"))
    fgrad = late_fgrad(pair, mix)

    def cross(values, bit):
        return lax.ppermute(values, "dp", [(i, i ^ bit) for i in range(SEQS)])

    place = jnp.stack([side, quarter % 2, quarter // 2]).astype(jnp.int32)
    chip_fgrads = jnp.concatenate([fgrad, cross(fgrad, 1)], axis=0)
    far_fgrads = cross(chip_fgrads, 2)
    dvalue, chip_fgrads = lax.optimization_barrier((dvalue, chip_fgrads))
    sent, kept = back(place, dvalue, weights)
    sent, rest = middle(place, kept, cross(sent, 1))
    input_grad, filter_grad, skip_grad = last(place, rest, cross(sent, 2), chip_fgrads, far_fgrads)
    skip_grad = skip_grad[0, : skip.shape[0]]

    conv = out[:, 0].reshape(SIGNAL, LANES).astype(f32)
    key_grad = out[:, 1].reshape(SIGNAL, LANES)
    gated = (query_part * conv).astype(bf16)
    query_grad = (upstream * conv).astype(bf16)
    return (gated[None], query_grad[None], key_grad[None], input_grad[None], filter_grad, skip_grad)


def solution(mesh):
    by_channel = P("dp", "tensor", "context")
    by_row = P(("tensor", "context"), None)
    in_specs = (
        P("dp", "context", "tensor"),
        by_row,
        by_channel,
        by_channel,
        by_row,
        P(("tensor", "context")),
        by_channel,
    )
    out_specs = (
        by_channel,
        by_channel,
        by_channel,
        P("dp", "context", "tensor"),
        by_row,
        P(("tensor", "context")),
    )
    return jax.shard_map(
        per_device, mesh=mesh, in_specs=in_specs, out_specs=out_specs, check_vma=False
    )
```

time: 191 us -> 185 us (0.969); the launches traced: 188 us -> 185 us
  blocking collectives: 29.3 us -> 0 us
  waiting for transfers between devices: 33 us -> 55.4 us
  starting transfers between devices: 60.4 us -> 70.8 us
  local copies, waits for them, and re-layouts: 10.9 us -> 6.32 us
    all_to_all x1 -> x0, blocking collectives: 29.3 us -> none  [swap(): lax.all_to_all(values, axes, split_axis=0, concat_axis=0, tiled=True, axi...]
    all_to_all x3 -> x4, waiting for transfers between devices: 23.7 us -> 36.1 us  [swap(): lax.all_to_all(values, axes, split_axis=0, concat_axis=0, tiled=True, axi...]
    all_to_all x3 -> x4, starting transfers between devices: 37.5 us -> 48.3 us  [swap(): lax.all_to_all(values, axes, split_axis=0, concat_axis=0, tiled=True, axi...]
    all_gather x0 -> x1, waiting for transfers between devices: none -> 10.4 us  [per_device(): lax.all_gather(weight, 'context', axis=0, tiled=True, axis_index_groups=s...]
    unnamed x20 -> x16, local copies, waits for them, and re-layouts: 7.05 us -> 4.28 us
  transfers between devices with their start and end apart: 12 -> 14, of which waited for: 7 -> 7; matrix products, arithmetic and copies ran while one was open for 3% -> 2% of each run, Pallas kernels for 18% -> 19%
where the time goes in v4:
time: 185 us
  starting transfers between devices  70.8 us (38%)
  waiting for transfers between devices  55.4 us (30%)
  Pallas kernels  36 us (19%)
  between operations  14.1 us (8%)
  local copies, waits for them, and re-layouts  6.32 us (3%)
  other arithmetic  1.96 us (1%)
    all_to_all x4, starting transfers between devices, swap(): lax.all_to_all(values, axes, split_axis=0, concat_axis=0, tiled=True, axi...  48.3 us
    all_to_all x4, waiting for transfers between devices, swap(): lax.all_to_all(values, axes, split_axis=0, concat_axis=0, tiled=True, axi...  36.1 us
    ppermute x4, starting transfers between devices, cross(): return lax.ppermute(values, 'dp', [(i, i ^ bit) for i in range(SEQS)])  11.7 us
    ppermute x3, starting transfers between devices, per_device(): lax.ppermute(parts[step], 'tensor', [(i, (i + step) % 4) for i in range(4)])  10.5 us
    all_gather x1, waiting for transfers between devices, per_device(): lax.all_gather(weight, 'context', axis=0, tiled=True, axis_index_groups=s...  10.4 us
    pallas_call x1, Pallas kernels, late_conv(): pl.pallas_call(conv_kernel, grid=(GROUP // CONV,), in_specs=[any_spec, sm...  6.69 us
    ppermute x4, waiting for transfers between devices, cross(): return lax.ppermute(values, 'dp', [(i, i ^ bit) for i in range(SEQS)])  6.47 us
    pallas_call x1, Pallas kernels, early_dmix(): pl.pallas_call(dmix_kernel, grid=(GROUP // DMIX,), in_specs=[any_spec, sm...  5.92 us
  transfers between devices with their start and end apart: 14, of which 7 were waited for; matrix products, arithmetic and copies ran while one was open for 2% of the time, Pallas kernels for 19%

profile of v4, /device:TPU:1, one launch (start us, length us, event | category | flops | bytes accessed | tf_op | source)
XLA Modules:
  0.0 184.6 jit_solution(11665278151871918825)
XLA Ops:
  7.2 0.0 copy-start
  7.2 0.0 all-gather.9.cloned.1.call-start
  7.2 0.7 all-gather.9.cloned.1.call-update
  7.9 3.0 %pack.1 = bf16[1024,512]{1,0:T(8,128)(2,1)} custom-call(s32[1]{0:T(128)} %bitcast.4.quarter_ref, bf16[32,4096]{1,0:T(8,128)(2,1)} %weight_ref.1), custom_call_target="tpu_custom_call" | custom-call | tf_op jit(solution)/shard_map/pack/pallas_call | solution.py:314
  10.9 16.5 %all-to-all-start = ((bf16[32,32,512]{2,1,0:T(8,128)(2,1)}), bf16[32,32,512]{2,1,0:T(8,128)(2,1)S(1)}, u32[]{:S(2)}, u32[]{:S(2)}) async-start(bf16[32,32,512]{2,1,0:T(8,128)(2,1)} %bitcast.5), calls=%async_computation | async-start | bytes 2097152 | tf_op jit(solution)/shard_map/all_to_all | solution.py:479
  27.4 0.0 all-gather.5.cloned.1.call-start
  27.5 0.0 copy-done
  27.5 0.0 copy-start.3
  27.5 0.0 copy-start.4
  27.5 0.0 copy-start.6
  27.6 3.5 %build_taps.1.taps_ref = bf16[8,4096,128]{2,1,0:T(8,128)(2,1)S(1)} custom-call(f32[8,4096]{1,0:T(8,128)S(1)} %constant_dynamic-slice_fusion.filters_ref), custom_call_target="tpu_custom_call" | custom-call | tf_op jit(solution)/shard_map/build_taps/pallas_call | solution.py:327
  31.0 0.0 copy-start.1
  31.0 3.3 %copy-done.1 = bf16[8,4096,128]{2,1,0:T(8,128)(2,1)} copy-done((bf16[8,4096,128]{2,1,0:T(8,128)(2,1)}, bf16[8,4096,128]{2,1,0:T(8,128)(2,1)S(1)}, u32[]{:S(2)}) %copy-start.1) | copy-done | bytes 8388632
  34.3 0.0 copy-done.3
  34.3 0.0 copy-done.4
  34.3 0.1 fusion.3
  34.4 0.0 copy-done.6
  34.4 0.9 pad_maximum_fusion
  35.3 23.0 %all-to-all-done = bf16[32,32,512]{2,1,0:T(8,128)(2,1)S(1)} async-done(((bf16[32,32,512]{2,1,0:T(8,128)(2,1)}), bf16[32,32,512]{2,1,0:T(8,128)(2,1)S(1)}, u32[]{:S(2)}, u32[]{:S(2)}) %all-to-all-start) | async-done | bytes 1048608 | tf_op jit(solution)/shard_map/all_to_all | solution.py:479
  58.3 1.0 copy-done.2
  59.2 0.0 all-gather.5.cloned.1.call-update
  59.2 0.0 copy-start.7
  59.3 11.2 %all-to-all-start.1 = ((bf16[128,2,8,128]{3,2,1,0:T(8,128)(2,1)}), bf16[128,2,8,128]{3,2,1,0:T(8,128)(2,1)S(1)}, u32[]{:S(2)}, u32[]{:S(2)}) async-start(bf16[128,2,8,128]{3,2,1,0:T(8,128)(2,1)} %pad_maximum_fusion), calls=%async_computation.1 | async-start | bytes 1048576 | tf_op jit(solution)/shard_map/all_to_all | solution.py:479
  70.5 0.0 all-gather.9.cloned.1.call-done
  70.5 4.3 %project.1 = (bf16[128,1024]{1,0:T(8,128)(2,1)S(1)}, bf16[128,1024]{1,0:T(8,128)(2,1)S(1)}, bf16[128,1024]{1,0:T(8,128)(2,1)S(1)}, bf16[128,1024]{1,0:T(8,128)(2,1)S(1)}) custom-call(s32[1]{0:T(128)} %bitcast.8.column_ref, bf16[1024,512]{1,0:T(8,128)(2,1)} %bitcast.38, bf16[1024,1024]{1,0:T(8,128)(2,1)} %bitcast.39), custom_call_target="tpu_custom_call" | custom-call | tf_op jit(solution)/shard_map/project/pallas_call | solution.py:362
  74.9 3.1 %collective-permute-start = (bf16[128,1024]{1,0:T(8,128)(2,1)S(1)}, bf16[128,1024]{1,0:T(8,128)(2,1)S(1)}, u32[]{:S(2)}, u32[]{:S(2)}) collective-permute-start(bf16[128,1024]{1,0:T(8,128)(2,1)S(1)} %get-tuple-element.32), channel_id=1, source_target_pairs={{0,32},{32,64},{64,96},{96,0},{1,33},{33,65},{65,97},{97,1},{2,34}... | collective-permute-start | bytes 786440 | tf_op jit(solution)/shard_map/ppermute | solution.py:507
  78.0 4.5 %collective-permute-start.1 = (bf16[128,1024]{1,0:T(8,128)(2,1)S(1)}, bf16[128,1024]{1,0:T(8,128)(2,1)S(1)}, u32[]{:S(2)}, u32[]{:S(2)}) collective-permute-start(bf16[128,1024]{1,0:T(8,128)(2,1)S(1)} %get-tuple-element.33), channel_id=1, source_target_pairs={{0,64},{32,96},{64,0},{96,32},{1,65},{33,97},{65,1},{97,33},{2,66}... | collective-permute-start | bytes 786440 | tf_op jit(solution)/shard_map/ppermute | solution.py:507
  82.5 3.0 %collective-permute-start.2 = (bf16[128,1024]{1,0:T(8,128)(2,1)S(1)}, bf16[128,1024]{1,0:T(8,128)(2,1)S(1)}, u32[]{:S(2)}, u32[]{:S(2)}) collective-permute-start(bf16[128,1024]{1,0:T(8,128)(2,1)S(1)} %get-tuple-element.34), channel_id=1, source_target_pairs={{0,96},{32,0},{64,32},{96,64},{1,97},{33,1},{65,33},{97,65},{2,98}... | collective-permute-start | bytes 786440 | tf_op jit(solution)/shard_map/ppermute | solution.py:507
  85.4 0.0 copy-done.7
  85.4 0.1 dynamic_slice.7.skip_ref
  85.5 5.0 %all-to-all-done.1 = bf16[128,2,8,128]{3,2,1,0:T(8,128)(2,1)S(1)} async-done(((bf16[128,2,8,128]{3,2,1,0:T(8,128)(2,1)}), bf16[128,2,8,128]{3,2,1,0:T(8,128)(2,1)S(1)}, u32[]{:S(2)}, u32[]{:S(2)}) %all-to-all-start.1) | async-done | bytes 524320 | tf_op jit(solution)/shard_map/all_to_all | solution.py:479
  90.5 5.9 %early_dmix.1 = (bf16[1024,128]{1,0:T(8,128)(2,1)S(1)}, bf16[256,512]{1,0:T(8,128)(2,1)S(1)}) custom-call(bf16[8,4096,128]{2,1,0:T(8,128)(2,1)} %copy-done.1, f32[8]{0:T(128)S(1)} %dynamic_slice.7.skip_ref, bf16[2048,128]{1,0:T(8,128)(2,1)S(1)} %bitcast.33), custom_call_target="tpu_custom_call" | custom-call | tf_op jit(solution)/shard_map/early_dmix/pallas_call | solution.py:340
  96.4 0.0 collective-permute-done.part1
  96.5 0.0 collective-permute-done.1.part2
  96.5 0.0 collective-permute-done.2.part3
  96.5 1.0 join.1
  97.4 9.1 %all-to-all-start.2 = ((bf16[32,16,512]{2,1,0:T(8,128)(2,1)}), bf16[32,16,512]{2,1,0:T(8,128)(2,1)S(1)}, u32[]{:S(2)}, u32[]{:S(2)}) async-start(bf16[32,16,512]{2,1,0:T(8,128)(2,1)} %bitcast.10), calls=%async_computation.2 | async-start | bytes 1048576 | tf_op jit(solution)/shard_map/all_to_all | solution.py:479
  106.6 0.0 all-gather.7.cloned.1.call-start
  106.6 10.4 %all-gather.5.cloned.1.call-done.weights_ref = bf16[2048,512]{1,0:T(8,128)(2,1)} async-done(((bf16[1024,512]{1,0:T(8,128)(2,1)}), bf16[2048,512]{1,0:T(8,128)(2,1)}) %all-gather.5.cloned.1.call-update) | async-done | bytes 2097168 | tf_op jit(solution)/shard_map/all_gather | solution.py:510
  117.1 8.1 %all-to-all-done.2 = bf16[32,16,512]{2,1,0:T(8,128)(2,1)S(1)} async-done(((bf16[32,16,512]{2,1,0:T(8,128)(2,1)}), bf16[32,16,512]{2,1,0:T(8,128)(2,1)S(1)}, u32[]{:S(2)}, u32[]{:S(2)}) %all-to-all-start.2) | async-done | bytes 524320 | tf_op jit(solution)/shard_map/all_to_all | solution.py:479
  125.1 0.7 slice_bitcast_fusion.2
  125.8 0.0 all-gather.7.cloned.1.call-update
  125.9 6.7 %late_conv.1 = (bf16[2048,128]{1,0:T(8,128)(2,1)}, bf16[1024,128]{1,0:T(8,128)(2,1)S(1)}) custom-call(bf16[8,4096,128]{2,1,0:T(8,128)(2,1)} %copy-done.1, f32[8]{0:T(128)S(1)} %dynamic_slice.7.skip_ref, bf16[2048,128]{1,0:T(8,128)(2,1)S(1)} %bitcast.34, bf16[512,512]{1,0:T(8,128)(2,1)S(1)} %bitcast.36, bf16[1024,128]{1,0:T(8,128)(2,1)S(1)} %get-tuple-element.37.dmix_ref), custom_call_target="tpu_custom_call" | custom-call | tf_op jit(solution)/shard_map/late_conv/pallas_call | solution.py:432
  132.6 11.5 %all-to-all-start.3 = ((bf16[128,2,8,128]{3,2,1,0:T(8,128)(2,1)}), bf16[128,2,8,128]{3,2,1,0:T(8,128)(2,1)S(1)}, u32[]{:S(2)}, u32[]{:S(2)}) async-start(bf16[128,2,8,128]{3,2,1,0:T(8,128)(2,1)} %bitcast.12), calls=%async_computation.3 | async-start | bytes 1048576 | tf_op jit(solution)/shard_map/all_to_all | solution.py:479
  144.1 5.0 %late_fgrad.1 = bf16[32,1024]{1,0:T(8,128)(2,1)S(1)} custom-call(bf16[2048,128]{1,0:T(8,128)(2,1)S(1)} %bitcast.35, bf16[1024,128]{1,0:T(8,128)(2,1)S(1)} %get-tuple-element.39.mix_ref), custom_call_target="tpu_custom_call" | custom-call | tf_op jit(solution)/shard_map/late_fgrad/pallas_call | solution.py:460
  149.1 3.0 %collective-permute-start.3 = (bf16[32,1024]{1,0:T(8,128)(2,1)S(1)}, bf16[32,1024]{1,0:T(8,128)(2,1)S(1)}, u32[]{:S(2)}, u32[]{:S(2)}) collective-permute-start(bf16[32,1024]{1,0:T(8,128)(2,1)S(1)} %late_fgrad.1), channel_id=1, source_target_pairs={{0,128},{128,0},{256,384},{384,256},{1,129},{129,1},{257,385},{385... | collective-permute-start | bytes 196616 | tf_op jit(solution)/shard_map/ppermute | solution.py:521
  152.1 0.1 pad_add_fusion.place_ref
  152.2 0.8 collective-permute-done.3
  153.0 0.0 copy-start.5
  153.0 1.7 all-gather.7.cloned.1.call-done.dvalue_ref
  154.7 4.5 %back.1 = (bf16[256,1024]{1,0:T(8,128)(2,1)S(1)}, f32[256,1024]{1,0:T(8,128)S(1)}) custom-call(s32[3]{0:T(128)S(1)} %pad_add_fusion.place_ref, bf16[1024,512]{1,0:T(8,128)(2,1)} %all-gather.7.cloned.1.call-done.dvalue_ref, bf16[2048,512]{1,0:T(8,128)(2,1)} %all-gather.5.cloned.1.call-done.weights_ref), custom_call_target="tpu_custom_call" | custom-call | tf_op jit(solution)/shard_map/back/pallas_call | solution.py:388
  159.2 3.5 %collective-permute-start.4 = (bf16[256,1024]{1,0:T(8,128)(2,1)S(1)}, bf16[256,1024]{1,0:T(8,128)(2,1)S(1)}, u32[]{:S(2)}, u32[]{:S(2)}) collective-permute-start(bf16[256,1024]{1,0:T(8,128)(2,1)S(1)} %get-tuple-element.43), channel_id=1, source_target_pairs={{0,128},{128,0},{256,384},{384,256},{1,129},{129,1},{257,385},{385... | collective-permute-start | bytes 1572872 | tf_op jit(solution)/shard_map/ppermute | solution.py:521
  162.7 3.1 %collective-permute-start.6 = (bf16[64,1024]{1,0:T(8,128)(2,1)S(1)}, bf16[64,1024]{1,0:T(8,128)(2,1)S(1)}, u32[]{:S(2)}, u32[]{:S(2)}) collective-permute-start(bf16[64,1024]{1,0:T(8,128)(2,1)S(1)} %pad_maximum_fusion.1.near_ref), channel_id=1, source_target_pairs={{0,256},{128,384},{256,0},{384,128},{1,257},{129,385},{257,1},{385... | collective-permute-start | bytes 393224 | tf_op jit(solution)/shard_map/ppermute | solution.py:521
  165.8 0.0 collective-permute-done.4.received_ref
  165.8 0.6 middle.1
  166.5 2.2 %collective-permute-start.5 = (bf16[128,1024]{1,0:T(8,128)(2,1)S(1)}, bf16[128,1024]{1,0:T(8,128)(2,1)S(1)}, u32[]{:S(2)}, u32[]{:S(2)}) collective-permute-start(bf16[128,1024]{1,0:T(8,128)(2,1)S(1)} %get-tuple-element.45), channel_id=1, source_target_pairs={{0,256},{128,384},{256,0},{384,128},{1,257},{129,385},{257,1},{385... | collective-permute-start | bytes 786440 | tf_op jit(solution)/shard_map/ppermute | solution.py:521
  168.6 0.0 all-to-all-done.3
  168.7 0.0 copy-done.5
  168.7 0.9 fusion.2
  169.6 0.7 slice_bitcast_fusion
  170.3 0.0 collective-permute-done.6.far_ref
  170.3 5.7 %collective-permute-done.5.received_ref = bf16[128,1024]{1,0:T(8,128)(2,1)S(1)} collective-permute-done((bf16[128,1024]{1,0:T(8,128)(2,1)S(1)}, bf16[128,1024]{1,0:T(8,128)(2,1)S(1)}, u32[]{:S(2)}, u32[]{:S(2)}) %collective-permute-start.5) | collective-permute-done | bytes 262176 | tf_op jit(solution)/shard_map/ppermute | solution.py:521
  176.0 1.5 last.1
  177.5 0.5 slice_bitcast_fusion.3
  (3 shorter events, 0.0 us)
Async XLA Ops:
  7.2 20.3 %copy-start = (f32[32,4096]{1,0:T(8,128)S(1)}, f32[32,4096]{1,0:T(8,128)}, u32[]{:S(2)}) copy-start(f32[32,4096]{1,0:T(8,128)} %param.11) | copy-start | bytes 1572868
  7.2 63.3 %all-gather.9.cloned.1.call-start = ((), (), s32[]{:S(2)}) async-start(), calls=%async_computation.6 | async-start | bytes 2359296 | tf_op jit(solution)/shard_map/all_gather | solution.py:489
  10.9 47.3 %all-to-all-start = ((bf16[32,32,512]{2,1,0:T(8,128)(2,1)}), bf16[32,32,512]{2,1,0:T(8,128)(2,1)S(1)}, u32[]{:S(2)}, u32[]{:S(2)}) async-start(bf16[32,32,512]{2,1,0:T(8,128)(2,1)} %bitcast.5), calls=%async_computation | async-start | bytes 2097152 | tf_op jit(solution)/shard_map/all_to_all | solution.py:479
  27.4 89.6 %all-gather.5.cloned.1.call-start = ((), (), s32[]{:S(2)}) async-start(), calls=%async_computation.4 | async-start | bytes 3145728 | tf_op jit(solution)/shard_map/all_gather | solution.py:510
  27.5 6.8 %copy-start.3 = (bf16[1,1024,128]{2,1,0:T(8,128)(2,1)S(1)}, bf16[1,1024,128]{2,1,0:T(8,128)(2,1)}, u32[]{:S(2)}) copy-start(bf16[1,1024,128]{2,1,0:T(8,128)(2,1)} %param.13) | copy-start | bytes 786436
  27.5 6.8 %copy-start.4 = (bf16[1,1024,128]{2,1,0:T(8,128)(2,1)S(1)}, bf16[1,1024,128]{2,1,0:T(8,128)(2,1)}, u32[]{:S(2)}) copy-start(bf16[1,1024,128]{2,1,0:T(8,128)(2,1)} %param.9) | copy-start | bytes 786436
  27.5 6.8 %copy-start.6 = (bf16[1,1024,128]{2,1,0:T(8,128)(2,1)S(1)}, bf16[1,1024,128]{2,1,0:T(8,128)(2,1)}, u32[]{:S(2)}) copy-start(bf16[1,1024,128]{2,1,0:T(8,128)(2,1)} %param.10) | copy-start | bytes 786436
  31.0 3.3 %copy-start.1 = (bf16[8,4096,128]{2,1,0:T(8,128)(2,1)}, bf16[8,4096,128]{2,1,0:T(8,128)(2,1)S(1)}, u32[]{:S(2)}) copy-start(bf16[8,4096,128]{2,1,0:T(8,128)(2,1)S(1)} %build_taps.1.taps_ref) | copy-start | bytes 25165828
  58.2 1.0 copy-start.2
  59.2 26.2 %copy-start.7 = (f32[32]{0:T(128)S(1)}, f32[32]{0:T(128)}, u32[]{:S(2)}) copy-start(f32[32]{0:T(128)} %param.12) | copy-start | bytes 388
  59.3 31.3 %all-to-all-start.1 = ((bf16[128,2,8,128]{3,2,1,0:T(8,128)(2,1)}), bf16[128,2,8,128]{3,2,1,0:T(8,128)(2,1)S(1)}, u32[]{:S(2)}, u32[]{:S(2)}) async-start(bf16[128,2,8,128]{3,2,1,0:T(8,128)(2,1)} %pad_maximum_fusion), calls=%async_computation.1 | async-start | bytes 1048576 | tf_op jit(solution)/shard_map/all_to_all | solution.py:479
  74.9 21.6 %collective-permute-start = (bf16[128,1024]{1,0:T(8,128)(2,1)S(1)}, bf16[128,1024]{1,0:T(8,128)(2,1)S(1)}, u32[]{:S(2)}, u32[]{:S(2)}) collective-permute-start(bf16[128,1024]{1,0:T(8,128)(2,1)S(1)} %get-tuple-element.32), channel_id=1, source_target_pairs={{0,32},{32,64},{64,96},{96,0},{1,33},{33,65},{65,97},{97,1},{2,34}... | collective-permute-start | bytes 786440 | tf_op jit(solution)/shard_map/ppermute | solution.py:507
  78.0 18.5 %collective-permute-start.1 = (bf16[128,1024]{1,0:T(8,128)(2,1)S(1)}, bf16[128,1024]{1,0:T(8,128)(2,1)S(1)}, u32[]{:S(2)}, u32[]{:S(2)}) collective-permute-start(bf16[128,1024]{1,0:T(8,128)(2,1)S(1)} %get-tuple-element.33), channel_id=1, source_target_pairs={{0,64},{32,96},{64,0},{96,32},{1,65},{33,97},{65,1},{97,33},{2,66}... | collective-permute-start | bytes 786440 | tf_op jit(solution)/shard_map/ppermute | solution.py:507
  82.5 14.0 %collective-permute-start.2 = (bf16[128,1024]{1,0:T(8,128)(2,1)S(1)}, bf16[128,1024]{1,0:T(8,128)(2,1)S(1)}, u32[]{:S(2)}, u32[]{:S(2)}) collective-permute-start(bf16[128,1024]{1,0:T(8,128)(2,1)S(1)} %get-tuple-element.34), channel_id=1, source_target_pairs={{0,96},{32,0},{64,32},{96,64},{1,97},{33,1},{65,33},{97,65},{2,98}... | collective-permute-start | bytes 786440 | tf_op jit(solution)/shard_map/ppermute | solution.py:507
  97.4 27.7 %all-to-all-start.2 = ((bf16[32,16,512]{2,1,0:T(8,128)(2,1)}), bf16[32,16,512]{2,1,0:T(8,128)(2,1)S(1)}, u32[]{:S(2)}, u32[]{:S(2)}) async-start(bf16[32,16,512]{2,1,0:T(8,128)(2,1)} %bitcast.10), calls=%async_computation.2 | async-start | bytes 1048576 | tf_op jit(solution)/shard_map/all_to_all | solution.py:479
  106.6 48.2 %all-gather.7.cloned.1.call-start = ((), (), s32[]{:S(2)}) async-start(), calls=%async_computation.5 | async-start | bytes 1310720 | tf_op jit(solution)/shard_map/all_gather | solution.py:515
  132.6 36.1 %all-to-all-start.3 = ((bf16[128,2,8,128]{3,2,1,0:T(8,128)(2,1)}), bf16[128,2,8,128]{3,2,1,0:T(8,128)(2,1)S(1)}, u32[]{:S(2)}, u32[]{:S(2)}) async-start(bf16[128,2,8,128]{3,2,1,0:T(8,128)(2,1)} %bitcast.12), calls=%async_computation.3 | async-start | bytes 1048576 | tf_op jit(solution)/shard_map/all_to_all | solution.py:479
  149.1 3.9 %collective-permute-start.3 = (bf16[32,1024]{1,0:T(8,128)(2,1)S(1)}, bf16[32,1024]{1,0:T(8,128)(2,1)S(1)}, u32[]{:S(2)}, u32[]{:S(2)}) collective-permute-start(bf16[32,1024]{1,0:T(8,128)(2,1)S(1)} %late_fgrad.1), channel_id=1, source_target_pairs={{0,128},{128,0},{256,384},{384,256},{1,129},{129,1},{257,385},{385... | collective-permute-start | bytes 196616 | tf_op jit(solution)/shard_map/ppermute | solution.py:521
  153.0 15.7 %copy-start.5 = (bf16[1,1024,128]{2,1,0:T(8,128)(2,1)S(1)}, bf16[1,1024,128]{2,1,0:T(8,128)(2,1)}, u32[]{:S(2)}) copy-start(bf16[1,1024,128]{2,1,0:T(8,128)(2,1)} %param.9) | copy-start | bytes 786436
  159.2 6.6 %collective-permute-start.4 = (bf16[256,1024]{1,0:T(8,128)(2,1)S(1)}, bf16[256,1024]{1,0:T(8,128)(2,1)S(1)}, u32[]{:S(2)}, u32[]{:S(2)}) collective-permute-start(bf16[256,1024]{1,0:T(8,128)(2,1)S(1)} %get-tuple-element.43), channel_id=1, source_target_pairs={{0,128},{128,0},{256,384},{384,256},{1,129},{129,1},{257,385},{385... | collective-permute-start | bytes 1572872 | tf_op jit(solution)/shard_map/ppermute | solution.py:521
  162.7 7.6 %collective-permute-start.6 = (bf16[64,1024]{1,0:T(8,128)(2,1)S(1)}, bf16[64,1024]{1,0:T(8,128)(2,1)S(1)}, u32[]{:S(2)}, u32[]{:S(2)}) collective-permute-start(bf16[64,1024]{1,0:T(8,128)(2,1)S(1)} %pad_maximum_fusion.1.near_ref), channel_id=1, source_target_pairs={{0,256},{128,384},{256,0},{384,128},{1,257},{129,385},{257,1},{385... | collective-permute-start | bytes 393224 | tf_op jit(solution)/shard_map/ppermute | solution.py:521
  166.5 9.5 %collective-permute-start.5 = (bf16[128,1024]{1,0:T(8,128)(2,1)S(1)}, bf16[128,1024]{1,0:T(8,128)(2,1)S(1)}, u32[]{:S(2)}, u32[]{:S(2)}) collective-permute-start(bf16[128,1024]{1,0:T(8,128)(2,1)S(1)} %get-tuple-element.45), channel_id=1, source_target_pairs={{0,256},{128,384},{256,0},{384,128},{1,257},{129,385},{257,1},{385... | collective-permute-start | bytes 786440 | tf_op jit(solution)/shard_map/ppermute | solution.py:521
Sparse Core Ops, SparseCore 0:
  10.1 57.2 all-gather.8
  69.5 47.4 all-gather.4
  126.0 28.6 all-gather.6

commit v5 on v4

--- a/solution.py
+++ b/solution.py
@@ -159,7 +159,7 @@
             out_ref[index * HALF : (index + 1) * HALF, :] = tile.astype(bf16)
 
 
-def back_kernel(place_ref, dvalue_ref, weights_ref, sent_ref, kept_ref, total):
+def back_kernel(place_ref, dvalue_ref, own_ref, other_ref, sent_ref, kept_ref, total):
     index = pl.program_id(0)
     dvalue = dvalue_ref[...].astype(f32)
     tiles = [[], []]
@@ -168,8 +168,10 @@
         pair = halves_of(dvalue[start : start + GROUP, :], dvalue[start + GROUP : start + HALF, :])
         for half in range(2):
             tiles[half].append(pair[half])
-    rows = jnp.concatenate([jnp.concatenate(part, axis=0).astype(bf16) for part in tiles], axis=0)
-    columns = jnp.concatenate([weights_ref[0:SPAN, :], weights_ref[SPAN:, :]], axis=1)
+    upper, lower = [jnp.concatenate(part, axis=0).astype(bf16) for part in tiles]
+    first = place_ref[0] == 0
+    rows = jnp.concatenate([jnp.where(first, upper, lower), jnp.where(first, lower, upper)], axis=0)
+    columns = jnp.concatenate([own_ref[...], other_ref[...]], axis=1)
     term = lax.dot_general(rows, columns, (((0,), (1,)), ((), ())), preferred_element_type=f32)
 
     @pl.when(index == 0)
@@ -384,14 +386,15 @@
     )(*parts, dvalue)
 
 
-def back(place, dvalue, weights):
+def back(place, dvalue, own, other):
     return pl.pallas_call(
         back_kernel,
         grid=(4,),
         in_specs=[
             smem,
             pl.BlockSpec((BLOCKS * GROUP, SEQS * LANES), lambda step: (step, 0)),
-            pl.BlockSpec((2 * SPAN, LANES), lambda step: (0, step)),
+            pl.BlockSpec((SPAN, LANES), lambda step: (0, step)),
+            pl.BlockSpec((SPAN, LANES), lambda step: (0, step)),
         ],
         out_specs=[whole((2 * LANES, SPAN)), whole((2 * LANES, SPAN))],
         out_shape=[
@@ -401,7 +404,7 @@
         scratch_shapes=[pltpu.VMEM((SEQS * LANES, SPAN), f32)],
         compiler_params=params,
         name="back",
-    )(place, *[pltpu.with_memory_space_constraint(x, pltpu.HBM) for x in (dvalue, weights)])
+    )(place, *[pltpu.with_memory_space_constraint(x, pltpu.HBM) for x in (dvalue, own, other)])
 
 
 def middle(place, kept, received):
@@ -506,12 +509,11 @@
     parts = [parts[0]] + [
         lax.ppermute(parts[step], "tensor", [(i, (i + step) % 4) for i in range(4)]) for step in (1, 2, 3)
     ]
-    sides = [[2 * k, 2 * k + 1] for k in range(BLOCKS // 2)]
-    weights = lax.all_gather(weight, "context", axis=0, tiled=True, axis_index_groups=sides)
+    other = lax.ppermute(weight, "context", [(k, k ^ 1) for k in range(BLOCKS)])
     dmix, dvalue = early_dmix(taps, own_skip, pair)
 
     both = swap(join(parts, dvalue).reshape(BLOCKS, HALF, SEQS * LANES), "context")
-    both, weights = lax.optimization_barrier((both, weights))
+    both, other = lax.optimization_barrier((both, other))
     dvalue = lax.all_gather(both[:, GROUP:].reshape(BLOCKS * GROUP, SEQS * LANES), "tensor", axis=0, tiled=True)
     out, mix = late_conv(taps, own_skip, pair, both.reshape(BLOCKS * HALF, SEQS * LANES), dmix)
     out = swap(out.reshape(ROWS, 2, GROUP, LANES), ("context", "dp"))
@@ -524,7 +526,7 @@
     chip_fgrads = jnp.concatenate([fgrad, cross(fgrad, 1)], axis=0)
     far_fgrads = cross(chip_fgrads, 2)
     dvalue, chip_fgrads = lax.optimization_barrier((dvalue, chip_fgrads))
-    sent, kept = back(place, dvalue, weights)
+    sent, kept = back(place, dvalue, weight, other)
     sent, rest = middle(place, kept, cross(sent, 1))
     input_grad, filter_grad, skip_grad = last(place, rest, cross(sent, 2), chip_fgrads, far_fgrads)
     skip_grad = skip_grad[0, : skip.shape[0]]

time: 185 us -> 182 us (0.984)
  waiting for transfers between devices: 55.4 us -> 50 us
  starting transfers between devices: 70.8 us -> 73.9 us
    all_gather x1 -> x0, waiting for transfers between devices: 10.4 us -> none  [per_device(): lax.all_gather(weight, 'context', axis=0, tiled=True, axis_index_groups=s...]
    ppermute x0 -> x1, waiting for transfers between devices: none -> 4.05 us  [per_device(): other = lax.ppermute(weight, 'context', [(k, k ^ 1) for k in range(BLOCKS)])]
    all_to_all x4, waiting for transfers between devices: 36.1 us -> 39.4 us  [swap(): lax.all_to_all(values, axes, split_axis=0, concat_axis=0, tiled=True, axi...]
    ppermute x0 -> x1, starting transfers between devices: none -> 3.31 us  [per_device(): other = lax.ppermute(weight, 'context', [(k, k ^ 1) for k in range(BLOCKS)])]
  transfers between devices with their start and end apart: 14 -> 14, of which waited for: 7 -> 6; matrix products, arithmetic and copies ran while one was open for 2% -> 2% of each run, Pallas kernels for 19% -> 19%
where the time goes in v5:
time: 182 us
  starting transfers between devices  73.9 us (41%)
  waiting for transfers between devices  50 us (27%)
  Pallas kernels  36 us (20%)
  between operations  14.4 us (8%)
  local copies, waits for them, and re-layouts  5.36 us (3%)
  other arithmetic  1.95 us (1%)
    all_to_all x4, starting transfers between devices, swap(): lax.all_to_all(values, axes, split_axis=0, concat_axis=0, tiled=True, axi...  49.4 us
    all_to_all x4, waiting for transfers between devices, swap(): lax.all_to_all(values, axes, split_axis=0, concat_axis=0, tiled=True, axi...  39.4 us
    ppermute x3, starting transfers between devices, per_device(): lax.ppermute(parts[step], 'tensor', [(i, (i + step) % 4) for i in range(4)])  10.6 us
    ppermute x4, starting transfers between devices, cross(): return lax.ppermute(values, 'dp', [(i, i ^ bit) for i in range(SEQS)])  10.5 us
    pallas_call x1, Pallas kernels, late_conv(): pl.pallas_call(conv_kernel, grid=(GROUP // CONV,), in_specs=[any_spec, sm...  6.69 us
    pallas_call x1, Pallas kernels, early_dmix(): pl.pallas_call(dmix_kernel, grid=(GROUP // DMIX,), in_specs=[any_spec, sm...  5.92 us
    ppermute x4, waiting for transfers between devices, cross(): return lax.ppermute(values, 'dp', [(i, i ^ bit) for i in range(SEQS)])  5.79 us
    pallas_call x1, Pallas kernels, late_fgrad(): pl.pallas_call(fgrad_kernel, grid=(GROUP // FGRAD,), in_specs=[pair_spec,...  5.01 us
  transfers between devices with their start and end apart: 14, of which 6 were waited for; matrix products, arithmetic and copies ran while one was open for 2% of the time, Pallas kernels for 19%

profile of v5, /device:TPU:1, one launch (start us, length us, event | category | flops | bytes accessed | tf_op | source)
XLA Modules:
  0.0 181.6 jit_solution(3360912765476404004)
XLA Ops:
  7.2 0.0 copy-start
  7.2 0.0 copy-start.3
  7.2 0.0 copy-start.4
  7.2 0.0 copy-start.6
  7.2 0.0 all-gather.6.cloned.1.call-start
  7.3 0.7 all-gather.6.cloned.1.call-update
  8.0 3.0 %pack.1 = bf16[1024,512]{1,0:T(8,128)(2,1)} custom-call(s32[1]{0:T(128)} %bitcast.4.quarter_ref, bf16[32,4096]{1,0:T(8,128)(2,1)} %weight_ref.1), custom_call_target="tpu_custom_call" | custom-call | tf_op jit(solution)/shard_map/pack/pallas_call | solution.py:316
  11.0 0.0 copy-start.7
  11.0 16.6 %all-to-all-start = ((bf16[32,32,512]{2,1,0:T(8,128)(2,1)}), bf16[32,32,512]{2,1,0:T(8,128)(2,1)S(1)}, u32[]{:S(2)}, u32[]{:S(2)}) async-start(bf16[32,32,512]{2,1,0:T(8,128)(2,1)} %bitcast.5), calls=%async_computation | async-start | bytes 2097152 | tf_op jit(solution)/shard_map/all_to_all | solution.py:482
  27.6 0.0 copy-done
  27.6 3.5 %build_taps.1.taps_ref = bf16[8,4096,128]{2,1,0:T(8,128)(2,1)S(1)} custom-call(f32[8,4096]{1,0:T(8,128)S(1)} %constant_dynamic-slice_fusion.filters_ref), custom_call_target="tpu_custom_call" | custom-call | tf_op jit(solution)/shard_map/build_taps/pallas_call | solution.py:329
  31.1 0.0 copy-start.1
  31.1 3.3 %copy-done.1 = bf16[8,4096,128]{2,1,0:T(8,128)(2,1)} copy-done((bf16[8,4096,128]{2,1,0:T(8,128)(2,1)}, bf16[8,4096,128]{2,1,0:T(8,128)(2,1)S(1)}, u32[]{:S(2)}) %copy-start.1) | copy-done | bytes 8388632
  34.4 0.0 copy-done.3
  34.4 0.0 copy-done.4
  34.4 0.1 fusion.3
  34.5 0.0 copy-done.6
  34.5 0.9 pad_maximum_fusion
  35.4 23.1 %all-to-all-done = bf16[32,32,512]{2,1,0:T(8,128)(2,1)S(1)} async-done(((bf16[32,32,512]{2,1,0:T(8,128)(2,1)}), bf16[32,32,512]{2,1,0:T(8,128)(2,1)S(1)}, u32[]{:S(2)}, u32[]{:S(2)}) %all-to-all-start) | async-done | bytes 1048608 | tf_op jit(solution)/shard_map/all_to_all | solution.py:482
  58.4 0.0 copy-start.2
  58.4 11.2 %all-to-all-start.1 = ((bf16[128,2,8,128]{3,2,1,0:T(8,128)(2,1)}), bf16[128,2,8,128]{3,2,1,0:T(8,128)(2,1)S(1)}, u32[]{:S(2)}, u32[]{:S(2)}) async-start(bf16[128,2,8,128]{3,2,1,0:T(8,128)(2,1)} %pad_maximum_fusion), calls=%async_computation.1 | async-start | bytes 1048576 | tf_op jit(solution)/shard_map/all_to_all | solution.py:482
  69.6 0.0 all-gather.6.cloned.1.call-done
  69.7 0.0 copy-done.2
  69.7 4.3 %project.1 = (bf16[128,1024]{1,0:T(8,128)(2,1)S(1)}, bf16[128,1024]{1,0:T(8,128)(2,1)S(1)}, bf16[128,1024]{1,0:T(8,128)(2,1)S(1)}, bf16[128,1024]{1,0:T(8,128)(2,1)S(1)}) custom-call(s32[1]{0:T(128)} %bitcast.8.column_ref, bf16[1024,512]{1,0:T(8,128)(2,1)} %bitcast.37, bf16[1024,1024]{1,0:T(8,128)(2,1)} %bitcast.40), custom_call_target="tpu_custom_call" | custom-call | tf_op jit(solution)/shard_map/project/pallas_call | solution.py:364
  74.0 3.1 %collective-permute-start = (bf16[128,1024]{1,0:T(8,128)(2,1)S(1)}, bf16[128,1024]{1,0:T(8,128)(2,1)S(1)}, u32[]{:S(2)}, u32[]{:S(2)}) collective-permute-start(bf16[128,1024]{1,0:T(8,128)(2,1)S(1)} %get-tuple-element.32), channel_id=1, source_target_pairs={{0,32},{32,64},{64,96},{96,0},{1,33},{33,65},{65,97},{97,1},{2,34}... | collective-permute-start | bytes 786440 | tf_op jit(solution)/shard_map/ppermute | solution.py:510
  77.2 4.4 %collective-permute-start.1 = (bf16[128,1024]{1,0:T(8,128)(2,1)S(1)}, bf16[128,1024]{1,0:T(8,128)(2,1)S(1)}, u32[]{:S(2)}, u32[]{:S(2)}) collective-permute-start(bf16[128,1024]{1,0:T(8,128)(2,1)S(1)} %get-tuple-element.33), channel_id=1, source_target_pairs={{0,64},{32,96},{64,0},{96,32},{1,65},{33,97},{65,1},{97,33},{2,66}... | collective-permute-start | bytes 786440 | tf_op jit(solution)/shard_map/ppermute | solution.py:510
  81.6 3.1 %collective-permute-start.2 = (bf16[128,1024]{1,0:T(8,128)(2,1)S(1)}, bf16[128,1024]{1,0:T(8,128)(2,1)S(1)}, u32[]{:S(2)}, u32[]{:S(2)}) collective-permute-start(bf16[128,1024]{1,0:T(8,128)(2,1)S(1)} %get-tuple-element.34), channel_id=1, source_target_pairs={{0,96},{32,0},{64,32},{96,64},{1,97},{33,1},{65,33},{97,65},{2,98}... | collective-permute-start | bytes 786440 | tf_op jit(solution)/shard_map/ppermute | solution.py:510
  84.6 3.3 %collective-permute-start.3 = (bf16[1024,512]{1,0:T(8,128)(2,1)}, bf16[1024,512]{1,0:T(8,128)(2,1)}, u32[]{:S(2)}, u32[]{:S(2)}) collective-permute-start(bf16[1024,512]{1,0:T(8,128)(2,1)} %bitcast.38), channel_id=1, source_target_pairs={{0,1},{1,0},{2,3},{3,2},{4,5},{5,4},{6,7},{7,6},{8,9},{9,8},{10,11... | collective-permute-start | bytes 3145736 | tf_op jit(solution)/shard_map/ppermute | solution.py:512
  87.9 0.0 copy-done.7
  87.9 0.1 dynamic_slice.7.skip_ref
  88.0 1.7 all-to-all-done.1
  89.7 5.9 %early_dmix.1 = (bf16[1024,128]{1,0:T(8,128)(2,1)S(1)}, bf16[256,512]{1,0:T(8,128)(2,1)S(1)}) custom-call(bf16[8,4096,128]{2,1,0:T(8,128)(2,1)} %copy-done.1, f32[8]{0:T(128)S(1)} %dynamic_slice.7.skip_ref, bf16[2048,128]{1,0:T(8,128)(2,1)S(1)} %bitcast.33), custom_call_target="tpu_custom_call" | custom-call | tf_op jit(solution)/shard_map/early_dmix/pallas_call | solution.py:342
  95.6 0.0 collective-permute-done.part1
  95.6 0.0 collective-permute-done.1.part2
  95.6 0.0 collective-permute-done.2.part3
  95.6 1.0 join.1
  96.6 9.5 %all-to-all-start.2 = ((bf16[32,16,512]{2,1,0:T(8,128)(2,1)}), bf16[32,16,512]{2,1,0:T(8,128)(2,1)S(1)}, u32[]{:S(2)}, u32[]{:S(2)}) async-start(bf16[32,16,512]{2,1,0:T(8,128)(2,1)} %bitcast.10), calls=%async_computation.2 | async-start | bytes 1048576 | tf_op jit(solution)/shard_map/all_to_all | solution.py:482
  106.1 0.0 all-gather.4.cloned.1.call-start
  106.1 4.1 %collective-permute-done.3.other_ref = bf16[1024,512]{1,0:T(8,128)(2,1)} collective-permute-done((bf16[1024,512]{1,0:T(8,128)(2,1)}, bf16[1024,512]{1,0:T(8,128)(2,1)}, u32[]{:S(2)}, u32[]{:S(2)}) %collective-permute-start.3) | collective-permute-done | bytes 1048608 | tf_op jit(solution)/shard_map/ppermute | solution.py:512
  110.2 14.7 %all-to-all-done.2 = bf16[32,16,512]{2,1,0:T(8,128)(2,1)S(1)} async-done(((bf16[32,16,512]{2,1,0:T(8,128)(2,1)}), bf16[32,16,512]{2,1,0:T(8,128)(2,1)S(1)}, u32[]{:S(2)}, u32[]{:S(2)}) %all-to-all-start.2) | async-done | bytes 524320 | tf_op jit(solution)/shard_map/all_to_all | solution.py:482
  124.9 0.7 slice_bitcast_fusion.2
  125.6 0.0 all-gather.4.cloned.1.call-update
  125.6 0.0 copy-start.5
  125.6 6.7 %late_conv.1 = (bf16[2048,128]{1,0:T(8,128)(2,1)}, bf16[1024,128]{1,0:T(8,128)(2,1)S(1)}) custom-call(bf16[8,4096,128]{2,1,0:T(8,128)(2,1)} %copy-done.1, f32[8]{0:T(128)S(1)} %dynamic_slice.7.skip_ref, bf16[2048,128]{1,0:T(8,128)(2,1)S(1)} %bitcast.34, bf16[512,512]{1,0:T(8,128)(2,1)S(1)} %bitcast.36, bf16[1024,128]{1,0:T(8,128)(2,1)S(1)} %get-tuple-element.37.dmix_ref), custom_call_target="tpu_custom_call" | custom-call | tf_op jit(solution)/shard_map/late_conv/pallas_call | solution.py:435
  132.3 12.1 %all-to-all-start.3 = ((bf16[128,2,8,128]{3,2,1,0:T(8,128)(2,1)}), bf16[128,2,8,128]{3,2,1,0:T(8,128)(2,1)S(1)}, u32[]{:S(2)}, u32[]{:S(2)}) async-start(bf16[128,2,8,128]{3,2,1,0:T(8,128)(2,1)} %bitcast.12), calls=%async_computation.3 | async-start | bytes 1048576 | tf_op jit(solution)/shard_map/all_to_all | solution.py:482
  144.5 5.0 %late_fgrad.1 = bf16[32,1024]{1,0:T(8,128)(2,1)S(1)} custom-call(bf16[2048,128]{1,0:T(8,128)(2,1)S(1)} %bitcast.35, bf16[1024,128]{1,0:T(8,128)(2,1)S(1)} %get-tuple-element.39.mix_ref), custom_call_target="tpu_custom_call" | custom-call | tf_op jit(solution)/shard_map/late_fgrad/pallas_call | solution.py:463
  149.5 3.0 %collective-permute-start.4 = (bf16[32,1024]{1,0:T(8,128)(2,1)S(1)}, bf16[32,1024]{1,0:T(8,128)(2,1)S(1)}, u32[]{:S(2)}, u32[]{:S(2)}) collective-permute-start(bf16[32,1024]{1,0:T(8,128)(2,1)S(1)} %late_fgrad.1), channel_id=1, source_target_pairs={{0,128},{128,0},{256,384},{384,256},{1,129},{129,1},{257,385},{385... | collective-permute-start | bytes 196616 | tf_op jit(solution)/shard_map/ppermute | solution.py:523
  152.5 0.1 pad_add_fusion.place_ref
  152.5 0.8 collective-permute-done.4
  153.4 0.0 all-gather.4.cloned.1.call-done.dvalue_ref
  153.4 4.5 %back.1 = (bf16[256,1024]{1,0:T(8,128)(2,1)S(1)}, f32[256,1024]{1,0:T(8,128)S(1)}) custom-call(s32[3]{0:T(128)S(1)} %pad_add_fusion.place_ref, bf16[1024,512]{1,0:T(8,128)(2,1)} %all-gather.4.cloned.1.call-done.dvalue_ref, bf16[1024,512]{1,0:T(8,128)(2,1)} %bitcast.39, bf16[1024,512]{1,0:T(8,128)(2,1)} %collective-permute-done.3.other_ref), custom_call_target="tpu_custom_call" | custom-call | tf_op jit(solution)/shard_map/back/pallas_call | solution.py:390
  157.8 2.3 %collective-permute-start.5 = (bf16[256,1024]{1,0:T(8,128)(2,1)S(1)}, bf16[256,1024]{1,0:T(8,128)(2,1)S(1)}, u32[]{:S(2)}, u32[]{:S(2)}) collective-permute-start(bf16[256,1024]{1,0:T(8,128)(2,1)S(1)} %get-tuple-element.43), channel_id=1, source_target_pairs={{0,128},{128,0},{256,384},{384,256},{1,129},{129,1},{257,385},{385... | collective-permute-start | bytes 1572872 | tf_op jit(solution)/shard_map/ppermute | solution.py:523
  160.1 2.6 %collective-permute-start.7 = (bf16[64,1024]{1,0:T(8,128)(2,1)S(1)}, bf16[64,1024]{1,0:T(8,128)(2,1)S(1)}, u32[]{:S(2)}, u32[]{:S(2)}) collective-permute-start(bf16[64,1024]{1,0:T(8,128)(2,1)S(1)} %pad_maximum_fusion.1.near_ref), channel_id=1, source_target_pairs={{0,256},{128,384},{256,0},{384,128},{1,257},{129,385},{257,1},{385... | collective-permute-start | bytes 393224 | tf_op jit(solution)/shard_map/ppermute | solution.py:523
  162.7 0.0 collective-permute-done.5.received_ref
  162.7 0.6 middle.1
  163.4 2.7 %collective-permute-start.6 = (bf16[128,1024]{1,0:T(8,128)(2,1)S(1)}, bf16[128,1024]{1,0:T(8,128)(2,1)S(1)}, u32[]{:S(2)}, u32[]{:S(2)}) collective-permute-start(bf16[128,1024]{1,0:T(8,128)(2,1)S(1)} %get-tuple-element.45), channel_id=1, source_target_pairs={{0,256},{128,384},{256,0},{384,128},{1,257},{129,385},{257,1},{385... | collective-permute-start | bytes 786440 | tf_op jit(solution)/shard_map/ppermute | solution.py:523
  166.1 0.0 all-to-all-done.3
  166.1 0.0 copy-done.5
  166.1 0.9 fusion.2
  167.0 0.7 slice_bitcast_fusion
  167.7 0.0 collective-permute-done.7.far_ref
  167.7 5.0 %collective-permute-done.6.received_ref = bf16[128,1024]{1,0:T(8,128)(2,1)S(1)} collective-permute-done((bf16[128,1024]{1,0:T(8,128)(2,1)S(1)}, bf16[128,1024]{1,0:T(8,128)(2,1)S(1)}, u32[]{:S(2)}, u32[]{:S(2)}) %collective-permute-start.6) | collective-permute-done | bytes 262176 | tf_op jit(solution)/shard_map/ppermute | solution.py:523
  172.7 1.5 last.1
  174.3 0.5 slice_bitcast_fusion.3
  (2 shorter events, 0.0 us)
Async XLA Ops:
  7.2 20.4 %copy-start = (f32[32,4096]{1,0:T(8,128)S(1)}, f32[32,4096]{1,0:T(8,128)}, u32[]{:S(2)}) copy-start(f32[32,4096]{1,0:T(8,128)} %param.11) | copy-start | bytes 1572868
  7.2 27.2 %copy-start.3 = (bf16[1,1024,128]{2,1,0:T(8,128)(2,1)S(1)}, bf16[1,1024,128]{2,1,0:T(8,128)(2,1)}, u32[]{:S(2)}) copy-start(bf16[1,1024,128]{2,1,0:T(8,128)(2,1)} %param.13) | copy-start | bytes 786436
  7.2 27.2 %copy-start.4 = (bf16[1,1024,128]{2,1,0:T(8,128)(2,1)S(1)}, bf16[1,1024,128]{2,1,0:T(8,128)(2,1)}, u32[]{:S(2)}) copy-start(bf16[1,1024,128]{2,1,0:T(8,128)(2,1)} %param.9) | copy-start | bytes 786436
  7.2 27.3 %copy-start.6 = (bf16[1,1024,128]{2,1,0:T(8,128)(2,1)S(1)}, bf16[1,1024,128]{2,1,0:T(8,128)(2,1)}, u32[]{:S(2)}) copy-start(bf16[1,1024,128]{2,1,0:T(8,128)(2,1)} %param.10) | copy-start | bytes 786436
  7.2 62.4 %all-gather.6.cloned.1.call-start = ((), (), s32[]{:S(2)}) async-start(), calls=%async_computation.5 | async-start | bytes 2359296 | tf_op jit(solution)/shard_map/all_gather | solution.py:492
  11.0 77.0 %copy-start.7 = (f32[32]{0:T(128)S(1)}, f32[32]{0:T(128)}, u32[]{:S(2)}) copy-start(f32[32]{0:T(128)} %param.12) | copy-start | bytes 388
  11.0 47.5 %all-to-all-start = ((bf16[32,32,512]{2,1,0:T(8,128)(2,1)}), bf16[32,32,512]{2,1,0:T(8,128)(2,1)S(1)}, u32[]{:S(2)}, u32[]{:S(2)}) async-start(bf16[32,32,512]{2,1,0:T(8,128)(2,1)} %bitcast.5), calls=%async_computation | async-start | bytes 2097152 | tf_op jit(solution)/shard_map/all_to_all | solution.py:482
  31.1 3.3 %copy-start.1 = (bf16[8,4096,128]{2,1,0:T(8,128)(2,1)}, bf16[8,4096,128]{2,1,0:T(8,128)(2,1)S(1)}, u32[]{:S(2)}) copy-start(bf16[8,4096,128]{2,1,0:T(8,128)(2,1)S(1)} %build_taps.1.taps_ref) | copy-start | bytes 25165828
  58.4 11.2 %copy-start.2 = (bf16[32,32,512]{2,1,0:T(8,128)(2,1)}, bf16[32,32,512]{2,1,0:T(8,128)(2,1)S(1)}, u32[]{:S(2)}) copy-start(bf16[32,32,512]{2,1,0:T(8,128)(2,1)S(1)} %all-to-all-done) | copy-start | bytes 3145732
  58.4 31.3 %all-to-all-start.1 = ((bf16[128,2,8,128]{3,2,1,0:T(8,128)(2,1)}), bf16[128,2,8,128]{3,2,1,0:T(8,128)(2,1)S(1)}, u32[]{:S(2)}, u32[]{:S(2)}) async-start(bf16[128,2,8,128]{3,2,1,0:T(8,128)(2,1)} %pad_maximum_fusion), calls=%async_computation.1 | async-start | bytes 1048576 | tf_op jit(solution)/shard_map/all_to_all | solution.py:482
  74.0 21.6 %collective-permute-start = (bf16[128,1024]{1,0:T(8,128)(2,1)S(1)}, bf16[128,1024]{1,0:T(8,128)(2,1)S(1)}, u32[]{:S(2)}, u32[]{:S(2)}) collective-permute-start(bf16[128,1024]{1,0:T(8,128)(2,1)S(1)} %get-tuple-element.32), channel_id=1, source_target_pairs={{0,32},{32,64},{64,96},{96,0},{1,33},{33,65},{65,97},{97,1},{2,34}... | collective-permute-start | bytes 786440 | tf_op jit(solution)/shard_map/ppermute | solution.py:510
  77.2 18.4 %collective-permute-start.1 = (bf16[128,1024]{1,0:T(8,128)(2,1)S(1)}, bf16[128,1024]{1,0:T(8,128)(2,1)S(1)}, u32[]{:S(2)}, u32[]{:S(2)}) collective-permute-start(bf16[128,1024]{1,0:T(8,128)(2,1)S(1)} %get-tuple-element.33), channel_id=1, source_target_pairs={{0,64},{32,96},{64,0},{96,32},{1,65},{33,97},{65,1},{97,33},{2,66}... | collective-permute-start | bytes 786440 | tf_op jit(solution)/shard_map/ppermute | solution.py:510
  81.6 14.1 %collective-permute-start.2 = (bf16[128,1024]{1,0:T(8,128)(2,1)S(1)}, bf16[128,1024]{1,0:T(8,128)(2,1)S(1)}, u32[]{:S(2)}, u32[]{:S(2)}) collective-permute-start(bf16[128,1024]{1,0:T(8,128)(2,1)S(1)} %get-tuple-element.34), channel_id=1, source_target_pairs={{0,96},{32,0},{64,32},{96,64},{1,97},{33,1},{65,33},{97,65},{2,98}... | collective-permute-start | bytes 786440 | tf_op jit(solution)/shard_map/ppermute | solution.py:510
  84.6 25.6 %collective-permute-start.3 = (bf16[1024,512]{1,0:T(8,128)(2,1)}, bf16[1024,512]{1,0:T(8,128)(2,1)}, u32[]{:S(2)}, u32[]{:S(2)}) collective-permute-start(bf16[1024,512]{1,0:T(8,128)(2,1)} %bitcast.38), channel_id=1, source_target_pairs={{0,1},{1,0},{2,3},{3,2},{4,5},{5,4},{6,7},{7,6},{8,9},{9,8},{10,11... | collective-permute-start | bytes 3145736 | tf_op jit(solution)/shard_map/ppermute | solution.py:512
  96.6 28.3 %all-to-all-start.2 = ((bf16[32,16,512]{2,1,0:T(8,128)(2,1)}), bf16[32,16,512]{2,1,0:T(8,128)(2,1)S(1)}, u32[]{:S(2)}, u32[]{:S(2)}) async-start(bf16[32,16,512]{2,1,0:T(8,128)(2,1)} %bitcast.10), calls=%async_computation.2 | async-start | bytes 1048576 | tf_op jit(solution)/shard_map/all_to_all | solution.py:482
  106.1 47.3 %all-gather.4.cloned.1.call-start = ((), (), s32[]{:S(2)}) async-start(), calls=%async_computation.4 | async-start | bytes 1310720 | tf_op jit(solution)/shard_map/all_gather | solution.py:517
  125.6 40.5 %copy-start.5 = (bf16[1,1024,128]{2,1,0:T(8,128)(2,1)S(1)}, bf16[1,1024,128]{2,1,0:T(8,128)(2,1)}, u32[]{:S(2)}) copy-start(bf16[1,1024,128]{2,1,0:T(8,128)(2,1)} %param.9) | copy-start | bytes 786436
  132.3 33.8 %all-to-all-start.3 = ((bf16[128,2,8,128]{3,2,1,0:T(8,128)(2,1)}), bf16[128,2,8,128]{3,2,1,0:T(8,128)(2,1)S(1)}, u32[]{:S(2)}, u32[]{:S(2)}) async-start(bf16[128,2,8,128]{3,2,1,0:T(8,128)(2,1)} %bitcast.12), calls=%async_computation.3 | async-start | bytes 1048576 | tf_op jit(solution)/shard_map/all_to_all | solution.py:482
  149.5 3.9 %collective-permute-start.4 = (bf16[32,1024]{1,0:T(8,128)(2,1)S(1)}, bf16[32,1024]{1,0:T(8,128)(2,1)S(1)}, u32[]{:S(2)}, u32[]{:S(2)}) collective-permute-start(bf16[32,1024]{1,0:T(8,128)(2,1)S(1)} %late_fgrad.1), channel_id=1, source_target_pairs={{0,128},{128,0},{256,384},{384,256},{1,129},{129,1},{257,385},{385... | collective-permute-start | bytes 196616 | tf_op jit(solution)/shard_map/ppermute | solution.py:523
  157.8 4.9 %collective-permute-start.5 = (bf16[256,1024]{1,0:T(8,128)(2,1)S(1)}, bf16[256,1024]{1,0:T(8,128)(2,1)S(1)}, u32[]{:S(2)}, u32[]{:S(2)}) collective-permute-start(bf16[256,1024]{1,0:T(8,128)(2,1)S(1)} %get-tuple-element.43), channel_id=1, source_target_pairs={{0,128},{128,0},{256,384},{384,256},{1,129},{129,1},{257,385},{385... | collective-permute-start | bytes 1572872 | tf_op jit(solution)/shard_map/ppermute | solution.py:523
  160.1 7.6 %collective-permute-start.7 = (bf16[64,1024]{1,0:T(8,128)(2,1)S(1)}, bf16[64,1024]{1,0:T(8,128)(2,1)S(1)}, u32[]{:S(2)}, u32[]{:S(2)}) collective-permute-start(bf16[64,1024]{1,0:T(8,128)(2,1)S(1)} %pad_maximum_fusion.1.near_ref), channel_id=1, source_target_pairs={{0,256},{128,384},{256,0},{384,128},{1,257},{129,385},{257,1},{385... | collective-permute-start | bytes 393224 | tf_op jit(solution)/shard_map/ppermute | solution.py:523
  163.4 9.3 %collective-permute-start.6 = (bf16[128,1024]{1,0:T(8,128)(2,1)S(1)}, bf16[128,1024]{1,0:T(8,128)(2,1)S(1)}, u32[]{:S(2)}, u32[]{:S(2)}) collective-permute-start(bf16[128,1024]{1,0:T(8,128)(2,1)S(1)} %get-tuple-element.45), channel_id=1, source_target_pairs={{0,256},{128,384},{256,0},{384,128},{1,257},{129,385},{257,1},{385... | collective-permute-start | bytes 786440 | tf_op jit(solution)/shard_map/ppermute | solution.py:523
Sparse Core Ops, SparseCore 0:
  10.1 57.3 all-gather.5
  125.7 25.1 all-gather.3

commit v6 on v5

--- a/solution.py
+++ b/solution.py
@@ -198,8 +198,7 @@
         target[...] = (kept_ref[rows, :] + received_ref[rows, :].astype(f32)).astype(bf16)
 
 
-def last_kernel(place_ref, rest_ref, received_ref, near_ref, far_ref, grad_ref, fgrad_ref, skip_ref):
-    grad_ref[...] = (rest_ref[...].astype(f32) + received_ref[...].astype(f32)).astype(bf16)
+def order_kernel(place_ref, near_ref, far_ref, fgrad_ref, skip_ref):
     pieces = []
     for ref in (near_ref, far_ref):
         both = ref[...].astype(f32)
@@ -417,18 +416,14 @@
     )(place, kept, received)
 
 
-def last(place, rest, received, near, far):
-    return pl.pallas_call(
-        last_kernel,
-        in_specs=vmem_specs(4),
-        out_shape=[
-            jax.ShapeDtypeStruct((LANES, SPAN), bf16),
-            jax.ShapeDtypeStruct((2 * HALF, TAPS), f32),
-            jax.ShapeDtypeStruct((1, LANES), f32),
-        ],
-        compiler_params=params,
-        name="last",
-    )(place, rest, received, near, far)
+def order(place, near, far):
+    return pl.pallas_call(
+        order_kernel,
+        in_specs=vmem_specs(2),
+        out_shape=[jax.ShapeDtypeStruct((SEQS * GROUP, TAPS), f32), jax.ShapeDtypeStruct((1, LANES), f32)],
+        compiler_params=params,
+        name="order",
+    )(place, near, far)
 
 
 def late_conv(taps, skip, pair, value, dmix):
@@ -528,7 +523,9 @@
     dvalue, chip_fgrads = lax.optimization_barrier((dvalue, chip_fgrads))
     sent, kept = back(place, dvalue, weight, other)
     sent, rest = middle(place, kept, cross(sent, 1))
-    input_grad, filter_grad, skip_grad = last(place, rest, cross(sent, 2), chip_fgrads, far_fgrads)
+    sent, rest, out, chip_fgrads = lax.optimization_barrier((sent, rest, out, chip_fgrads))
+    input_grad = (rest.astype(f32) + cross(sent, 2).astype(f32)).astype(bf16)
+    filter_grad, skip_grad = order(place, chip_fgrads, far_fgrads)
     skip_grad = skip_grad[0, : skip.shape[0]]
 
     conv = out[:, 0].reshape(SIGNAL, LANES).astype(f32)

time: 182 us -> 182 us (level)
  transfers between devices with their start and end apart: 14 -> 14, of which waited for: 6 -> 7; matrix products, arithmetic and copies ran while one was open for 2% -> 2% of each run, Pallas kernels for 19% -> 20%
where the time goes in v6:
time: 182 us; the launch traced here: 181 us
  starting transfers between devices  73.4 us (40%)
  waiting for transfers between devices  49.7 us (27%)
  Pallas kernels  35.9 us (20%)
  between operations  14.4 us (8%)
  local copies, waits for them, and re-layouts  5.36 us (3%)
  other arithmetic  2.72 us (1%)
    all_to_all x4, starting transfers between devices, swap(): lax.all_to_all(values, axes, split_axis=0, concat_axis=0, tiled=True, axi...  49.4 us
    all_to_all x4, waiting for transfers between devices, swap(): lax.all_to_all(values, axes, split_axis=0, concat_axis=0, tiled=True, axi...  40.5 us
    ppermute x3, starting transfers between devices, per_device(): lax.ppermute(parts[step], 'tensor', [(i, (i + step) % 4) for i in range(4)])  10.6 us
    ppermute x4, starting transfers between devices, cross(): return lax.ppermute(values, 'dp', [(i, i ^ bit) for i in range(SEQS)])  10.1 us
    pallas_call x1, Pallas kernels, late_conv(): pl.pallas_call(conv_kernel, grid=(GROUP // CONV,), in_specs=[any_spec, sm...  6.69 us
    pallas_call x1, Pallas kernels, early_dmix(): pl.pallas_call(dmix_kernel, grid=(GROUP // DMIX,), in_specs=[any_spec, sm...  5.92 us
    pallas_call x1, Pallas kernels, late_fgrad(): pl.pallas_call(fgrad_kernel, grid=(GROUP // FGRAD,), in_specs=[pair_spec,...  5.01 us
    pallas_call x1, Pallas kernels, back(): pl.pallas_call(back_kernel, grid=(4,), in_specs=[smem, pl.BlockSpec((BLOC...  4.46 us
  transfers between devices with their start and end apart: 14, of which 7 were waited for; matrix products, arithmetic and copies ran while one was open for 2% of the time, Pallas kernels for 20%

profile of v6, /device:TPU:1, one launch (start us, length us, event | category | flops | bytes accessed | tf_op | source)
XLA Modules:
  0.0 181.5 jit_solution(4960458756666798193)
XLA Ops:
  7.2 0.0 copy-start
  7.2 0.0 copy-start.3
  7.2 0.0 copy-start.4
  7.2 0.0 copy-start.6
  7.2 0.0 all-gather.6.cloned.1.call-start
  7.3 0.7 all-gather.6.cloned.1.call-update
  8.0 3.0 %pack.1 = bf16[1024,512]{1,0:T(8,128)(2,1)} custom-call(s32[1]{0:T(128)} %bitcast.8.quarter_ref, bf16[32,4096]{1,0:T(8,128)(2,1)} %weight_ref.1), custom_call_target="tpu_custom_call" | custom-call | tf_op jit(solution)/shard_map/pack/pallas_call | solution.py:315
  11.0 0.0 copy-start.7
  11.0 16.6 %all-to-all-start = ((bf16[32,32,512]{2,1,0:T(8,128)(2,1)}), bf16[32,32,512]{2,1,0:T(8,128)(2,1)S(1)}, u32[]{:S(2)}, u32[]{:S(2)}) async-start(bf16[32,32,512]{2,1,0:T(8,128)(2,1)} %bitcast.9), calls=%async_computation | async-start | bytes 2097152 | tf_op jit(solution)/shard_map/all_to_all | solution.py:477
  27.6 0.0 copy-done
  27.6 3.5 %build_taps.1.taps_ref = bf16[8,4096,128]{2,1,0:T(8,128)(2,1)S(1)} custom-call(f32[8,4096]{1,0:T(8,128)S(1)} %constant_dynamic-slice_fusion.filters_ref), custom_call_target="tpu_custom_call" | custom-call | tf_op jit(solution)/shard_map/build_taps/pallas_call | solution.py:328
  31.1 0.0 copy-start.1
  31.1 3.3 %copy-done.1 = bf16[8,4096,128]{2,1,0:T(8,128)(2,1)} copy-done((bf16[8,4096,128]{2,1,0:T(8,128)(2,1)}, bf16[8,4096,128]{2,1,0:T(8,128)(2,1)S(1)}, u32[]{:S(2)}) %copy-start.1) | copy-done | bytes 8388632
  34.4 0.0 copy-done.3
  34.4 0.0 copy-done.4
  34.4 0.1 fusion.4
  34.5 0.0 copy-done.6
  34.5 0.9 pad_maximum_fusion
  35.4 23.1 %all-to-all-done = bf16[32,32,512]{2,1,0:T(8,128)(2,1)S(1)} async-done(((bf16[32,32,512]{2,1,0:T(8,128)(2,1)}), bf16[32,32,512]{2,1,0:T(8,128)(2,1)S(1)}, u32[]{:S(2)}, u32[]{:S(2)}) %all-to-all-start) | async-done | bytes 1048608 | tf_op jit(solution)/shard_map/all_to_all | solution.py:477
  58.4 11.2 %all-to-all-start.1 = ((bf16[128,2,8,128]{3,2,1,0:T(8,128)(2,1)}), bf16[128,2,8,128]{3,2,1,0:T(8,128)(2,1)S(1)}, u32[]{:S(2)}, u32[]{:S(2)}) async-start(bf16[128,2,8,128]{3,2,1,0:T(8,128)(2,1)} %pad_maximum_fusion), calls=%async_computation.1 | async-start | bytes 1048576 | tf_op jit(solution)/shard_map/all_to_all | solution.py:477
  69.6 0.0 all-gather.6.cloned.1.call-done
  69.7 0.0 copy-done.2
  69.7 4.3 %project.1 = (bf16[128,1024]{1,0:T(8,128)(2,1)S(1)}, bf16[128,1024]{1,0:T(8,128)(2,1)S(1)}, bf16[128,1024]{1,0:T(8,128)(2,1)S(1)}, bf16[128,1024]{1,0:T(8,128)(2,1)S(1)}) custom-call(s32[1]{0:T(128)} %bitcast.3.column_ref, bf16[1024,512]{1,0:T(8,128)(2,1)} %bitcast.35, bf16[1024,1024]{1,0:T(8,128)(2,1)} %bitcast.38), custom_call_target="tpu_custom_call" | custom-call | tf_op jit(solution)/shard_map/project/pallas_call | solution.py:363
  74.0 3.1 %collective-permute-start = (bf16[128,1024]{1,0:T(8,128)(2,1)S(1)}, bf16[128,1024]{1,0:T(8,128)(2,1)S(1)}, u32[]{:S(2)}, u32[]{:S(2)}) collective-permute-start(bf16[128,1024]{1,0:T(8,128)(2,1)S(1)} %get-tuple-element.33), channel_id=1, source_target_pairs={{0,32},{32,64},{64,96},{96,0},{1,33},{33,65},{65,97},{97,1},{2,34}... | collective-permute-start | bytes 786440 | tf_op jit(solution)/shard_map/ppermute | solution.py:505
  77.2 4.4 %collective-permute-start.1 = (bf16[128,1024]{1,0:T(8,128)(2,1)S(1)}, bf16[128,1024]{1,0:T(8,128)(2,1)S(1)}, u32[]{:S(2)}, u32[]{:S(2)}) collective-permute-start(bf16[128,1024]{1,0:T(8,128)(2,1)S(1)} %get-tuple-element.34), channel_id=1, source_target_pairs={{0,64},{32,96},{64,0},{96,32},{1,65},{33,97},{65,1},{97,33},{2,66}... | collective-permute-start | bytes 786440 | tf_op jit(solution)/shard_map/ppermute | solution.py:505
  81.6 3.1 %collective-permute-start.2 = (bf16[128,1024]{1,0:T(8,128)(2,1)S(1)}, bf16[128,1024]{1,0:T(8,128)(2,1)S(1)}, u32[]{:S(2)}, u32[]{:S(2)}) collective-permute-start(bf16[128,1024]{1,0:T(8,128)(2,1)S(1)} %get-tuple-element.35), channel_id=1, source_target_pairs={{0,96},{32,0},{64,32},{96,64},{1,97},{33,1},{65,33},{97,65},{2,98}... | collective-permute-start | bytes 786440 | tf_op jit(solution)/shard_map/ppermute | solution.py:505
  84.6 3.3 %collective-permute-start.3 = (bf16[1024,512]{1,0:T(8,128)(2,1)}, bf16[1024,512]{1,0:T(8,128)(2,1)}, u32[]{:S(2)}, u32[]{:S(2)}) collective-permute-start(bf16[1024,512]{1,0:T(8,128)(2,1)} %bitcast.36), channel_id=1, source_target_pairs={{0,1},{1,0},{2,3},{3,2},{4,5},{5,4},{6,7},{7,6},{8,9},{9,8},{10,11... | collective-permute-start | bytes 3145736 | tf_op jit(solution)/shard_map/ppermute | solution.py:507
  87.9 0.0 copy-done.7
  87.9 0.1 dynamic_slice.7.skip_ref
  88.0 1.7 all-to-all-done.1
  89.7 5.9 %early_dmix.1 = (bf16[1024,128]{1,0:T(8,128)(2,1)S(1)}, bf16[256,512]{1,0:T(8,128)(2,1)S(1)}) custom-call(bf16[8,4096,128]{2,1,0:T(8,128)(2,1)} %copy-done.1, f32[8]{0:T(128)S(1)} %dynamic_slice.7.skip_ref, bf16[2048,128]{1,0:T(8,128)(2,1)S(1)} %bitcast.31), custom_call_target="tpu_custom_call" | custom-call | tf_op jit(solution)/shard_map/early_dmix/pallas_call | solution.py:341
  95.6 0.0 collective-permute-done.part1
  95.6 0.0 collective-permute-done.1.part2
  95.6 0.0 collective-permute-done.2.part3
  95.6 1.0 join.1
  96.6 9.5 %all-to-all-start.2 = ((bf16[32,16,512]{2,1,0:T(8,128)(2,1)}), bf16[32,16,512]{2,1,0:T(8,128)(2,1)S(1)}, u32[]{:S(2)}, u32[]{:S(2)}) async-start(bf16[32,16,512]{2,1,0:T(8,128)(2,1)} %bitcast.13), calls=%async_computation.2 | async-start | bytes 1048576 | tf_op jit(solution)/shard_map/all_to_all | solution.py:477
  106.1 0.0 all-gather.4.cloned.1.call-start
  106.1 4.1 %collective-permute-done.3.other_ref = bf16[1024,512]{1,0:T(8,128)(2,1)} collective-permute-done((bf16[1024,512]{1,0:T(8,128)(2,1)}, bf16[1024,512]{1,0:T(8,128)(2,1)}, u32[]{:S(2)}, u32[]{:S(2)}) %collective-permute-start.3) | collective-permute-done | bytes 1048608 | tf_op jit(solution)/shard_map/ppermute | solution.py:507
  110.2 14.7 %all-to-all-done.2 = bf16[32,16,512]{2,1,0:T(8,128)(2,1)S(1)} async-done(((bf16[32,16,512]{2,1,0:T(8,128)(2,1)}), bf16[32,16,512]{2,1,0:T(8,128)(2,1)S(1)}, u32[]{:S(2)}, u32[]{:S(2)}) %all-to-all-start.2) | async-done | bytes 524320 | tf_op jit(solution)/shard_map/all_to_all | solution.py:477
  124.9 0.7 slice_bitcast_fusion.1
  125.6 0.0 all-gather.4.cloned.1.call-update
  125.6 0.0 copy-start.5
  125.6 6.7 %late_conv.1 = (bf16[2048,128]{1,0:T(8,128)(2,1)}, bf16[1024,128]{1,0:T(8,128)(2,1)S(1)}) custom-call(bf16[8,4096,128]{2,1,0:T(8,128)(2,1)} %copy-done.1, f32[8]{0:T(128)S(1)} %dynamic_slice.7.skip_ref, bf16[2048,128]{1,0:T(8,128)(2,1)S(1)} %bitcast.32, bf16[512,512]{1,0:T(8,128)(2,1)S(1)} %bitcast.34, bf16[1024,128]{1,0:T(8,128)(2,1)S(1)} %get-tuple-element.40.dmix_ref), custom_call_target="tpu_custom_call" | custom-call | tf_op jit(solution)/shard_map/late_conv/pallas_call | solution.py:430
  132.3 12.1 %all-to-all-start.3 = ((bf16[128,2,8,128]{3,2,1,0:T(8,128)(2,1)}), bf16[128,2,8,128]{3,2,1,0:T(8,128)(2,1)S(1)}, u32[]{:S(2)}, u32[]{:S(2)}) async-start(bf16[128,2,8,128]{3,2,1,0:T(8,128)(2,1)} %bitcast.16), calls=%async_computation.3 | async-start | bytes 1048576 | tf_op jit(solution)/shard_map/all_to_all | solution.py:477
  144.5 5.0 %late_fgrad.1 = bf16[32,1024]{1,0:T(8,128)(2,1)S(1)} custom-call(bf16[2048,128]{1,0:T(8,128)(2,1)S(1)} %bitcast.33, bf16[1024,128]{1,0:T(8,128)(2,1)S(1)} %get-tuple-element.41.mix_ref), custom_call_target="tpu_custom_call" | custom-call | tf_op jit(solution)/shard_map/late_fgrad/pallas_call | solution.py:458
  149.5 3.0 %collective-permute-start.4 = (bf16[32,1024]{1,0:T(8,128)(2,1)S(1)}, bf16[32,1024]{1,0:T(8,128)(2,1)S(1)}, u32[]{:S(2)}, u32[]{:S(2)}) collective-permute-start(bf16[32,1024]{1,0:T(8,128)(2,1)S(1)} %late_fgrad.1), channel_id=1, source_target_pairs={{0,128},{128,0},{256,384},{384,256},{1,129},{129,1},{257,385},{385... | collective-permute-start | bytes 196616 | tf_op jit(solution)/shard_map/ppermute | solution.py:518
  152.5 0.1 pad_add_fusion.place_ref
  152.5 0.8 collective-permute-done.4
  153.4 0.0 all-gather.4.cloned.1.call-done.dvalue_ref
  153.4 4.5 %back.1 = (bf16[256,1024]{1,0:T(8,128)(2,1)S(1)}, f32[256,1024]{1,0:T(8,128)S(1)}) custom-call(s32[3]{0:T(128)S(1)} %pad_add_fusion.place_ref, bf16[1024,512]{1,0:T(8,128)(2,1)} %all-gather.4.cloned.1.call-done.dvalue_ref, bf16[1024,512]{1,0:T(8,128)(2,1)} %bitcast.37, bf16[1024,512]{1,0:T(8,128)(2,1)} %collective-permute-done.3.other_ref), custom_call_target="tpu_custom_call" | custom-call | tf_op jit(solution)/shard_map/back/pallas_call | solution.py:389
  157.8 2.3 %collective-permute-start.5 = (bf16[256,1024]{1,0:T(8,128)(2,1)S(1)}, bf16[256,1024]{1,0:T(8,128)(2,1)S(1)}, u32[]{:S(2)}, u32[]{:S(2)}) collective-permute-start(bf16[256,1024]{1,0:T(8,128)(2,1)S(1)} %get-tuple-element.45), channel_id=1, source_target_pairs={{0,128},{128,0},{256,384},{384,256},{1,129},{129,1},{257,385},{385... | collective-permute-start | bytes 1572872 | tf_op jit(solution)/shard_map/ppermute | solution.py:518
  160.1 2.6 %collective-permute-start.7 = (bf16[64,1024]{1,0:T(8,128)(2,1)S(1)}, bf16[64,1024]{1,0:T(8,128)(2,1)S(1)}, u32[]{:S(2)}, u32[]{:S(2)}) collective-permute-start(bf16[64,1024]{1,0:T(8,128)(2,1)S(1)} %pad_maximum_fusion.1.near_ref), channel_id=1, source_target_pairs={{0,256},{128,384},{256,0},{384,128},{1,257},{129,385},{257,1},{385... | collective-permute-start | bytes 393224 | tf_op jit(solution)/shard_map/ppermute | solution.py:518
  162.7 0.0 collective-permute-done.5.received_ref
  162.7 0.6 middle.1
  163.4 1.1 all-to-all-done.3
  164.5 2.2 %collective-permute-start.6 = (bf16[128,1024]{1,0:T(8,128)(2,1)S(1)}, bf16[128,1024]{1,0:T(8,128)(2,1)S(1)}, u32[]{:S(2)}, u32[]{:S(2)}) collective-permute-start(bf16[128,1024]{1,0:T(8,128)(2,1)S(1)} %get-tuple-element.52), channel_id=1, source_target_pairs={{0,256},{128,384},{256,0},{384,128},{1,257},{129,385},{257,1},{385... | collective-permute-start | bytes 786440 | tf_op jit(solution)/shard_map/ppermute | solution.py:518
  166.7 0.7 slice_bitcast_fusion
  167.4 0.0 collective-permute-done.7.far_ref
  167.4 1.4 order.1
  168.9 0.5 slice_bitcast_fusion.2
  169.4 0.0 copy-done.5
  169.4 0.9 fusion.2
  170.3 3.6 %collective-permute-done.6 = bf16[128,1024]{1,0:T(8,128)(2,1)S(1)} collective-permute-done((bf16[128,1024]{1,0:T(8,128)(2,1)S(1)}, bf16[128,1024]{1,0:T(8,128)(2,1)S(1)}, u32[]{:S(2)}, u32[]{:S(2)}) %collective-permute-start.6) | collective-permute-done | bytes 262176 | tf_op jit(solution)/shard_map/ppermute | solution.py:518
  173.9 0.8 fusion.3
  (3 shorter events, 0.0 us)
Async XLA Ops:
  7.2 20.4 %copy-start = (f32[32,4096]{1,0:T(8,128)S(1)}, f32[32,4096]{1,0:T(8,128)}, u32[]{:S(2)}) copy-start(f32[32,4096]{1,0:T(8,128)} %param.11) | copy-start | bytes 1572868
  7.2 27.2 %copy-start.3 = (bf16[1,1024,128]{2,1,0:T(8,128)(2,1)S(1)}, bf16[1,1024,128]{2,1,0:T(8,128)(2,1)}, u32[]{:S(2)}) copy-start(bf16[1,1024,128]{2,1,0:T(8,128)(2,1)} %param.13) | copy-start | bytes 786436
  7.2 27.2 %copy-start.4 = (bf16[1,1024,128]{2,1,0:T(8,128)(2,1)S(1)}, bf16[1,1024,128]{2,1,0:T(8,128)(2,1)}, u32[]{:S(2)}) copy-start(bf16[1,1024,128]{2,1,0:T(8,128)(2,1)} %param.9) | copy-start | bytes 786436
  7.2 27.3 %copy-start.6 = (bf16[1,1024,128]{2,1,0:T(8,128)(2,1)S(1)}, bf16[1,1024,128]{2,1,0:T(8,128)(2,1)}, u32[]{:S(2)}) copy-start(bf16[1,1024,128]{2,1,0:T(8,128)(2,1)} %param.10) | copy-start | bytes 786436
  7.2 62.4 %all-gather.6.cloned.1.call-start = ((), (), s32[]{:S(2)}) async-start(), calls=%async_computation.5 | async-start | bytes 2359296 | tf_op jit(solution)/shard_map/all_gather | solution.py:487
  11.0 77.0 %copy-start.7 = (f32[32]{0:T(128)S(1)}, f32[32]{0:T(128)}, u32[]{:S(2)}) copy-start(f32[32]{0:T(128)} %param.12) | copy-start | bytes 388
  11.0 47.5 %all-to-all-start = ((bf16[32,32,512]{2,1,0:T(8,128)(2,1)}), bf16[32,32,512]{2,1,0:T(8,128)(2,1)S(1)}, u32[]{:S(2)}, u32[]{:S(2)}) async-start(bf16[32,32,512]{2,1,0:T(8,128)(2,1)} %bitcast.9), calls=%async_computation | async-start | bytes 2097152 | tf_op jit(solution)/shard_map/all_to_all | solution.py:477
  31.1 3.3 %copy-start.1 = (bf16[8,4096,128]{2,1,0:T(8,128)(2,1)}, bf16[8,4096,128]{2,1,0:T(8,128)(2,1)S(1)}, u32[]{:S(2)}) copy-start(bf16[8,4096,128]{2,1,0:T(8,128)(2,1)S(1)} %build_taps.1.taps_ref) | copy-start | bytes 25165828
  58.4 11.2 %copy-start.2 = (bf16[32,32,512]{2,1,0:T(8,128)(2,1)}, bf16[32,32,512]{2,1,0:T(8,128)(2,1)S(1)}, u32[]{:S(2)}) copy-start(bf16[32,32,512]{2,1,0:T(8,128)(2,1)S(1)} %all-to-all-done) | copy-start | bytes 3145732
  58.4 31.3 %all-to-all-start.1 = ((bf16[128,2,8,128]{3,2,1,0:T(8,128)(2,1)}), bf16[128,2,8,128]{3,2,1,0:T(8,128)(2,1)S(1)}, u32[]{:S(2)}, u32[]{:S(2)}) async-start(bf16[128,2,8,128]{3,2,1,0:T(8,128)(2,1)} %pad_maximum_fusion), calls=%async_computation.1 | async-start | bytes 1048576 | tf_op jit(solution)/shard_map/all_to_all | solution.py:477
  74.0 21.6 %collective-permute-start = (bf16[128,1024]{1,0:T(8,128)(2,1)S(1)}, bf16[128,1024]{1,0:T(8,128)(2,1)S(1)}, u32[]{:S(2)}, u32[]{:S(2)}) collective-permute-start(bf16[128,1024]{1,0:T(8,128)(2,1)S(1)} %get-tuple-element.33), channel_id=1, source_target_pairs={{0,32},{32,64},{64,96},{96,0},{1,33},{33,65},{65,97},{97,1},{2,34}... | collective-permute-start | bytes 786440 | tf_op jit(solution)/shard_map/ppermute | solution.py:505
  77.2 18.4 %collective-permute-start.1 = (bf16[128,1024]{1,0:T(8,128)(2,1)S(1)}, bf16[128,1024]{1,0:T(8,128)(2,1)S(1)}, u32[]{:S(2)}, u32[]{:S(2)}) collective-permute-start(bf16[128,1024]{1,0:T(8,128)(2,1)S(1)} %get-tuple-element.34), channel_id=1, source_target_pairs={{0,64},{32,96},{64,0},{96,32},{1,65},{33,97},{65,1},{97,33},{2,66}... | collective-permute-start | bytes 786440 | tf_op jit(solution)/shard_map/ppermute | solution.py:505
  81.6 14.1 %collective-permute-start.2 = (bf16[128,1024]{1,0:T(8,128)(2,1)S(1)}, bf16[128,1024]{1,0:T(8,128)(2,1)S(1)}, u32[]{:S(2)}, u32[]{:S(2)}) collective-permute-start(bf16[128,1024]{1,0:T(8,128)(2,1)S(1)} %get-tuple-element.35), channel_id=1, source_target_pairs={{0,96},{32,0},{64,32},{96,64},{1,97},{33,1},{65,33},{97,65},{2,98}... | collective-permute-start | bytes 786440 | tf_op jit(solution)/shard_map/ppermute | solution.py:505
  84.6 25.6 %collective-permute-start.3 = (bf16[1024,512]{1,0:T(8,128)(2,1)}, bf16[1024,512]{1,0:T(8,128)(2,1)}, u32[]{:S(2)}, u32[]{:S(2)}) collective-permute-start(bf16[1024,512]{1,0:T(8,128)(2,1)} %bitcast.36), channel_id=1, source_target_pairs={{0,1},{1,0},{2,3},{3,2},{4,5},{5,4},{6,7},{7,6},{8,9},{9,8},{10,11... | collective-permute-start | bytes 3145736 | tf_op jit(solution)/shard_map/ppermute | solution.py:507
  96.6 28.3 %all-to-all-start.2 = ((bf16[32,16,512]{2,1,0:T(8,128)(2,1)}), bf16[32,16,512]{2,1,0:T(8,128)(2,1)S(1)}, u32[]{:S(2)}, u32[]{:S(2)}) async-start(bf16[32,16,512]{2,1,0:T(8,128)(2,1)} %bitcast.13), calls=%async_computation.2 | async-start | bytes 1048576 | tf_op jit(solution)/shard_map/all_to_all | solution.py:477
  106.1 47.3 %all-gather.4.cloned.1.call-start = ((), (), s32[]{:S(2)}) async-start(), calls=%async_computation.4 | async-start | bytes 1310720 | tf_op jit(solution)/shard_map/all_gather | solution.py:512
  125.6 43.8 %copy-start.5 = (bf16[1,1024,128]{2,1,0:T(8,128)(2,1)S(1)}, bf16[1,1024,128]{2,1,0:T(8,128)(2,1)}, u32[]{:S(2)}) copy-start(bf16[1,1024,128]{2,1,0:T(8,128)(2,1)} %param.9) | copy-start | bytes 786436
  132.3 32.2 %all-to-all-start.3 = ((bf16[128,2,8,128]{3,2,1,0:T(8,128)(2,1)}), bf16[128,2,8,128]{3,2,1,0:T(8,128)(2,1)S(1)}, u32[]{:S(2)}, u32[]{:S(2)}) async-start(bf16[128,2,8,128]{3,2,1,0:T(8,128)(2,1)} %bitcast.16), calls=%async_computation.3 | async-start | bytes 1048576 | tf_op jit(solution)/shard_map/all_to_all | solution.py:477
  149.5 3.9 %collective-permute-start.4 = (bf16[32,1024]{1,0:T(8,128)(2,1)S(1)}, bf16[32,1024]{1,0:T(8,128)(2,1)S(1)}, u32[]{:S(2)}, u32[]{:S(2)}) collective-permute-start(bf16[32,1024]{1,0:T(8,128)(2,1)S(1)} %late_fgrad.1), channel_id=1, source_target_pairs={{0,128},{128,0},{256,384},{384,256},{1,129},{129,1},{257,385},{385... | collective-permute-start | bytes 196616 | tf_op jit(solution)/shard_map/ppermute | solution.py:518
  157.8 4.9 %collective-permute-start.5 = (bf16[256,1024]{1,0:T(8,128)(2,1)S(1)}, bf16[256,1024]{1,0:T(8,128)(2,1)S(1)}, u32[]{:S(2)}, u32[]{:S(2)}) collective-permute-start(bf16[256,1024]{1,0:T(8,128)(2,1)S(1)} %get-tuple-element.45), channel_id=1, source_target_pairs={{0,128},{128,0},{256,384},{384,256},{1,129},{129,1},{257,385},{385... | collective-permute-start | bytes 1572872 | tf_op jit(solution)/shard_map/ppermute | solution.py:518
  160.1 7.3 %collective-permute-start.7 = (bf16[64,1024]{1,0:T(8,128)(2,1)S(1)}, bf16[64,1024]{1,0:T(8,128)(2,1)S(1)}, u32[]{:S(2)}, u32[]{:S(2)}) collective-permute-start(bf16[64,1024]{1,0:T(8,128)(2,1)S(1)} %pad_maximum_fusion.1.near_ref), channel_id=1, source_target_pairs={{0,256},{128,384},{256,0},{384,128},{1,257},{129,385},{257,1},{385... | collective-permute-start | bytes 393224 | tf_op jit(solution)/shard_map/ppermute | solution.py:518
  164.5 9.4 %collective-permute-start.6 = (bf16[128,1024]{1,0:T(8,128)(2,1)S(1)}, bf16[128,1024]{1,0:T(8,128)(2,1)S(1)}, u32[]{:S(2)}, u32[]{:S(2)}) collective-permute-start(bf16[128,1024]{1,0:T(8,128)(2,1)S(1)} %get-tuple-element.52), channel_id=1, source_target_pairs={{0,256},{128,384},{256,0},{384,128},{1,257},{129,385},{257,1},{385... | collective-permute-start | bytes 786440 | tf_op jit(solution)/shard_map/ppermute | solution.py:518
Sparse Core Ops, SparseCore 0:
  10.1 57.3 all-gather.5
  125.7 25.1 all-gather.3
